TPU v7x, 128 devices: a whole 4x4x4 slice. The times are simulated.
128 devices in a mesh: band: 8 (over y_lo, x), dom: 16 (over z, y_hi, core).
Axes of the slice: x: 4, y: 4 (y_hi: 2, y_lo: 2; y = y_hi * 2 + y_lo), z: 4, core: 2. Of those that a mesh axis runs over, the one named last changes fastest.
Arguments:
- orbitals: bfloat16 [32, 64, 256, 256], P('band', 'dom'), may hold values from -12.5 to 12.5, as said below
- owner_band: int32 [1], replicated, may hold values from 0 to 7
Outputs:
- exchange_field: float32 [32, 64, 256, 256], P('band', 'dom')
- ace_block: float32 [8, 6, 4], P('band')
Inputs may be any that keep to these rules, and one draw needn't show every extreme that they name: `orbitals`: real-valued orbital samples, independent from cell to cell.
All inputs are finite; a program needn't handle non-finite values.
Results may differ from a plain program's by a relative error of at most 0.00035.
Values may be sent and summed in bfloat16 or wider, within the bound.
No kernel may reach another device: no remote copies, remote signals or barrier semaphores. Data moves between devices by JAX's collectives and lax.ppermute only.
A program may use at most 256 MiB of HBM per device.

v0:
```python
import math

import jax
import jax.numpy as jnp
from jax import lax
from jax.sharding import PartitionSpec as P

PANEL = 2
SWEEPS = 3


SCREEN = 0.1


def spread(value, axis, source):
    kept = jnp.where(lax.axis_index(axis) == source, value, 0).astype(value.dtype)
    return lax.psum(kept, axis)


def padded_2(cells, sides, width):
    for axis, dim in sides:
        count = lax.axis_size(axis)
        head = lax.slice_in_dim(cells, 0, width, axis=dim)
        tail = lax.slice_in_dim(cells, cells.shape[dim] - width, cells.shape[dim], axis=dim)
        cells = jnp.concatenate(
            [
                lax.ppermute(tail, axis, [(i, (i + 1) % count) for i in range(count)]),
                cells,
                lax.ppermute(head, axis, [((i + 1) % count, i) for i in range(count)]),
            ],
            axis=dim,
        )
    return cells


def sweep_weights(count):
    return [
        1.0 / (1.0 + 6.0 / (6.0 + SCREEN) * math.cos(math.pi * (2 * sweep + 1) / (2 * count)))
        for sweep in range(count)
    ]


def relaxed_step(padded, pair_density, factor):
    inverse = 1.0 / (6.0 + SCREEN)
    centre = padded[:, :, 1:-1]
    summed = padded[:, :, 2:] + padded[:, :, :-2]
    summed = summed + jnp.roll(centre, 1, 3) + jnp.roll(centre, -1, 3)
    summed = summed + jnp.roll(centre, 1, 4) + jnp.roll(centre, -1, 4)
    return centre + factor * ((pair_density - ((6.0 + SCREEN) * centre - summed)) * inverse)


def local(orbitals, owner_band):
    inverse = 1.0 / (6.0 + SCREEN)
    factors = sweep_weights(SWEEPS)
    panel_block = spread(orbitals[:PANEL], "band", owner_band[0])
    panel_float = panel_block.astype(jnp.float32)
    planes = orbitals.shape[1]
    pair_density = panel_float[:, None] * orbitals[None].astype(jnp.float32)
    potential = factors[0] * (pair_density * inverse)
    for sweep in range(1, SWEEPS):
        padded = padded_2(potential, (("dom", 2),), 1)
        potential = relaxed_step(padded, pair_density, factors[sweep])
    exchange = -jnp.sum(potential * panel_float[:, None], axis=0)
    sources = jnp.concatenate([panel_float, orbitals.astype(jnp.float32)], axis=0)
    partial_sums = jnp.einsum("axyz,jxyz->aj", sources, exchange, precision=lax.Precision.HIGHEST)
    cell_count = float(planes * lax.axis_size("dom") * orbitals.shape[2] * orbitals.shape[3])
    ace_block = lax.psum(partial_sums, "dom") / cell_count
    return (exchange, ace_block[None])


def solution(mesh):
    placed = (P("band", "dom", None, None), P())
    return jax.shard_map(
        local,
        mesh=mesh,
        in_specs=placed,
        out_specs=(P("band", "dom", None, None), P("band", None, None)),
        check_vma=False,
    )
```

profile of v0, /device:TPU:0, one launch (start us, length us, event | category | flops | bytes accessed | tf_op | source)
XLA Modules:
  0.0 399.6 jit_solution(4283166294143256178)
XLA Ops:
  7.2 0.0 copy-start.3
  7.2 0.0 all-reduce.2.cloned.1.call-start
  8.0 2.3 slice_select_fusion
  10.3 0.0 all-reduce.2.cloned.1.call-update
  10.3 4.5 %copy.16 = f32[4,4,256,256]{2,1,3,0:T(4,128)} copy(bf16[4,4,256,256]{3,2,1,0:T(8,128)(2,1)} %param.2) | data formatting | bytes 6291456 | tf_op jit(solution)/shard_map/convert_element_type | solution.py:58
  14.8 0.0 copy-done.3
  14.8 2.4 convert_element_type.11
  17.2 72.7 %all-reduce.2.cloned.1.call-done = bf16[2,4,256,256]{3,2,1,0:T(8,128)(2,1)} async-done(((bf16[2,4,256,256]{3,2,1,0:T(8,128)(2,1)}), bf16[2,4,256,256]{3,2,1,0:T(8,128)(2,1)}) %all-reduce.2.cloned.1.call-update) | async-done | bytes 1048592 | tf_op jit(solution)/shard_map/psum | solution.py:17
  89.9 1.7 copy.15
  91.6 0.0 copy-start.1
  91.6 8.2 %multiply_multiply_fusion.1 = f32[2,4,4,256,256]{3,2,4,1,0:T(4,128)} fusion(f32[4,4,256,256]{2,1,3,0:T(4,128)} %copy.16, f32[2,4,256,256]{2,1,3,0:T(4,128)S(1)} %copy.15), kind=kLoop, calls=%fused_computation.3 | loop fusion | flops 4194304 | bytes 14680064 | tf_op jit(solution)/shard_map/mul | solution.py:59
  99.9 9.0 %fusion.34 = (f32[2,4,4,1,256]{3,2,4,1,0:T(4,128)}, f32[2,4,4,1,256]{3,2,4,1,0:T(4,128)}) fusion(f32[2,4,4,256,256]{3,2,4,1,0:T(4,128)} %multiply_multiply_fusion.1), kind=kLoop, calls=%fused_computation.41 | loop fusion | bytes 131072 | tf_op jit(solution)/shard_map/jit(_roll_static)/slice | solution.py:47
  108.9 12.0 %fusion.35 = (f32[2,4,1,256,256]{3,2,4,1,0:T(1,128)}, f32[2,4,1,256,256]{3,2,4,1,0:T(1,128)}) fusion(f32[2,4,4,256,256]{3,2,4,1,0:T(4,128)} %multiply_multiply_fusion.1), kind=kLoop, calls=%fused_computation.42 | loop fusion | bytes 8388608 | tf_op jit(solution)/shard_map/slice | solution.py:23
  120.9 0.9 fusion.32
  121.8 0.0 collective-permute-start
  121.8 0.9 collective-permute-start.1
  122.7 0.0 copy-done.4
  122.7 0.2 convert_element_type.10
  122.9 0.0 slice-start.1
  122.9 5.6 %pad_maximum_fusion.4 = f32[6,4,256,256]{3,2,1,0:T(8,128)} fusion(f32[4,4,256,256]{3,2,1,0:T(8,128)} %convert_element_type.11, f32[2,4,256,256]{3,2,1,0:T(8,128)S(1)} %convert_element_type.10), kind=kLoop, calls=%fused_computation.28 | loop fusion | flops 1572864 | bytes 12582912 | tf_op jit(solution)/shard_map/concatenate | solution.py:64
  128.5 0.0 slice-done
  128.5 0.0 slice-done.1
  128.5 6.7 %fusion.31 = (f32[2,4,4,256,255]{3,2,4,1,0:T(4,128)}, f32[2,4,4,256,255]{3,2,4,1,0:T(4,128)}) fusion(f32[2,4,4,256,256]{3,2,4,1,0:T(4,128)S(1)} %bitcast.9), kind=kLoop, calls=%fused_computation.38 | loop fusion | bytes 33423360 | tf_op jit(solution)/shard_map/jit(_roll_static)/slice | solution.py:48
  135.2 8.3 %fusion.33 = (f32[2,4,4,255,256]{3,2,4,1,0:T(4,128)}, f32[2,4,4,255,256]{3,2,4,1,0:T(4,128)}) fusion(f32[2,4,4,256,256]{3,2,4,1,0:T(4,128)S(1)} %bitcast.9), kind=kLoop, calls=%fused_computation.40 | loop fusion | bytes 33423360 | tf_op jit(solution)/shard_map/jit(_roll_static)/slice | solution.py:47
  143.5 21.9 %collective-permute-done = f32[2,4,1,256,256]{3,2,4,1,0:T(1,128)} collective-permute-done((f32[2,4,1,256,256]{3,2,4,1,0:T(1,128)}, f32[2,4,1,256,256]{3,2,4,1,0:T(1,128)}, u32[]{:S(2)}, u32[]{:S(2)}) %collective-permute-start) | collective-permute-done | bytes 2097184 | tf_op jit(solution)/shard_map/ppermute | solution.py:29
  165.4 8.3 %collective-permute-done.1 = f32[2,4,1,256,256]{3,2,4,1,0:T(1,128)} collective-permute-done((f32[2,4,1,256,256]{3,2,4,1,0:T(1,128)}, f32[2,4,1,256,256]{3,2,4,1,0:T(1,128)}, u32[]{:S(2)}, u32[]{:S(2)}) %collective-permute-start.1) | collective-permute-done | bytes 2097184 | tf_op jit(solution)/shard_map/ppermute | solution.py:27
  173.7 0.0 copy-done.1
  173.7 33.4 %fusion.2 = f32[2,4,4,256,256]{3,2,4,1,0:T(4,128)} fusion(f32[2,4,4,256,256]{3,2,4,1,0:T(4,128)} %multiply_multiply_fusion.1, f32[2,4,1,256,256]{3,2,4,1,0:T(1,128)} %collective-permute-done.1, f32[2,4,1,256,256]{3,2,4,1,0:T(1,128)} %collective-permute-done, f32[2,4,4,255,256]{3,2,4,1,0:T(4,128)} %get-tuple-element.17, ...), kind=kLoop, calls=%fused_computation.6 | loop fusion | flops 35651584 | bytes 60817408 | tf_op jit(solution)/shard_map/add | solution.py:49
  207.1 9.1 %fusion.29 = (f32[2,4,4,1,256]{3,2,4,1,0:T(4,128)}, f32[2,4,4,1,256]{3,2,4,1,0:T(4,128)}) fusion(f32[2,4,4,256,256]{3,2,4,1,0:T(4,128)} %fusion.2), kind=kLoop, calls=%fused_computation.36 | loop fusion | bytes 131072 | tf_op jit(solution)/shard_map/jit(_roll_static)/slice | solution.py:47
  216.2 11.8 %fusion.30 = (f32[2,4,1,256,256]{3,2,4,1,0:T(1,128)}, f32[2,4,1,256,256]{3,2,4,1,0:T(1,128)}) fusion(f32[2,4,4,256,256]{3,2,4,1,0:T(4,128)} %fusion.2), kind=kLoop, calls=%fused_computation.37 | loop fusion | bytes 8388608 | tf_op jit(solution)/shard_map/slice | solution.py:23
  228.0 0.8 fusion.27
  228.8 0.0 collective-permute-start.2
  228.8 0.0 slice-start.2
  228.8 0.0 slice-start.3
  228.8 0.5 collective-permute-start.3
  229.3 13.5 %fusion.26 = (f32[2,4,4,256,255]{3,2,4,1,0:T(4,128)}, f32[2,4,4,256,255]{3,2,4,1,0:T(4,128)}) fusion(f32[2,4,4,256,256]{3,2,4,1,0:T(4,128)} %fusion.2), kind=kLoop, calls=%fused_computation.33 | loop fusion | bytes 33423360 | tf_op jit(solution)/shard_map/jit(_roll_static)/slice | solution.py:48
  242.8 0.0 copy-start
  242.8 8.3 %fusion.28 = (f32[2,4,4,255,256]{3,2,4,1,0:T(4,128)}, f32[2,4,4,255,256]{3,2,4,1,0:T(4,128)}) fusion(f32[2,4,4,256,256]{3,2,4,1,0:T(4,128)S(1)} %bitcast.11), kind=kLoop, calls=%fused_computation.35 | loop fusion | bytes 33423360 | tf_op jit(solution)/shard_map/jit(_roll_static)/slice | solution.py:47
  251.1 23.8 %collective-permute-done.2 = f32[2,4,1,256,256]{3,2,4,1,0:T(1,128)} collective-permute-done((f32[2,4,1,256,256]{3,2,4,1,0:T(1,128)}, f32[2,4,1,256,256]{3,2,4,1,0:T(1,128)}, u32[]{:S(2)}, u32[]{:S(2)}) %collective-permute-start.2) | collective-permute-done | bytes 2097184 | tf_op jit(solution)/shard_map/ppermute | solution.py:29
  274.9 3.5 collective-permute-done.3
  278.4 31.6 %fusion.6 = f32[4,4,256,256]{2,1,3,0:T(4,128)} fusion(f32[2,4,4,256,256]{3,2,4,1,0:T(4,128)S(1)} %bitcast.11, f32[2,4,1,256,256]{3,2,4,1,0:T(1,128)} %collective-permute-done.3, f32[2,4,1,256,256]{3,2,4,1,0:T(1,128)} %collective-permute-done.2, f32[2,4,4,255,256]{3,2,4,1,0:T(4,128)} %get-tuple-element.7, f32[2,4,4,1,256]{3,2,4,1,0:T(4,128)} %get-tuple-element.9, ...), kind=kLoop, calls=%fused_computation.10 | loop fusion | flops 38797312 | bytes 56623104 | tf_op jit(solution)/shard_map/reduce_sum | solution.py:63
  310.1 5.4 %copy.21 = f32[4,4,256,256]{3,2,1,0:T(8,128)} copy(f32[4,4,256,256]{2,1,3,0:T(4,128)} %fusion.6) | data formatting | bytes 8388608
  315.4 2.7 neg.3
  318.1 0.0 copy-start.2
  318.1 2.0 copy-done.2
  320.1 36.6 %fusion.21 = f32[6,4]{0,1:T(4,128)S(1)} fusion(f32[4,4,256,256]{3,2,1,0:T(8,128)S(1)} %neg.3, f32[6,4,256,256]{3,2,1,0:T(8,128)S(1)} %bitcast.13), kind=kOutput, calls=%fused_computation.30 | convolution fusion | flops 75497472 | bytes 10485856 | tf_op jit(solution)/shard_map/axyz,jxyz->aj/dot_general | solution.py:65
  356.8 35.2 %psum.15 = f32[6,4]{0,1:T(4,128)S(1)} all-reduce(f32[6,4]{0,1:T(4,128)S(1)} %fusion.21), channel_id=1, replica_groups=mesh['band'=8,'dom'=16] {'dom'}, use_global_device_ids=true, to_apply=%region_2.3 | all-reduce | flops 24 | bytes 192 | tf_op jit(solution)/shard_map/psum | solution.py:67
  392.0 0.6 multiply_bitcast_fusion
  (12 shorter events, 0.0 us)
Async XLA Ops:
  7.2 7.7 %copy-start.3 = (bf16[4,4,256,256]{3,2,1,0:T(8,128)(2,1)S(1)}, bf16[4,4,256,256]{3,2,1,0:T(8,128)(2,1)}, u32[]{:S(2)}) copy-start(bf16[4,4,256,256]{3,2,1,0:T(8,128)(2,1)} %param.2) | copy-start | bytes 6291460
  7.2 82.8 %all-reduce.2.cloned.1.call-start = ((), (), s32[]{:S(2)}) async-start(), calls=%async_computation | async-start | bytes 2097152 | tf_op jit(solution)/shard_map/psum | solution.py:17
  91.6 82.1 %copy-start.1 = (f32[2,4,256,256]{2,1,3,0:T(4,128)}, f32[2,4,256,256]{2,1,3,0:T(4,128)S(1)}, u32[]{:S(2)}) copy-start(f32[2,4,256,256]{2,1,3,0:T(4,128)S(1)} %copy.15) | copy-start | bytes 6291460
  108.9 13.9 %copy-start.4 = (bf16[2,4,256,256]{3,2,1,0:T(8,128)(2,1)S(1)}, bf16[2,4,256,256]{3,2,1,0:T(8,128)(2,1)}, u32[]{:S(2)}) copy-start(bf16[2,4,256,256]{3,2,1,0:T(8,128)(2,1)} %all-reduce.2.cloned.1.call-done) | copy-start | bytes 3145732
  120.9 7.7 %slice-start = ((s8[8388608]{0:T(1024)(128)(4,1)}), s8[4194304]{0:T(1024)(128)(4,1)S(1)}, s32[]{:S(2)}) async-start(s8[8388608]{0:T(1024)(128)(4,1)} %bitcast.8), calls=%async_computation.1 | async-start | bytes 8388608
  121.8 43.6 %collective-permute-start = (f32[2,4,1,256,256]{3,2,4,1,0:T(1,128)}, f32[2,4,1,256,256]{3,2,4,1,0:T(1,128)}, u32[]{:S(2)}, u32[]{:S(2)}) collective-permute-start(f32[2,4,1,256,256]{3,2,4,1,0:T(1,128)} %get-tuple-element.20), channel_id=1, source_target_pairs={{1,0},{2,1},{3,2},{4,3},{5,4},{6,5},{7,6},{8,7},{9,8},{10,9},{11,1... | collective-permute-start | bytes 6291464 | tf_op jit(solution)/shard_map/ppermute | solution.py:29
  121.8 51.9 %collective-permute-start.1 = (f32[2,4,1,256,256]{3,2,4,1,0:T(1,128)}, f32[2,4,1,256,256]{3,2,4,1,0:T(1,128)}, u32[]{:S(2)}, u32[]{:S(2)}) collective-permute-start(f32[2,4,1,256,256]{3,2,4,1,0:T(1,128)} %get-tuple-element.21), channel_id=1, source_target_pairs={{0,1},{1,2},{2,3},{3,4},{4,5},{5,6},{6,7},{7,8},{8,9},{9,10},{10,1... | collective-permute-start | bytes 6291464 | tf_op jit(solution)/shard_map/ppermute | solution.py:27
  122.9 5.6 %slice-start.1 = ((s8[8388608]{0:T(1024)(128)(4,1)}), s8[4194304]{0:T(1024)(128)(4,1)S(1)}, s32[]{:S(2)}) async-start(s8[8388608]{0:T(1024)(128)(4,1)} %bitcast.8), calls=%async_computation.2 | async-start | bytes 8388608
  228.8 46.2 %collective-permute-start.2 = (f32[2,4,1,256,256]{3,2,4,1,0:T(1,128)}, f32[2,4,1,256,256]{3,2,4,1,0:T(1,128)}, u32[]{:S(2)}, u32[]{:S(2)}) collective-permute-start(f32[2,4,1,256,256]{3,2,4,1,0:T(1,128)} %get-tuple-element.10), channel_id=1, source_target_pairs={{1,0},{2,1},{3,2},{4,3},{5,4},{6,5},{7,6},{8,7},{9,8},{10,9},{11,1... | collective-permute-start | bytes 6291464 | tf_op jit(solution)/shard_map/ppermute | solution.py:29
  228.8 14.0 %slice-start.2 = ((s8[8388608]{0:T(1024)(128)(4,1)}), s8[4194304]{0:T(1024)(128)(4,1)S(1)}, s32[]{:S(2)}) async-start(s8[8388608]{0:T(1024)(128)(4,1)} %bitcast.10), calls=%async_computation.3 | async-start | bytes 8388608
  228.8 14.0 %slice-start.3 = ((s8[8388608]{0:T(1024)(128)(4,1)}), s8[4194304]{0:T(1024)(128)(4,1)S(1)}, s32[]{:S(2)}) async-start(s8[8388608]{0:T(1024)(128)(4,1)} %bitcast.10), calls=%async_computation.4 | async-start | bytes 8388608
  228.8 49.6 %collective-permute-start.3 = (f32[2,4,1,256,256]{3,2,4,1,0:T(1,128)}, f32[2,4,1,256,256]{3,2,4,1,0:T(1,128)}, u32[]{:S(2)}, u32[]{:S(2)}) collective-permute-start(f32[2,4,1,256,256]{3,2,4,1,0:T(1,128)} %get-tuple-element.11), channel_id=1, source_target_pairs={{0,1},{1,2},{2,3},{3,4},{4,5},{5,6},{6,7},{7,8},{8,9},{9,10},{10,1... | collective-permute-start | bytes 6291464 | tf_op jit(solution)/shard_map/ppermute | solution.py:27
  242.8 35.6 %copy-start = (f32[4,4,256,256]{2,1,3,0:T(4,128)S(1)}, f32[4,4,256,256]{2,1,3,0:T(4,128)}, u32[]{:S(2)}) copy-start(f32[4,4,256,256]{2,1,3,0:T(4,128)} %copy.16) | copy-start | bytes 12582916
  310.1 10.1 %slice-start.4 = ((s8[6291456]{0:T(1024)(128)(4,1)}), s8[2097152]{0:T(1024)(128)(4,1)S(1)}, s32[]{:S(2)}) async-start(s8[6291456]{0:T(1024)(128)(4,1)} %bitcast.12), calls=%async_computation.5 | async-start | bytes 4194304
  315.4 4.7 %slice-start.5 = ((s8[6291456]{0:T(1024)(128)(4,1)}), s8[4194304]{0:T(1024)(128)(4,1)S(1)}, s32[]{:S(2)}) async-start(s8[6291456]{0:T(1024)(128)(4,1)} %bitcast.12), calls=%async_computation.6 | async-start | bytes 8388608
  318.1 2.0 copy-start.2
Sparse Core Ops, SparseCore 0:
  10.5 79.3 all-reduce.1
where the time goes:
time: 408 us; the launch traced here: 400 us
  waiting for transfers between devices  130 us (32%)
  local copies, waits for them, and re-layouts  93.9 us (23%)
  other arithmetic  87 us (21%)
  matrix products  36.6 us (9%)
  blocking collectives  35.2 us (9%)
  between operations  15.2 us (4%)
    psum x1, waiting for transfers between devices, spread(): return lax.psum(kept, axis)  72.7 us
    ppermute x2, waiting for transfers between devices, padded_2(): lax.ppermute(head, axis, [((i + 1) % count, i) for i in range(count)])  45.7 us
    dot_general x1, matrix products, local(): jnp.einsum('axyz,jxyz->aj', sources, exchange, precision=lax.Precision.HI...  36.6 us
    psum x1, blocking collectives, local(): ace_block = lax.psum(partial_sums, 'dom') / cell_count  35.2 us
    slice x4, local copies, waits for them, and re-layouts, relaxed_step(): summed = summed + jnp.roll(centre, 1, 3) + jnp.roll(centre, -1, 3)  34.7 us
    add x1, other arithmetic, relaxed_step(): centre + factor * ((pair_density - ((6.0 + SCREEN) * centre - summed)) *...  33.4 us
    reduce_sum x1, other arithmetic, local(): exchange = -jnp.sum(potential * panel_float[:, None], axis=0)  31.6 us
    slice x2, local copies, waits for them, and re-layouts, padded_2(): head = lax.slice_in_dim(cells, 0, width, axis=dim)  23.8 us
  transfers between devices with their start and end apart: 5, of which 5 were waited for; matrix products, arithmetic and copies ran while one was open for 12% of the time, Pallas kernels for 0%

commit v1 on v0

v1 whole, which is shorter than its diff:
```python
import math

import jax
import jax.numpy as jnp
import numpy as np
from jax import lax
from jax.experimental import pallas as pl
from jax.experimental.pallas import tpu as pltpu
from jax.sharding import PartitionSpec as P

PANEL, SWEEPS, SCREEN = 2, 3, 0.1
PAD = 8
STRIP = 32

def poly():
    d = 6.0 + SCREEN
    w = [1.0 / (1.0 + 6.0 / d * math.cos(math.pi * (2 * k + 1) / (2 * SWEEPS))) for k in range(SWEEPS)]
    p = [w[0] / d]
    for k in range(1, SWEEPS):
        n = [0.0] * (len(p) + 1)
        for i, c in enumerate(p):
            n[i] += c * (1.0 - w[k])
            n[i + 1] += c * w[k] / d
        n[0] += w[k] / d
        p = n
    return p

def mixing(nz, beta):
    near = np.zeros((nz, nz), np.float32)
    far = np.zeros((nz, nz), np.float32)
    for z in range(nz):
        for s, m in ((1, near), (2, far)):
            m[(z - s) % nz, z] += 1.0
            m[(z + s) % nz, z] += 1.0
    return jnp.asarray(np.concatenate([near, near, beta * far], 0)).astype(jnp.bfloat16)

def kernel(o, olo, ohi, p, plo, phi, mix, e, ace, rho, sig, left, base):
    g0, g1, g2 = poly()
    beta = g2 / g1
    kappa = g0 / g1 + 6.0 * beta
    nj, nx, ny, nz = o.shape
    na = p.shape[0]
    steps = ny // STRIP
    f32, bf = jnp.float32, jnp.bfloat16

    def per_orbital(j, _):
        for src_p, src_o, first, count in ((plo, olo, 0, 2), (p, o, 2, nx), (phi, ohi, 2 + nx, 2)):
            def per_plane(k, _):
                for i in range(steps):
                    rows = slice(i * STRIP, (i + 1) * STRIP)
                    ov = src_o[j, k, rows, :].astype(f32)
                    for a in range(na):
                        rho[a, first + k, PAD + i * STRIP:PAD + (i + 1) * STRIP, :] = src_p[a, k, rows, :].astype(f32) * ov
                for a in range(na):
                    rho[a, first + k, PAD - 2:PAD, :] = rho[a, first + k, PAD + ny - 2:PAD + ny, :]
                    rho[a, first + k, PAD + ny:PAD + ny + 2, :] = rho[a, first + k, PAD:PAD + 2, :]
                return 0
            lax.fori_loop(0, count, per_plane, 0)

        def per_out(x, acc):
            for a in range(na):
                for r in range(0, ny + 2 * PAD, 16):
                    sig[a, r:r + 16, :] = rho[a, x + 1, r:r + 16, :] + rho[a, x + 3, r:r + 16, :]
            for a in range(na):
                for i in range(steps):
                    r = PAD + i * STRIP
                    at = lambda ref, idx, s: ref[(*idx, slice(r + s, r + s + STRIP), slice(None))]
                    c = at(rho, (a, x + 2), 0)
                    q = at(sig, (a,), 0) + (at(rho, (a, x + 2), -1) + at(rho, (a, x + 2), 1))
                    far = (at(rho, (a, x), 0) + at(rho, (a, x + 4), 0)) + (at(rho, (a, x + 2), -2) + at(rho, (a, x + 2), 2))
                    side = at(sig, (a,), -1) + at(sig, (a,), 1)
                    v = c + (2.0 * beta) * q
                    hi = v.astype(bf)
                    rows = slice(i * STRIP, (i + 1) * STRIP)
                    left[a, rows, :nz] = hi
                    left[a, rows, nz:2 * nz] = (v - hi.astype(f32)).astype(bf)
                    left[a, rows, 2 * nz:] = c.astype(bf)
                    base[a, rows, :] = (kappa * c + q) + beta * (far + (side + side))
            mixed = [jnp.dot(left[a], mix[...], preferred_element_type=f32) for a in range(na)]
            acc = list(acc)
            for i in range(steps):
                rows = slice(i * STRIP, (i + 1) * STRIP)
                total = None
                pan = []
                for a in range(na):
                    pa = p[a, x, rows, :].astype(f32)
                    pan.append(pa)
                    w = pa * (base[a, rows, :] + mixed[a][rows])
                    total = w if total is None else total + w
                total = total * (-g1)
                e[j, x, rows, :] = total
                for s_i in range(na + nj):
                    src = pan[s_i] if s_i < na else o[s_i - na, x, rows, :].astype(f32)
                    m = src * total
                    m = m[:, :128] + m[:, 128:]
                    acc[s_i] = acc[s_i] + jnp.sum(m.reshape(STRIP // 8, 8, 128), axis=0)
            return tuple(acc)

        acc = lax.fori_loop(0, nx, per_out, tuple(jnp.zeros((8, 128), f32) for _ in range(na + nj)))
        for s_i in range(na + nj):
            ace[j, s_i:s_i + 1, :] = jnp.broadcast_to(jnp.sum(jnp.sum(acc[s_i], axis=0, keepdims=True), axis=1, keepdims=True), (1, 128))
        return 0

    lax.fori_loop(0, nj, per_orbital, 0)

def fields(o, olo, ohi, p, plo, phi):
    nj, nx, ny, nz = o.shape
    na = p.shape[0]
    g = poly()
    vm = pl.BlockSpec(memory_space=pltpu.VMEM)
    return pl.pallas_call(
        kernel,
        out_shape=(jax.ShapeDtypeStruct((nj, nx, ny, nz), jnp.float32), jax.ShapeDtypeStruct((nj, 8, 128), jnp.float32)),
        in_specs=[vm] * 7,
        out_specs=(vm, vm),
        scratch_shapes=[pltpu.VMEM((na, nx + 4, ny + 2 * PAD, nz), jnp.float32), pltpu.VMEM((na, ny + 2 * PAD, nz), jnp.float32),
                        pltpu.VMEM((na, ny, 3 * nz), jnp.bfloat16), pltpu.VMEM((na, ny, nz), jnp.float32)],
        compiler_params=pltpu.CompilerParams(vmem_limit_bytes=40 * 2**20),
    )(o, olo, ohi, p, plo, phi, mixing(nz, g[2] / g[1]))


def ring(count, shift):
    return [(i, (i + shift) % count) for i in range(count)]


def rows(shift, row):
    count = lax.axis_size("band")
    return [(i, i // row * row + (i + shift) % row) for i in range(count)]


def one_plane(array, index):
    return lax.dynamic_slice_in_dim(array, index, 1, 1)


def spread_panel(panel, owner):
    row = panel.shape[1]
    count = lax.axis_size("band")
    me = lax.axis_index("band")
    x, own_x = me % row, owner % row
    got = [one_plane(panel, x)]
    for k in range(1, row):
        got.append(lax.ppermute(one_plane(panel, (x + k) % row), "band", rows(k, row)))
    mine = lax.select_n((x - own_x) % row, *got)
    other = lax.ppermute(mine, "band", ring(count, row))
    mine = jnp.where(me // row == owner // row, mine, other)
    parts = [mine] + [lax.ppermute(mine, "band", rows(k, row)) for k in range(1, row)]
    turned = jnp.concatenate(parts[::-1] + parts[::-1], axis=1)
    return lax.dynamic_slice_in_dim(turned, row - 1 - x, row, 1)


def halos(array, width):
    count = lax.axis_size("dom")
    size = array.shape[1]
    low = lax.ppermute(array[:, size - width:], "dom", ring(count, 1))
    high = lax.ppermute(array[:, :width], "dom", ring(count, -1))
    return low, high


def total(part):
    count = lax.axis_size("dom")
    for group in ((1,), (2,), (4, 8, 12)):
        moved = [lax.ppermute(part, "dom", [(i, i ^ k) for i in range(count)]) for k in group]
        for m in moved:
            part = part + m
    return part


def local(orbitals, owner_band):
    low, high = halos(orbitals, 2)
    panel = spread_panel(orbitals[:PANEL], owner_band[0])
    panel_low, panel_high = halos(panel, 2)
    exchange, sums = fields(orbitals, low, high, panel, panel_low, panel_high)
    cells = float(orbitals.shape[1] * lax.axis_size("dom") * orbitals.shape[2] * orbitals.shape[3])
    sums = total(sums)
    ace_block = jnp.transpose(sums[:, :PANEL + orbitals.shape[0], 0]) / cells
    return exchange, ace_block[None]


def solution(mesh):
    placed = (P("band", "dom", None, None), P())
    return jax.shard_map(
        local,
        mesh=mesh,
        in_specs=placed,
        out_specs=(P("band", "dom", None, None), P("band", None, None)),
        check_vma=False,
    )
```

time: 408 us -> 109 us (0.27); the launches traced: 400 us -> 109 us
  other arithmetic: 87 us -> 2.66 us
  local copies, waits for them, and re-layouts: 93.9 us -> 9.69 us
  waiting for transfers between devices: 130 us -> 52.6 us
  matrix products: 36.6 us -> 0 us
  blocking collectives: 35.2 us -> 0 us
  starting transfers between devices: 1.48 us -> 22.4 us
  Pallas kernels: 0 us -> 20.5 us
  between operations: 15.2 us -> 1.52 us
    slice x10 -> x3, local copies, waits for them, and re-layouts: 80.4 us -> 2.9 us  [the longest x2 1.6 us: halos(): high = lax.ppermute(array[:, :width], 'dom', ring(count, -1))]
    psum x1 -> x0, waiting for transfers between devices: 72.7 us -> none  [spread(): return lax.psum(kept, axis)]
    dot_general x1 -> x0, matrix products: 36.6 us -> none  [local(): jnp.einsum('axyz,jxyz->aj', sources, exchange, precision=lax.Precision.HI...]
    psum x1 -> x0, blocking collectives: 35.2 us -> none  [local(): ace_block = lax.psum(partial_sums, 'dom') / cell_count]
    add x1 -> x2, other arithmetic: 33.4 us -> 0.01 us  [total(): part = part + m]
    reduce_sum x1 -> x0, other arithmetic: 31.6 us -> none  [local(): exchange = -jnp.sum(potential * panel_float[:, None], axis=0)]
    ppermute x4 -> x16, starting transfers between devices: 1.44 us -> 22.4 us  [the longest x2 7.79 us: halos(): high = lax.ppermute(array[:, :width], 'dom', ring(count, -1))]
    pallas_call x0 -> x1, Pallas kernels: none -> 20.5 us  [fields(): pl.pallas_call(kernel, out_shape=(jax.ShapeDtypeStruct((nj, nx, ny, nz),...]
  transfers between devices with their start and end apart: 5 -> 16, of which waited for: 5 -> 14; matrix products, arithmetic and copies ran while one was open for 12% -> 7% of each run, Pallas kernels for 0% -> 0%
where the time goes in v1:
time: 109 us
  waiting for transfers between devices  52.6 us (48%)
  starting transfers between devices  22.4 us (21%)
  Pallas kernels  20.5 us (19%)
  local copies, waits for them, and re-layouts  9.69 us (9%)
  other arithmetic  2.66 us (2%)
  between operations  1.52 us (1%)
    pallas_call x1, Pallas kernels, fields(): pl.pallas_call(kernel, out_shape=(jax.ShapeDtypeStruct((nj, nx, ny, nz),...  20.5 us
    ppermute x2, waiting for transfers between devices, halos(): high = lax.ppermute(array[:, :width], 'dom', ring(count, -1))  13 us
    ppermute x3, waiting for transfers between devices, spread_panel(): lax.ppermute(one_plane(panel, (x + k) % row), 'band', rows(k, row))  10.4 us
    ppermute x2, waiting for transfers between devices, halos(): low = lax.ppermute(array[:, size - width:], 'dom', ring(count, 1))  10.1 us
    ppermute x5, waiting for transfers between devices, total(): lax.ppermute(part, 'dom', [(i, i ^ k) for i in range(count)])  8.31 us
    ppermute x2, starting transfers between devices, halos(): high = lax.ppermute(array[:, :width], 'dom', ring(count, -1))  7.79 us
    unnamed x13, local copies, waits for them, and re-layouts  5.85 us
    ppermute x1, waiting for transfers between devices, spread_panel(): other = lax.ppermute(mine, 'band', ring(count, row))  5.59 us
  transfers between devices with their start and end apart: 16, of which 14 were waited for; matrix products, arithmetic and copies ran while one was open for 7% of the time, Pallas kernels for 0%

profile of v1, /device:TPU:0, one launch (start us, length us, event | category | flops | bytes accessed | tf_op | source)
XLA Modules:
  0.0 109.4 jit_solution(10853631452964626483)
XLA Ops:
  0.7 1.3 %slice.20 = bf16[2,4,256,256]{3,2,1,0:T(8,128)(2,1)S(1)} slice(bf16[4,4,256,256]{3,2,1,0:T(8,128)(2,1)} %o.1), slice={[0:2], [0:4], [0:256], [0:256]} | slice | bytes 2097152 | tf_op jit(solution)/shard_map/slice | solution.py:170
  2.0 0.0 copy-start
  2.0 0.8 constant_dynamic-slice_fusion.5
  2.9 1.6 %collective-permute-start.2 = (bf16[2,1,256,256]{3,2,1,0:T(8,128)(2,1)}, bf16[2,1,256,256]{3,2,1,0:T(8,128)(2,1)}, u32[]{:S(2)}, u32[]{:S(2)}) collective-permute-start(bf16[2,1,256,256]{3,2,1,0:T(8,128)(2,1)} %get-tuple-element.10), channel_id=1, source_target_pairs={{0,16},{16,32},{32,48},{48,0},{64,80},{80,96},{96,112},{112,64},{1... | collective-permute-start | bytes 786440 | tf_op jit(solution)/shard_map/ppermute | solution.py:142
  4.4 1.7 %collective-permute-start.4 = (bf16[2,1,256,256]{3,2,1,0:T(8,128)(2,1)}, bf16[2,1,256,256]{3,2,1,0:T(8,128)(2,1)}, u32[]{:S(2)}, u32[]{:S(2)}) collective-permute-start(bf16[2,1,256,256]{3,2,1,0:T(8,128)(2,1)} %get-tuple-element.11), channel_id=1, source_target_pairs={{0,48},{16,0},{32,16},{48,32},{64,112},{80,64},{96,80},{112,96},{1... | collective-permute-start | bytes 786440 | tf_op jit(solution)/shard_map/ppermute | solution.py:142
  6.1 1.9 %collective-permute-start.3 = (bf16[2,1,256,256]{3,2,1,0:T(8,128)(2,1)S(1)}, bf16[2,1,256,256]{3,2,1,0:T(8,128)(2,1)}, u32[]{:S(2)}, u32[]{:S(2)}) collective-permute-start(bf16[2,1,256,256]{3,2,1,0:T(8,128)(2,1)S(1)} %get-tuple-element.12), channel_id=1, source_target_pairs={{0,32},{16,48},{32,0},{48,16},{64,96},{80,112},{96,64},{112,80},{1... | collective-permute-start | bytes 786440 | tf_op jit(solution)/shard_map/ppermute | solution.py:142
  8.7 3.6 %collective-permute-done.2 = bf16[2,1,256,256]{3,2,1,0:T(8,128)(2,1)} collective-permute-done((bf16[2,1,256,256]{3,2,1,0:T(8,128)(2,1)}, bf16[2,1,256,256]{3,2,1,0:T(8,128)(2,1)}, u32[]{:S(2)}, u32[]{:S(2)}) %collective-permute-start.2) | collective-permute-done | bytes 262176 | tf_op jit(solution)/shard_map/ppermute | solution.py:142
  12.3 1.7 %collective-permute-done.4 = bf16[2,1,256,256]{3,2,1,0:T(8,128)(2,1)} collective-permute-done((bf16[2,1,256,256]{3,2,1,0:T(8,128)(2,1)}, bf16[2,1,256,256]{3,2,1,0:T(8,128)(2,1)}, u32[]{:S(2)}, u32[]{:S(2)}) %collective-permute-start.4) | collective-permute-done | bytes 262176 | tf_op jit(solution)/shard_map/ppermute | solution.py:142
  14.0 5.1 %collective-permute-done.3 = bf16[2,1,256,256]{3,2,1,0:T(8,128)(2,1)} collective-permute-done((bf16[2,1,256,256]{3,2,1,0:T(8,128)(2,1)S(1)}, bf16[2,1,256,256]{3,2,1,0:T(8,128)(2,1)}, u32[]{:S(2)}, u32[]{:S(2)}) %collective-permute-start.3) | collective-permute-done | bytes 262176 | tf_op jit(solution)/shard_map/ppermute | solution.py:142
  19.1 1.0 select_select_fusion
  20.1 0.0 copy-start.2
  20.1 1.7 %collective-permute-start.5 = (bf16[2,1,256,256]{3,2,1,0:T(8,128)(2,1)S(1)}, bf16[2,1,256,256]{3,2,1,0:T(8,128)(2,1)S(1)}, u32[]{:S(2)}, u32[]{:S(2)}) collective-permute-start(bf16[2,1,256,256]{3,2,1,0:T(8,128)(2,1)S(1)} %select_select_fusion), channel_id=1, source_target_pairs={{0,64},{16,80},{32,96},{48,112},{64,0},{80,16},{96,32},{112,48},{1... | collective-permute-start | bytes 786440 | tf_op jit(solution)/shard_map/ppermute | solution.py:144
  21.8 5.6 %collective-permute-done.5 = bf16[2,1,256,256]{3,2,1,0:T(8,128)(2,1)S(1)} collective-permute-done((bf16[2,1,256,256]{3,2,1,0:T(8,128)(2,1)S(1)}, bf16[2,1,256,256]{3,2,1,0:T(8,128)(2,1)S(1)}, u32[]{:S(2)}, u32[]{:S(2)}) %collective-permute-start.5) | collective-permute-done | bytes 262176 | tf_op jit(solution)/shard_map/ppermute | solution.py:144
  27.4 1.0 broadcast_select_fusion
  28.4 1.0 collective-permute-start.8
  29.4 2.0 %collective-permute-start.7 = (bf16[2,1,256,256]{3,2,1,0:T(8,128)(2,1)S(1)}, bf16[2,1,256,256]{3,2,1,0:T(8,128)(2,1)}, u32[]{:S(2)}, u32[]{:S(2)}) collective-permute-start(bf16[2,1,256,256]{3,2,1,0:T(8,128)(2,1)S(1)} %broadcast_select_fusion), channel_id=1, source_target_pairs={{0,32},{16,48},{32,0},{48,16},{64,96},{80,112},{96,64},{112,80},{1... | collective-permute-start | bytes 786440 | tf_op jit(solution)/shard_map/ppermute | solution.py:146
  31.4 0.7 collective-permute-start.6
  32.1 1.5 %fusion.2 = (bf16[4,2,256,256]{3,2,1,0:T(8,128)(2,1)}, bf16[4,2,256,256]{3,2,1,0:T(8,128)(2,1)}) fusion(bf16[4,4,256,256]{3,2,1,0:T(8,128)(2,1)S(1)} %copy-done), kind=kLoop, calls=%fused_computation.21 | loop fusion | bytes 4194304 | tf_op jit(solution)/shard_map/slice | solution.py:155
  33.6 3.4 %collective-permute-start.1 = (bf16[4,2,256,256]{3,2,1,0:T(8,128)(2,1)}, bf16[4,2,256,256]{3,2,1,0:T(8,128)(2,1)S(1)}, u32[]{:S(2)}, u32[]{:S(2)}) collective-permute-start(bf16[4,2,256,256]{3,2,1,0:T(8,128)(2,1)} %get-tuple-element.8), channel_id=1, source_target_pairs={{0,15},{1,0},{2,1},{3,2},{4,3},{5,4},{6,5},{7,6},{8,7},{9,8},{10,9... | collective-permute-start | bytes 3145736 | tf_op jit(solution)/shard_map/ppermute | solution.py:155
  37.1 0.0 collective-permute-start
  37.1 5.2 %collective-permute-done.6 = bf16[2,1,256,256]{3,2,1,0:T(8,128)(2,1)} collective-permute-done((bf16[2,1,256,256]{3,2,1,0:T(8,128)(2,1)S(1)}, bf16[2,1,256,256]{3,2,1,0:T(8,128)(2,1)}, u32[]{:S(2)}, u32[]{:S(2)}) %collective-permute-start.6) | collective-permute-done | bytes 262176 | tf_op jit(solution)/shard_map/ppermute | solution.py:146
  42.3 1.0 constant_dynamic-update-slice_fusion.7
  43.2 0.0 collective-permute-done.7
  43.2 1.0 constant_dynamic-update-slice_fusion.6
  44.2 0.0 collective-permute-done.8
  44.2 1.0 constant_dynamic-update-slice_fusion.5
  45.2 1.0 constant_dynamic-update-slice_fusion.3
  46.2 1.0 constant_dynamic-update-slice_fusion.2
  47.2 1.0 constant_dynamic-update-slice_fusion.1
  48.2 0.0 copy-start.1
  48.2 0.1 constant_dynamic-slice_fusion
  48.3 4.4 %collective-permute-start.10 = (bf16[2,2,256,256]{3,2,1,0:T(8,128)(2,1)S(1)}, bf16[2,2,256,256]{3,2,1,0:T(8,128)(2,1)S(1)}, u32[]{:S(2)}, u32[]{:S(2)}) collective-permute-start(bf16[2,2,256,256]{3,2,1,0:T(8,128)(2,1)S(1)} %get-tuple-element.6), channel_id=1, source_target_pairs={{0,15},{1,0},{2,1},{3,2},{4,3},{5,4},{6,5},{7,6},{8,7},{9,8},{10,9... | collective-permute-start | bytes 1572872 | tf_op jit(solution)/shard_map/ppermute | solution.py:155
  52.6 0.0 collective-permute-start.9
  52.6 0.1 constant_dynamic-slice_fusion.2.p
  52.7 8.2 %collective-permute-done.1.ohi = bf16[4,2,256,256]{3,2,1,0:T(8,128)(2,1)S(1)} collective-permute-done((bf16[4,2,256,256]{3,2,1,0:T(8,128)(2,1)}, bf16[4,2,256,256]{3,2,1,0:T(8,128)(2,1)S(1)}, u32[]{:S(2)}, u32[]{:S(2)}) %collective-permute-start.1) | collective-permute-done | bytes 1048608 | tf_op jit(solution)/shard_map/ppermute | solution.py:155
  60.9 5.6 %collective-permute-done.olo = bf16[4,2,256,256]{3,2,1,0:T(8,128)(2,1)} collective-permute-done((bf16[4,2,256,256]{3,2,1,0:T(8,128)(2,1)}, bf16[4,2,256,256]{3,2,1,0:T(8,128)(2,1)}, u32[]{:S(2)}, u32[]{:S(2)}) %collective-permute-start) | collective-permute-done | bytes 1048608 | tf_op jit(solution)/shard_map/ppermute | solution.py:154
  66.5 4.7 %collective-permute-done.10.phi = bf16[2,2,256,256]{3,2,1,0:T(8,128)(2,1)S(1)} collective-permute-done((bf16[2,2,256,256]{3,2,1,0:T(8,128)(2,1)S(1)}, bf16[2,2,256,256]{3,2,1,0:T(8,128)(2,1)S(1)}, u32[]{:S(2)}, u32[]{:S(2)}) %collective-permute-start.10) | collective-permute-done | bytes 524320 | tf_op jit(solution)/shard_map/ppermute | solution.py:155
  71.3 4.5 %collective-permute-done.9.plo = bf16[2,2,256,256]{3,2,1,0:T(8,128)(2,1)S(1)} collective-permute-done((bf16[2,2,256,256]{3,2,1,0:T(8,128)(2,1)S(1)}, bf16[2,2,256,256]{3,2,1,0:T(8,128)(2,1)S(1)}, u32[]{:S(2)}, u32[]{:S(2)}) %collective-permute-start.9) | collective-permute-done | bytes 524320 | tf_op jit(solution)/shard_map/ppermute | solution.py:154
  75.8 20.5 %shard_map.50 = (f32[4,4,256,256]{3,2,1,0:T(8,128)}, f32[4,8,128]{2,1,0:T(8,128)S(1)}) custom-call(bf16[4,4,256,256]{3,2,1,0:T(8,128)(2,1)S(1)} %copy-done, bf16[4,2,256,256]{3,2,1,0:T(8,128)(2,1)} %collective-permute-done.olo, bf16[4,2,256,256]{3,2,1,0:T(8,128)(2,1)S(1)} %collective-permute-done.1.ohi, ...), custom_call_target="tpu_custom_call" | custom-call | tf_op jit(solution)/shard_map/pallas_call | solution.py:111
  96.3 0.0 collective-permute-start.11
  96.3 1.2 %collective-permute-done.11 = f32[4,8,128]{2,1,0:T(8,128)S(1)} collective-permute-done((f32[4,8,128]{2,1,0:T(8,128)S(1)}, f32[4,8,128]{2,1,0:T(8,128)S(1)}, u32[]{:S(2)}, u32[]{:S(2)}) %collective-permute-start.11) | collective-permute-done | bytes 16416 | tf_op jit(solution)/shard_map/ppermute | solution.py:162
  97.5 5.2 %collective-permute-done.12 = f32[4,8,128]{2,1,0:T(8,128)S(1)} collective-permute-done((f32[4,8,128]{2,1,0:T(8,128)S(1)}, f32[4,8,128]{2,1,0:T(8,128)S(1)}, u32[]{:S(2)}, u32[]{:S(2)}) %collective-permute-start.12) | collective-permute-done | bytes 16416 | tf_op jit(solution)/shard_map/ppermute | solution.py:162
  102.7 0.4 collective-permute-start.15
  103.1 3.7 %collective-permute-start.13 = (f32[4,8,128]{2,1,0:T(8,128)S(1)}, f32[4,8,128]{2,1,0:T(8,128)S(1)}, u32[]{:S(2)}, u32[]{:S(2)}) collective-permute-start(f32[4,8,128]{2,1,0:T(8,128)S(1)} %add.76), channel_id=1, source_target_pairs={{0,4},{1,5},{2,6},{3,7},{4,0},{5,1},{6,2},{7,3},{8,12},{9,13},{10,... | collective-permute-start | bytes 49160 | tf_op jit(solution)/shard_map/ppermute | solution.py:162
  106.8 0.9 collective-permute-done.15
  107.7 0.7 collective-permute-done.14
  108.4 0.3 collective-permute-done.13
  108.7 0.7 fusion.1
  (9 shorter events, 0.1 us)
Async XLA Ops:
  2.0 30.1 %copy-start = (bf16[4,4,256,256]{3,2,1,0:T(8,128)(2,1)S(1)}, bf16[4,4,256,256]{3,2,1,0:T(8,128)(2,1)}, u32[]{:S(2)}) copy-start(bf16[4,4,256,256]{3,2,1,0:T(8,128)(2,1)} %o.1) | copy-start | bytes 6291460
  2.9 9.5 %collective-permute-start.2 = (bf16[2,1,256,256]{3,2,1,0:T(8,128)(2,1)}, bf16[2,1,256,256]{3,2,1,0:T(8,128)(2,1)}, u32[]{:S(2)}, u32[]{:S(2)}) collective-permute-start(bf16[2,1,256,256]{3,2,1,0:T(8,128)(2,1)} %get-tuple-element.10), channel_id=1, source_target_pairs={{0,16},{16,32},{32,48},{48,0},{64,80},{80,96},{96,112},{112,64},{1... | collective-permute-start | bytes 786440 | tf_op jit(solution)/shard_map/ppermute | solution.py:142
  4.4 9.5 %collective-permute-start.4 = (bf16[2,1,256,256]{3,2,1,0:T(8,128)(2,1)}, bf16[2,1,256,256]{3,2,1,0:T(8,128)(2,1)}, u32[]{:S(2)}, u32[]{:S(2)}) collective-permute-start(bf16[2,1,256,256]{3,2,1,0:T(8,128)(2,1)} %get-tuple-element.11), channel_id=1, source_target_pairs={{0,48},{16,0},{32,16},{48,32},{64,112},{80,64},{96,80},{112,96},{1... | collective-permute-start | bytes 786440 | tf_op jit(solution)/shard_map/ppermute | solution.py:142
  6.1 13.0 %collective-permute-start.3 = (bf16[2,1,256,256]{3,2,1,0:T(8,128)(2,1)S(1)}, bf16[2,1,256,256]{3,2,1,0:T(8,128)(2,1)}, u32[]{:S(2)}, u32[]{:S(2)}) collective-permute-start(bf16[2,1,256,256]{3,2,1,0:T(8,128)(2,1)S(1)} %get-tuple-element.12), channel_id=1, source_target_pairs={{0,32},{16,48},{32,0},{48,16},{64,96},{80,112},{96,64},{112,80},{1... | collective-permute-start | bytes 786440 | tf_op jit(solution)/shard_map/ppermute | solution.py:142
  20.1 1.7 %copy-start.2 = (bf16[2,1,256,256]{3,2,1,0:T(8,128)(2,1)}, bf16[2,1,256,256]{3,2,1,0:T(8,128)(2,1)S(1)}, u32[]{:S(2)}) copy-start(bf16[2,1,256,256]{3,2,1,0:T(8,128)(2,1)S(1)} %select_select_fusion) | copy-start | bytes 786436
  20.1 7.3 %collective-permute-start.5 = (bf16[2,1,256,256]{3,2,1,0:T(8,128)(2,1)S(1)}, bf16[2,1,256,256]{3,2,1,0:T(8,128)(2,1)S(1)}, u32[]{:S(2)}, u32[]{:S(2)}) collective-permute-start(bf16[2,1,256,256]{3,2,1,0:T(8,128)(2,1)S(1)} %select_select_fusion), channel_id=1, source_target_pairs={{0,64},{16,80},{32,96},{48,112},{64,0},{80,16},{96,32},{112,48},{1... | collective-permute-start | bytes 786440 | tf_op jit(solution)/shard_map/ppermute | solution.py:144
  28.4 15.8 %collective-permute-start.8 = (bf16[2,1,256,256]{3,2,1,0:T(8,128)(2,1)S(1)}, bf16[2,1,256,256]{3,2,1,0:T(8,128)(2,1)}, u32[]{:S(2)}, u32[]{:S(2)}) collective-permute-start(bf16[2,1,256,256]{3,2,1,0:T(8,128)(2,1)S(1)} %broadcast_select_fusion), channel_id=1, source_target_pairs={{0,16},{16,32},{32,48},{48,0},{64,80},{80,96},{96,112},{112,64},{1... | collective-permute-start | bytes 786440 | tf_op jit(solution)/shard_map/ppermute | solution.py:146
  29.4 13.9 %collective-permute-start.7 = (bf16[2,1,256,256]{3,2,1,0:T(8,128)(2,1)S(1)}, bf16[2,1,256,256]{3,2,1,0:T(8,128)(2,1)}, u32[]{:S(2)}, u32[]{:S(2)}) collective-permute-start(bf16[2,1,256,256]{3,2,1,0:T(8,128)(2,1)S(1)} %broadcast_select_fusion), channel_id=1, source_target_pairs={{0,32},{16,48},{32,0},{48,16},{64,96},{80,112},{96,64},{112,80},{1... | collective-permute-start | bytes 786440 | tf_op jit(solution)/shard_map/ppermute | solution.py:146
  31.4 10.9 %collective-permute-start.6 = (bf16[2,1,256,256]{3,2,1,0:T(8,128)(2,1)S(1)}, bf16[2,1,256,256]{3,2,1,0:T(8,128)(2,1)}, u32[]{:S(2)}, u32[]{:S(2)}) collective-permute-start(bf16[2,1,256,256]{3,2,1,0:T(8,128)(2,1)S(1)} %broadcast_select_fusion), channel_id=1, source_target_pairs={{0,48},{16,0},{32,16},{48,32},{64,112},{80,64},{96,80},{112,96},{1... | collective-permute-start | bytes 786440 | tf_op jit(solution)/shard_map/ppermute | solution.py:146
  33.6 27.3 %collective-permute-start.1 = (bf16[4,2,256,256]{3,2,1,0:T(8,128)(2,1)}, bf16[4,2,256,256]{3,2,1,0:T(8,128)(2,1)S(1)}, u32[]{:S(2)}, u32[]{:S(2)}) collective-permute-start(bf16[4,2,256,256]{3,2,1,0:T(8,128)(2,1)} %get-tuple-element.8), channel_id=1, source_target_pairs={{0,15},{1,0},{2,1},{3,2},{4,3},{5,4},{6,5},{7,6},{8,7},{9,8},{10,9... | collective-permute-start | bytes 3145736 | tf_op jit(solution)/shard_map/ppermute | solution.py:155
  37.1 29.5 %collective-permute-start = (bf16[4,2,256,256]{3,2,1,0:T(8,128)(2,1)}, bf16[4,2,256,256]{3,2,1,0:T(8,128)(2,1)}, u32[]{:S(2)}, u32[]{:S(2)}) collective-permute-start(bf16[4,2,256,256]{3,2,1,0:T(8,128)(2,1)} %get-tuple-element.9), channel_id=1, source_target_pairs={{0,1},{1,2},{2,3},{3,4},{4,5},{5,6},{6,7},{7,8},{8,9},{9,10},{10,1... | collective-permute-start | bytes 3145736 | tf_op jit(solution)/shard_map/ppermute | solution.py:154
  48.2 27.6 %copy-start.1 = (bf16[768,256]{1,0:T(8,128)(2,1)S(1)}, bf16[768,256]{1,0:T(8,128)(2,1)}, u32[]{:S(2)}) copy-start(bf16[768,256]{1,0:T(8,128)(2,1)} %constant.73.mix) | copy-start | bytes 1179652
  48.3 23.0 %collective-permute-start.10 = (bf16[2,2,256,256]{3,2,1,0:T(8,128)(2,1)S(1)}, bf16[2,2,256,256]{3,2,1,0:T(8,128)(2,1)S(1)}, u32[]{:S(2)}, u32[]{:S(2)}) collective-permute-start(bf16[2,2,256,256]{3,2,1,0:T(8,128)(2,1)S(1)} %get-tuple-element.6), channel_id=1, source_target_pairs={{0,15},{1,0},{2,1},{3,2},{4,3},{5,4},{6,5},{7,6},{8,7},{9,8},{10,9... | collective-permute-start | bytes 1572872 | tf_op jit(solution)/shard_map/ppermute | solution.py:155
  52.6 23.1 %collective-permute-start.9 = (bf16[2,2,256,256]{3,2,1,0:T(8,128)(2,1)S(1)}, bf16[2,2,256,256]{3,2,1,0:T(8,128)(2,1)S(1)}, u32[]{:S(2)}, u32[]{:S(2)}) collective-permute-start(bf16[2,2,256,256]{3,2,1,0:T(8,128)(2,1)S(1)} %get-tuple-element.7), channel_id=1, source_target_pairs={{0,1},{1,2},{2,3},{3,4},{4,5},{5,6},{6,7},{7,8},{8,9},{9,10},{10,1... | collective-permute-start | bytes 1572872 | tf_op jit(solution)/shard_map/ppermute | solution.py:154
  96.3 1.2 %collective-permute-start.11 = (f32[4,8,128]{2,1,0:T(8,128)S(1)}, f32[4,8,128]{2,1,0:T(8,128)S(1)}, u32[]{:S(2)}, u32[]{:S(2)}) collective-permute-start(f32[4,8,128]{2,1,0:T(8,128)S(1)} %get-tuple-element.5), channel_id=1, source_target_pairs={{0,1},{1,0},{2,3},{3,2},{4,5},{5,4},{6,7},{7,6},{8,9},{9,8},{10,11... | collective-permute-start | bytes 49160 | tf_op jit(solution)/shard_map/ppermute | solution.py:162
  97.5 5.2 %collective-permute-start.12 = (f32[4,8,128]{2,1,0:T(8,128)S(1)}, f32[4,8,128]{2,1,0:T(8,128)S(1)}, u32[]{:S(2)}, u32[]{:S(2)}) collective-permute-start(f32[4,8,128]{2,1,0:T(8,128)S(1)} %add.75), channel_id=1, source_target_pairs={{0,2},{1,3},{2,0},{3,1},{4,6},{5,7},{6,4},{7,5},{8,10},{9,11},{10,... | collective-permute-start | bytes 49160 | tf_op jit(solution)/shard_map/ppermute | solution.py:162
  102.7 4.9 %collective-permute-start.15 = (f32[4,8,128]{2,1,0:T(8,128)S(1)}, f32[4,8,128]{2,1,0:T(8,128)S(1)}, u32[]{:S(2)}, u32[]{:S(2)}) collective-permute-start(f32[4,8,128]{2,1,0:T(8,128)S(1)} %add.76), channel_id=1, source_target_pairs={{0,12},{1,13},{2,14},{3,15},{4,8},{5,9},{6,10},{7,11},{8,4},{9,5},... | collective-permute-start | bytes 49160 | tf_op jit(solution)/shard_map/ppermute | solution.py:162
  103.1 5.2 %collective-permute-start.14 = (f32[4,8,128]{2,1,0:T(8,128)S(1)}, f32[4,8,128]{2,1,0:T(8,128)S(1)}, u32[]{:S(2)}, u32[]{:S(2)}) collective-permute-start(f32[4,8,128]{2,1,0:T(8,128)S(1)} %add.76), channel_id=1, source_target_pairs={{0,8},{1,9},{2,10},{3,11},{4,12},{5,13},{6,14},{7,15},{8,0},{9,1},... | collective-permute-start | bytes 49160 | tf_op jit(solution)/shard_map/ppermute | solution.py:162
  103.1 5.6 %collective-permute-start.13 = (f32[4,8,128]{2,1,0:T(8,128)S(1)}, f32[4,8,128]{2,1,0:T(8,128)S(1)}, u32[]{:S(2)}, u32[]{:S(2)}) collective-permute-start(f32[4,8,128]{2,1,0:T(8,128)S(1)} %add.76), channel_id=1, source_target_pairs={{0,4},{1,5},{2,6},{3,7},{4,0},{5,1},{6,2},{7,3},{8,12},{9,13},{10,... | collective-permute-start | bytes 49160 | tf_op jit(solution)/shard_map/ppermute | solution.py:162

commit v2 on v1

v2 whole, which is shorter than its diff:
```python
import math

import jax
import jax.numpy as jnp
import numpy as np
from jax import lax
from jax.experimental import pallas as pl
from jax.experimental.pallas import tpu as pltpu
from jax.sharding import PartitionSpec as P

PANEL, SWEEPS, SCREEN = 2, 3, 0.1
PAD = 8
STRIP = 32


def polynomial():
    d = 6.0 + SCREEN
    w = [1.0 / (1.0 + 6.0 / d * math.cos(math.pi * (2 * k + 1) / (2 * SWEEPS))) for k in range(SWEEPS)]
    p = [w[0] / d]
    for k in range(1, SWEEPS):
        n = [0.0] * (len(p) + 1)
        for i, c in enumerate(p):
            n[i] += c * (1.0 - w[k])
            n[i + 1] += c * w[k] / d
        n[0] += w[k] / d
        p = n
    return p


def mixing(nz, beta):
    near = np.zeros((nz, nz), np.float32)
    far = np.zeros((nz, nz), np.float32)
    for z in range(nz):
        for s, m in ((1, near), (2, far)):
            m[(z - s) % nz, z] += 1.0
            m[(z + s) % nz, z] += 1.0
    return jnp.asarray(np.concatenate([near, near, beta * far], 0)).astype(jnp.bfloat16)


def at(ref, idx, start, size):
    return ref[(*idx, slice(start, start + size), slice(None))]


def wrap(ref, idx, ny, width):
    ref[(*idx, slice(PAD - width, PAD), slice(None))] = at(ref, idx, PAD + ny - width, width)
    ref[(*idx, slice(PAD + ny, PAD + ny + width), slice(None))] = at(ref, idx, PAD, width)


def split(left, a, rows, nz, v):
    hi = v.astype(jnp.bfloat16)
    left[a, rows, :nz] = hi
    left[a, rows, nz:2 * nz] = (v - hi.astype(jnp.float32)).astype(jnp.bfloat16)


def inner_kernel(o, p, mix, e, rho, *scratch):
    g0, g1, g2 = polynomial()
    beta = g2 / g1
    kappa = g0 / g1 + 6.0 * beta
    na, nx, ny, nz = p.shape
    steps = ny // STRIP
    f32, bf = jnp.float32, jnp.bfloat16
    sigs, lefts, bases = scratch[0:2], scratch[2:4], scratch[4:6]

    for x in range(nx):
        for i in range(steps):
            ov = at(o, (0, x), i * STRIP, STRIP).astype(f32)
            for a in range(na):
                rho[a, x, PAD + i * STRIP:PAD + (i + 1) * STRIP, :] = at(p, (a, x), i * STRIP, STRIP).astype(f32) * ov
        for a in range(na):
            wrap(rho, (a, x), ny, 2)

    def prepare(x):
        sig, left, base = sigs[x % 2], lefts[x % 2], bases[x % 2]
        near = [n for n in (x - 1, x + 1) if 0 <= n < nx]
        apart = [n for n in (x - 2, x + 2) if 0 <= n < nx]
        if len(near) > 1:
            for a in range(na):
                for r in range(0, ny + 2 * PAD, 16):
                    sig[a, r:r + 16, :] = at(rho, (a, near[0]), r, 16) + at(rho, (a, near[1]), r, 16)
        for a in range(na):
            s_ref, s_idx = (sig, (a,)) if len(near) > 1 else (rho, (a, near[0]))
            for i in range(steps):
                r = PAD + i * STRIP
                rows = slice(i * STRIP, (i + 1) * STRIP)
                c = at(rho, (a, x), r, STRIP)
                q = at(s_ref, s_idx, r, STRIP) + (at(rho, (a, x), r - 1, STRIP) + at(rho, (a, x), r + 1, STRIP))
                far = at(rho, (a, x), r - 2, STRIP) + at(rho, (a, x), r + 2, STRIP)
                for n in apart:
                    far = far + at(rho, (a, n), r, STRIP)
                side = at(s_ref, s_idx, r - 1, STRIP) + at(s_ref, s_idx, r + 1, STRIP)
                split(left, a, rows, nz, c + (2.0 * beta) * q)
                left[a, rows, 2 * nz:] = c.astype(bf)
                base[a, rows, :] = (kappa * c + q) + beta * (far + (side + side))

    def finish(x):
        left, base = lefts[x % 2], bases[x % 2]
        mixed = [jnp.dot(left[a], mix[...], preferred_element_type=f32) for a in range(na)]
        for i in range(steps):
            rows = slice(i * STRIP, (i + 1) * STRIP)
            total = None
            for a in range(na):
                w = at(p, (a, x), i * STRIP, STRIP).astype(f32) * (base[a, rows, :] + mixed[a][rows])
                total = w if total is None else total + w
            e[0, x, rows, :] = total * (-g1)

    prepare(0)
    for x in range(1, nx):
        prepare(x)
        finish(x - 1)
    finish(nx - 1)


def inner(o, p):
    nj, nx, ny, nz = o.shape
    na = p.shape[0]
    g = polynomial()
    f32, bf = jnp.float32, jnp.bfloat16
    mix = mixing(nz, g[2] / g[1])
    return pl.pallas_call(
        inner_kernel,
        grid=(nj,),
        out_shape=jax.ShapeDtypeStruct((nj, nx, ny, nz), f32),
        in_specs=[
            pl.BlockSpec((1, nx, ny, nz), lambda j: (j, 0, 0, 0)),
            pl.BlockSpec((na, nx, ny, nz), lambda j: (0, 0, 0, 0)),
            pl.BlockSpec(mix.shape, lambda j: (0, 0)),
        ],
        out_specs=pl.BlockSpec((1, nx, ny, nz), lambda j: (j, 0, 0, 0)),
        scratch_shapes=[pltpu.VMEM((na, nx, ny + 2 * PAD, nz), f32)]
        + [pltpu.VMEM((na, ny + 2 * PAD, nz), f32)] * 2
        + [pltpu.VMEM((na, ny, 3 * nz), bf)] * 2
        + [pltpu.VMEM((na, ny, nz), f32)] * 2,
        compiler_params=pltpu.CompilerParams(vmem_limit_bytes=40 * 2**20),
        cost_estimate=pl.CostEstimate(flops=6 * 10**9, bytes_accessed=8 * 2**20, transcendentals=0),
        name="inner_field",
    )(o, p, mix)


def outer_kernel(e_in, o, near_low, far_low, near_high, far_high, p, plo, phi, mix, e, ace, *scratch):
    g0, g1, g2 = polynomial()
    beta = g2 / g1
    na, nx, ny, nz = p.shape
    nj = o.shape[0]
    steps = ny // STRIP
    f32, bf = jnp.float32, jnp.bfloat16
    rhos, lefts, bases = scratch[0:2], scratch[2:4], scratch[4:6]
    sides = ((0, near_low, far_low, plo, 1, 0, 0, 1), (1, near_high, far_high, phi, 0, 1, nx - 1, nx - 2))

    def prepare(s, near, far, ph, h1, h2, t0, t1):
        rho, left, base = rhos[s], lefts[s], bases[s]
        for i in range(steps):
            ov = at(near, (0, 0), i * STRIP, STRIP).astype(f32)
            for a in range(na):
                rho[a, PAD + i * STRIP:PAD + (i + 1) * STRIP, :] = at(ph, (a, h1), i * STRIP, STRIP).astype(f32) * ov
        for a in range(na):
            wrap(rho, (a,), ny, 1)
        for i in range(steps):
            r = PAD + i * STRIP
            rows = slice(i * STRIP, (i + 1) * STRIP)
            ov = at(far, (0, 0), i * STRIP, STRIP).astype(f32)
            step = None
            for a in range(na):
                c = at(rho, (a,), r, STRIP)
                split(left, a, rows, nz, c)
                y = at(rho, (a,), r - 1, STRIP) + at(rho, (a,), r + 1, STRIP)
                base[a, rows, :] = (c + beta * (at(ph, (a, h2), i * STRIP, STRIP).astype(f32) * ov)) + (2.0 * beta) * y
                w = at(p, (a, t1), i * STRIP, STRIP).astype(f32) * c
                step = w if step is None else step + w
            e[0, t1, rows, :] = at(e_in, (0, t1), i * STRIP, STRIP) + step * (-g1 * beta)

    def finish(s, near, far, ph, h1, h2, t0, t1):
        left, base = lefts[s], bases[s]
        mixed = [jnp.dot(left[a], mix[:2 * nz, :], preferred_element_type=f32) for a in range(na)]
        for i in range(steps):
            rows = slice(i * STRIP, (i + 1) * STRIP)
            step = None
            for a in range(na):
                w = at(p, (a, t0), i * STRIP, STRIP).astype(f32) * (base[a, rows, :] + (2.0 * beta) * mixed[a][rows])
                step = w if step is None else step + w
            e[0, t0, rows, :] = at(e_in, (0, t0), i * STRIP, STRIP) + step * (-g1)

    prepare(*sides[0])
    prepare(*sides[1])
    finish(*sides[0])
    finish(*sides[1])

    def project(x, acc):
        acc = list(acc)
        for i in range(steps):
            field = at(e, (0, x), i * STRIP, STRIP)
            for s in range(na + nj):
                source = at(p, (s, x), i * STRIP, STRIP) if s < na else at(o, (s - na, x), i * STRIP, STRIP)
                m = source.astype(f32) * field
                m = m[:, :128] + m[:, 128:]
                acc[s] = acc[s] + jnp.sum(m.reshape(STRIP // 8, 8, 128), axis=0)
        return tuple(acc)

    acc = lax.fori_loop(0, nx, project, tuple(jnp.zeros((8, 128), f32) for _ in range(na + nj)))
    for s in range(na + nj):
        part = jnp.sum(jnp.sum(acc[s], axis=0, keepdims=True), axis=1, keepdims=True)
        ace[0, s:s + 1, :] = jnp.broadcast_to(part, (1, 128))


def outer(e, o, halo, p, plo, phi):
    nj, nx, ny, nz = o.shape
    na = p.shape[0]
    g = polynomial()
    f32, bf = jnp.float32, jnp.bfloat16
    mix = mixing(nz, g[2] / g[1])
    each = lambda shape: pl.BlockSpec((1, *shape[1:]), lambda j: (j, *(0,) * (len(shape) - 1)))
    whole = lambda shape: pl.BlockSpec(shape, lambda j: (0,) * len(shape))
    return pl.pallas_call(
        outer_kernel,
        grid=(nj,),
        out_shape=(jax.ShapeDtypeStruct(e.shape, f32), jax.ShapeDtypeStruct((nj, 8, 128), f32)),
        in_specs=[each(e.shape), whole(o.shape), *[each(h.shape) for h in halo], whole(p.shape), whole(plo.shape), whole(phi.shape), whole(mix.shape)],
        out_specs=(each(e.shape), each((nj, 8, 128))),
        input_output_aliases={0: 0},
        scratch_shapes=[pltpu.VMEM((na, ny + 2 * PAD, nz), f32)] * 2
        + [pltpu.VMEM((na, ny, 2 * nz), bf)] * 2
        + [pltpu.VMEM((na, ny, nz), f32)] * 2,
        compiler_params=pltpu.CompilerParams(vmem_limit_bytes=40 * 2**20),
        cost_estimate=pl.CostEstimate(flops=3 * 10**9, bytes_accessed=14 * 2**20, transcendentals=0),
        name="outer_field",
    )(e, o, *halo, p, plo, phi, mix)


def cut_kernel(row, orbitals, *refs):
    parts = refs[:PANEL * row]
    held, loaded, stored = refs[PANEL * row:]
    x = lax.rem(lax.axis_index("band"), row)
    loads = [pltpu.make_async_copy(orbitals.at[a], held.at[a], loaded.at[a]) for a in range(PANEL)]
    stores = [
        pltpu.make_async_copy(held.at[a, lax.rem(x + k, row)], parts[a * row + k], stored.at[a * row + k])
        for a in range(PANEL)
        for k in range(row)
    ]
    for a in range(PANEL):
        loads[a].start()
    for a in range(PANEL):
        loads[a].wait()
        for k in range(row):
            stores[a * row + k].start()
    for c in stores:
        c.wait()


def cut(orbitals):
    row, ny, nz = orbitals.shape[1:]
    part = jax.ShapeDtypeStruct((ny, nz), orbitals.dtype)
    anywhere = pl.BlockSpec(memory_space=pl.ANY)
    parts = pl.pallas_call(
        lambda *refs: cut_kernel(row, *refs),
        out_shape=(part,) * (PANEL * row),
        in_specs=[anywhere],
        out_specs=(anywhere,) * (PANEL * row),
        scratch_shapes=[
            pltpu.VMEM((PANEL, row, ny, nz), orbitals.dtype),
            pltpu.SemaphoreType.DMA((PANEL,)),
            pltpu.SemaphoreType.DMA((PANEL * row,)),
        ],
        name="cut_panel",
    )(orbitals)
    return [parts[a * row:(a + 1) * row] for a in range(PANEL)]


def join_kernel(row, *refs):
    parts, (panel, top, bottom), (held, loaded, stored) = refs[:PANEL * row], refs[PANEL * row:-3], refs[-3:]
    x = lax.rem(lax.axis_index("band"), row)
    loads = [
        pltpu.make_async_copy(parts[a * row + k], held.at[a, lax.rem(x + row - k, row)], loaded.at[a * row + k])
        for a in range(PANEL)
        for k in range(row)
    ]
    stores = [
        pltpu.make_async_copy(held.at[:, row - 2:], top, stored.at[0]),
        pltpu.make_async_copy(held.at[:, :2], bottom, stored.at[1]),
        pltpu.make_async_copy(held, panel, stored.at[2]),
    ]
    for c in loads:
        c.start()
    for c in loads:
        c.wait()
    for c in stores:
        c.start()
    for c in stores:
        c.wait()


def join(parts):
    row = len(parts) // PANEL
    ny, nz = parts[0].shape
    dtype = parts[0].dtype
    anywhere = pl.BlockSpec(memory_space=pl.ANY)
    edge = jax.ShapeDtypeStruct((PANEL, 2, ny, nz), dtype)
    return pl.pallas_call(
        lambda *refs: join_kernel(row, *refs),
        out_shape=(jax.ShapeDtypeStruct((PANEL, row, ny, nz), dtype), edge, edge),
        in_specs=[anywhere] * (PANEL * row),
        out_specs=(anywhere,) * 3,
        scratch_shapes=[
            pltpu.VMEM((PANEL, row, ny, nz), dtype),
            pltpu.SemaphoreType.DMA((PANEL * row,)),
            pltpu.SemaphoreType.DMA((3,)),
        ],
        name="join_panel",
    )(*parts)


def ring(count, shift):
    return [(i, (i + shift) % count) for i in range(count)]


def rows(shift, row):
    count = lax.axis_size("band")
    return [(i, i // row * row + (i + shift) % row) for i in range(count)]


def total(part):
    count = lax.axis_size("dom")
    for group in ((1,), (2,), (4, 8, 12)):
        moved = [lax.ppermute(part, "dom", [(i, i ^ k) for i in range(count)]) for k in group]
        for m in moved:
            part = part + m
    return part


def local(orbitals, owner_band):
    nj, nx, ny, nz = orbitals.shape
    row = nx
    me = lax.axis_index("band")
    owner = owner_band[0]
    behind = lax.rem(me + row - lax.rem(owner, row), row)
    same = lax.div(me, row) == lax.div(owner, row)
    up = lambda v: lax.ppermute(v, "dom", ring(lax.axis_size("dom"), 1))
    down = lambda v: lax.ppermute(v, "dom", ring(lax.axis_size("dom"), -1))
    along = lambda v, k: lax.ppermute(v, "band", rows(k, row))
    across = lambda v: lax.ppermute(v, "band", ring(lax.axis_size("band"), row))
    plane = lambda v, x: v[:, x:x + 1]

    pieces = cut(orbitals)
    got = [[pieces[a][0]] + [along(pieces[a][k], k) for k in range(1, row)] for a in range(PANEL)]
    mine = [lax.select_n(behind, *g) for g in got]
    mine[0], *near = lax.optimization_barrier((mine[0], plane(orbitals, nx - 1), plane(orbitals, 0)))
    near = (up(near[0]), down(near[1]))
    mine = [jnp.where(same, m, across(m)) for m in mine]
    parts = [[m, *[along(m, k) for k in range(1, row)]] for m in mine]
    *parts[0], near_low, near_high, far_low, far_high = lax.optimization_barrier(
        (*parts[0], *near, plane(orbitals, nx - 2), plane(orbitals, 1)))
    near, far = (near_low, near_high), (up(far_low), down(far_high))
    panel, top, bottom = join(parts[0] + parts[1])
    low, high = up(top), down(bottom)
    exchange = inner(orbitals, panel)
    exchange, sums = outer(exchange, orbitals, (near[0], far[0], near[1], far[1]), panel, low, high)
    cells = float(nx * lax.axis_size("dom") * ny * nz)
    ace_block = jnp.transpose(total(sums)[:, :PANEL + nj, 0]) / cells
    return exchange, ace_block[None]


def solution(mesh):
    placed = (P("band", "dom", None, None), P())
    return jax.shard_map(
        local,
        mesh=mesh,
        in_specs=placed,
        out_specs=(P("band", "dom", None, None), P("band", None, None)),
        check_vma=False,
    )
```

time: 109 us -> 91.4 us (0.84)
  waiting for transfers between devices: 52.6 us -> 13.1 us
  starting transfers between devices: 22.4 us -> 42.7 us
  Pallas kernels: 20.5 us -> 27.7 us
  local copies, waits for them, and re-layouts: 9.69 us -> 5.41 us
  other arithmetic: 2.66 us -> 0.78 us
    ppermute x11 -> x20, waiting for transfers between devices: 44.3 us -> 3.58 us  [the longest x12 3.56 us: local(): along = lambda v, k: lax.ppermute(v, 'band', rows(k, row))]
    ppermute x11 -> x20, starting transfers between devices: 18.3 us -> 38.6 us  [the longest x12 19.1 us: local(): along = lambda v, k: lax.ppermute(v, 'band', rows(k, row))]
    pallas_call x1 -> x4, Pallas kernels: 20.5 us -> 27.7 us  [the longest x1 13.9 us: inner(): pl.pallas_call(inner_kernel, grid=(nj,), out_shape=jax.ShapeDtypeStruct((...]
    unnamed x13 -> x28, local copies, waits for them, and re-layouts: 5.85 us -> 2.54 us
    select_n x2 -> x4, other arithmetic: 1.98 us -> 0.1 us  [the longest x2 0.07 us: local(): mine = [lax.select_n(behind, *g) for g in got]]
    ppermute x5, waiting for transfers between devices: 8.31 us -> 9.49 us  [total(): lax.ppermute(part, 'dom', [(i, i ^ k) for i in range(count)])]
    slice x3 -> x1, local copies, waits for them, and re-layouts: 2.9 us -> 2.87 us  [local(): plane = lambda v, x: v[:, x:x + 1]]
  transfers between devices with their start and end apart: 16 -> 25, of which waited for: 14 -> 7; matrix products, arithmetic and copies ran while one was open for 7% -> 3% of each run, Pallas kernels for 0% -> 18%
where the time goes in v2:
time: 91.4 us; the launch traced here: 91.1 us
  starting transfers between devices  42.7 us (47%)
  Pallas kernels  27.7 us (30%)
  waiting for transfers between devices  13.1 us (14%)
  local copies, waits for them, and re-layouts  5.41 us (6%)
  between operations  1.51 us (2%)
    ppermute x12, starting transfers between devices, local(): along = lambda v, k: lax.ppermute(v, 'band', rows(k, row))  19.1 us
    ppermute x3, starting transfers between devices, local(): down = lambda v: lax.ppermute(v, 'dom', ring(lax.axis_size('dom'), -1))  15.9 us
    pallas_call x1, Pallas kernels, inner(): pl.pallas_call(inner_kernel, grid=(nj,), out_shape=jax.ShapeDtypeStruct((...  13.9 us
    ppermute x5, waiting for transfers between devices, total(): lax.ppermute(part, 'dom', [(i, i ^ k) for i in range(count)])  9.49 us
    pallas_call x1, Pallas kernels, outer(): pl.pallas_call(outer_kernel, grid=(nj,), out_shape=(jax.ShapeDtypeStruct(...  8.95 us
    ppermute x5, starting transfers between devices, total(): lax.ppermute(part, 'dom', [(i, i ^ k) for i in range(count)])  4.1 us
    ppermute x12, waiting for transfers between devices, local(): along = lambda v, k: lax.ppermute(v, 'band', rows(k, row))  3.56 us
    ppermute x2, starting transfers between devices, local(): across = lambda v: lax.ppermute(v, 'band', ring(lax.axis_size('band'), row))  3.31 us
  transfers between devices with their start and end apart: 25, of which 7 were waited for; matrix products, arithmetic and copies ran while one was open for 3% of the time, Pallas kernels for 18%

profile of v2, /device:TPU:0, one launch (start us, length us, event | category | flops | bytes accessed | tf_op | source)
XLA Modules:
  0.0 91.1 jit_solution(15693366791484651752)
XLA Ops:
  0.6 2.1 %cut_panel.1 = (bf16[256,256]{1,0:T(8,128)(2,1)}, bf16[256,256]{1,0:T(8,128)(2,1)}, bf16[256,256]{1,0:T(8,128)(2,1)}, bf16[256,256]{1,0:T(8,128)(2,1)}, bf16[256...) custom-call(bf16[4,4,256,256]{3,2,1,0:T(8,128)(2,1)} %o.3), custom_call_target="tpu_custom_call" | custom-call | tf_op jit(solution)/shard_map/cut_panel/pallas_call | solution.py:252
  2.8 0.0 copy-start
  2.8 0.0 copy-start.3
  2.8 1.6 %collective-permute-start = (bf16[256,256]{1,0:T(8,128)(2,1)}, bf16[256,256]{1,0:T(8,128)(2,1)S(1)}, u32[]{:S(2)}, u32[]{:S(2)}) collective-permute-start(bf16[256,256]{1,0:T(8,128)(2,1)} %get-tuple-element.27), channel_id=1, source_target_pairs={{0,16},{16,32},{32,48},{48,0},{64,80},{80,96},{96,112},{112,64},{1... | collective-permute-start | bytes 393224 | tf_op jit(solution)/shard_map/ppermute | solution.py:337
  4.4 2.7 %collective-permute-start.1 = (bf16[256,256]{1,0:T(8,128)(2,1)}, bf16[256,256]{1,0:T(8,128)(2,1)S(1)}, u32[]{:S(2)}, u32[]{:S(2)}) collective-permute-start(bf16[256,256]{1,0:T(8,128)(2,1)} %get-tuple-element.28), channel_id=1, source_target_pairs={{0,32},{16,48},{32,0},{48,16},{64,96},{80,112},{96,64},{112,80},{1... | collective-permute-start | bytes 393224 | tf_op jit(solution)/shard_map/ppermute | solution.py:337
  7.2 1.4 %collective-permute-start.2 = (bf16[256,256]{1,0:T(8,128)(2,1)}, bf16[256,256]{1,0:T(8,128)(2,1)S(1)}, u32[]{:S(2)}, u32[]{:S(2)}) collective-permute-start(bf16[256,256]{1,0:T(8,128)(2,1)} %get-tuple-element.29), channel_id=1, source_target_pairs={{0,48},{16,0},{32,16},{48,32},{64,112},{80,64},{96,80},{112,96},{1... | collective-permute-start | bytes 393224 | tf_op jit(solution)/shard_map/ppermute | solution.py:337
  8.6 0.6 collective-permute-start.9
  9.2 0.9 collective-permute-start.10
  10.1 2.9 %fusion.2 = (bf16[4,1,256,256]{3,2,1,0:T(8,128)(2,1)}, bf16[4,1,256,256]{3,2,1,0:T(8,128)(2,1)}, bf16[4,1,256,256]{3,2,1,0:T(8,128)(2,1)}, bf16[4,1,256,256]{3,2,1,0:T(8,128)(2,1)}) fusion(bf16[4,4,256,256]{3,2,1,0:T(8,128)(2,1)} %o.3), kind=kLoop, calls=%fused_computation.9 | loop fusion | bytes 4194304 | tf_op jit(solution)/shard_map/slice | solution.py:339
  13.6 0.0 collective-permute-done
  13.6 1.9 %collective-permute-start.11 = (bf16[256,256]{1,0:T(8,128)(2,1)S(1)}, bf16[256,256]{1,0:T(8,128)(2,1)S(1)}, u32[]{:S(2)}, u32[]{:S(2)}) collective-permute-start(bf16[256,256]{1,0:T(8,128)(2,1)S(1)} %copy-done.13), channel_id=1, source_target_pairs={{0,48},{16,0},{32,16},{48,32},{64,112},{80,64},{96,80},{112,96},{1... | collective-permute-start | bytes 393224 | tf_op jit(solution)/shard_map/ppermute | solution.py:337
  15.5 1.7 %collective-permute-start.3 = (bf16[256,256]{1,0:T(8,128)(2,1)S(1)}, bf16[256,256]{1,0:T(8,128)(2,1)S(1)}, u32[]{:S(2)}, u32[]{:S(2)}) collective-permute-start(bf16[256,256]{1,0:T(8,128)(2,1)S(1)} %select_select_fusion.1), channel_id=1, source_target_pairs={{0,64},{16,80},{32,96},{48,112},{64,0},{80,16},{96,32},{112,48},{1... | collective-permute-start | bytes 393224 | tf_op jit(solution)/shard_map/ppermute | solution.py:338
  17.2 0.0 collective-permute-done.9
  17.2 1.8 %collective-permute-done.10 = bf16[256,256]{1,0:T(8,128)(2,1)S(1)} collective-permute-done((bf16[256,256]{1,0:T(8,128)(2,1)}, bf16[256,256]{1,0:T(8,128)(2,1)S(1)}, u32[]{:S(2)}, u32[]{:S(2)}) %collective-permute-start.10) | collective-permute-done | bytes 131104 | tf_op jit(solution)/shard_map/ppermute | solution.py:337
  19.0 0.3 collective-permute-done.11
  19.3 1.7 %collective-permute-start.12 = (bf16[256,256]{1,0:T(8,128)(2,1)S(1)}, bf16[256,256]{1,0:T(8,128)(2,1)S(1)}, u32[]{:S(2)}, u32[]{:S(2)}) collective-permute-start(bf16[256,256]{1,0:T(8,128)(2,1)S(1)} %select_select_fusion), channel_id=1, source_target_pairs={{0,64},{16,80},{32,96},{48,112},{64,0},{80,16},{96,32},{112,48},{1... | collective-permute-start | bytes 393224 | tf_op jit(solution)/shard_map/ppermute | solution.py:338
  21.0 0.0 collective-permute-start.7
  21.0 5.4 %collective-permute-start.8 = (bf16[4,1,256,256]{3,2,1,0:T(8,128)(2,1)}, bf16[4,1,256,256]{3,2,1,0:T(8,128)(2,1)S(1)}, u32[]{:S(2)}, u32[]{:S(2)}) collective-permute-start(bf16[4,1,256,256]{3,2,1,0:T(8,128)(2,1)} %get-tuple-element.32), channel_id=1, source_target_pairs={{0,15},{1,0},{2,1},{3,2},{4,3},{5,4},{6,5},{7,6},{8,7},{9,8},{10,9... | collective-permute-start | bytes 1572872 | tf_op jit(solution)/shard_map/ppermute | solution.py:336
  26.4 2.5 %collective-permute-start.6 = (bf16[256,256]{1,0:T(8,128)(2,1)S(1)}, bf16[256,256]{1,0:T(8,128)(2,1)S(1)}, u32[]{:S(2)}, u32[]{:S(2)}) collective-permute-start(bf16[256,256]{1,0:T(8,128)(2,1)S(1)} %broadcast_select_fusion.1.refs_0_), channel_id=1, source_target_pairs={{0,48},{16,0},{32,16},{48,32},{64,112},{80,64},{96,80},{112,96},{1... | collective-permute-start | bytes 393224 | tf_op jit(solution)/shard_map/ppermute | solution.py:337
  28.8 1.7 %collective-permute-start.5 = (bf16[256,256]{1,0:T(8,128)(2,1)S(1)}, bf16[256,256]{1,0:T(8,128)(2,1)S(1)}, u32[]{:S(2)}, u32[]{:S(2)}) collective-permute-start(bf16[256,256]{1,0:T(8,128)(2,1)S(1)} %broadcast_select_fusion.1.refs_0_), channel_id=1, source_target_pairs={{0,32},{16,48},{32,0},{48,16},{64,96},{80,112},{96,64},{112,80},{1... | collective-permute-start | bytes 393224 | tf_op jit(solution)/shard_map/ppermute | solution.py:337
  30.6 0.0 collective-permute-done.12
  30.6 1.5 %collective-permute-done.6.refs_3_ = bf16[256,256]{1,0:T(8,128)(2,1)S(1)} collective-permute-done((bf16[256,256]{1,0:T(8,128)(2,1)S(1)}, bf16[256,256]{1,0:T(8,128)(2,1)S(1)}, u32[]{:S(2)}, u32[]{:S(2)}) %collective-permute-start.6) | collective-permute-done | bytes 131104 | tf_op jit(solution)/shard_map/ppermute | solution.py:337
  32.1 3.8 %collective-permute-start.15 = (bf16[256,256]{1,0:T(8,128)(2,1)S(1)}, bf16[256,256]{1,0:T(8,128)(2,1)S(1)}, u32[]{:S(2)}, u32[]{:S(2)}) collective-permute-start(bf16[256,256]{1,0:T(8,128)(2,1)S(1)} %broadcast_select_fusion.refs_4_), channel_id=1, source_target_pairs={{0,48},{16,0},{32,16},{48,32},{64,112},{80,64},{96,80},{112,96},{1... | collective-permute-start | bytes 393224 | tf_op jit(solution)/shard_map/ppermute | solution.py:337
  35.9 1.7 %collective-permute-start.14 = (bf16[256,256]{1,0:T(8,128)(2,1)S(1)}, bf16[256,256]{1,0:T(8,128)(2,1)S(1)}, u32[]{:S(2)}, u32[]{:S(2)}) collective-permute-start(bf16[256,256]{1,0:T(8,128)(2,1)S(1)} %broadcast_select_fusion.refs_4_), channel_id=1, source_target_pairs={{0,32},{16,48},{32,0},{48,16},{64,96},{80,112},{96,64},{112,80},{1... | collective-permute-start | bytes 393224 | tf_op jit(solution)/shard_map/ppermute | solution.py:337
  37.6 0.2 collective-permute-start.13
  37.8 0.0 collective-permute-done.7.near_low
  37.8 0.0 collective-permute-done.8.near_high
  37.8 0.3 collective-permute-start.16
  38.1 5.2 %collective-permute-start.17 = (bf16[4,1,256,256]{3,2,1,0:T(8,128)(2,1)}, bf16[4,1,256,256]{3,2,1,0:T(8,128)(2,1)}, u32[]{:S(2)}, u32[]{:S(2)}) collective-permute-start(bf16[4,1,256,256]{3,2,1,0:T(8,128)(2,1)} %get-tuple-element.45), channel_id=1, source_target_pairs={{0,15},{1,0},{2,1},{3,2},{4,3},{5,4},{6,5},{7,6},{8,7},{9,8},{10,9... | collective-permute-start | bytes 1572872 | tf_op jit(solution)/shard_map/ppermute | solution.py:336
  43.3 0.0 collective-permute-done.15.refs_7_
  43.3 0.0 collective-permute-done.14.refs_6_
  43.3 0.6 copy-done.11
  43.9 0.7 copy-done.12
  44.6 0.0 collective-permute-done.13.refs_5_
  44.6 2.7 %join_panel.1 = (bf16[2,4,256,256]{3,2,1,0:T(8,128)(2,1)}, bf16[2,2,256,256]{3,2,1,0:T(8,128)(2,1)}, bf16[2,2,256,256]{3,2,1,0:T(8,128)(2,1)}) custom-call(bf16[256,256]{1,0:T(8,128)(2,1)} %copy-done.4, bf16[256,256]{1,0:T(8,128)(2,1)} %copy-done.10, bf16[256,256]{1,0:T(8,128)(2,1)} %copy-done.9, bf16[256,256]{1,0:T(8,128)(2,1)} %copy-done.8, ...), custom_call_target="tpu_custom_call" | custom-call | tf_op jit(solution)/shard_map/join_panel/pallas_call | solution.py:296
  47.3 0.1 collective-permute-start.18
  47.4 5.3 %collective-permute-start.19 = (bf16[2,2,256,256]{3,2,1,0:T(8,128)(2,1)}, bf16[2,2,256,256]{3,2,1,0:T(8,128)(2,1)S(1)}, u32[]{:S(2)}, u32[]{:S(2)}) collective-permute-start(bf16[2,2,256,256]{3,2,1,0:T(8,128)(2,1)} %get-tuple-element.47), channel_id=1, source_target_pairs={{0,15},{1,0},{2,1},{3,2},{4,3},{5,4},{6,5},{7,6},{8,7},{9,8},{10,9... | collective-permute-start | bytes 1572872 | tf_op jit(solution)/shard_map/ppermute | solution.py:336
  52.8 1.2 %copy-done.1 = bf16[2,4,256,256]{3,2,1,0:T(8,128)(2,1)S(1)} copy-done((bf16[2,4,256,256]{3,2,1,0:T(8,128)(2,1)S(1)}, bf16[2,4,256,256]{3,2,1,0:T(8,128)(2,1)}, u32[]{:S(2)}) %copy-start.1) | copy-done | bytes 1048600
  54.0 13.9 %inner_field.1.e_in = f32[4,4,256,256]{3,2,1,0:T(8,128)} custom-call(bf16[4,4,256,256]{3,2,1,0:T(8,128)(2,1)S(1)} %copy-done, bf16[2,4,256,256]{3,2,1,0:T(8,128)(2,1)S(1)} %copy-done.1, bf16[768,256]{1,0:T(8,128)(2,1)S(1)} %copy-done.3), custom_call_target="tpu_custom_call" | custom-call | flops 6000000000 | bytes 8388608 | tf_op jit(solution)/shard_map/inner_field/pallas_call | solution.py:119
  67.9 0.0 collective-permute-done.18.plo
  67.9 9.0 %outer_field.1 = (f32[4,4,256,256]{3,2,1,0:T(8,128)}, f32[4,8,128]{2,1,0:T(8,128)S(1)}) custom-call(f32[4,4,256,256]{3,2,1,0:T(8,128)} %inner_field.1.e_in, bf16[4,4,256,256]{3,2,1,0:T(8,128)(2,1)S(1)} %copy-done, bf16[4,1,256,256]{3,2,1,0:T(8,128)(2,1)S(1)} %collective-permute-done.7.near_low, ...), custom_call_target="tpu_custom_call", output_to_operand_aliasing={{0}: (0, {})} | custom-call | flops 3000000000 | bytes 14680064 | tf_op jit(solution)/shard_map/outer_field/pallas_call | solution.py:212
  76.9 1.2 %collective-permute-done.20 = f32[4,8,128]{2,1,0:T(8,128)S(1)} collective-permute-done((f32[4,8,128]{2,1,0:T(8,128)S(1)}, f32[4,8,128]{2,1,0:T(8,128)S(1)}, u32[]{:S(2)}, u32[]{:S(2)}) %collective-permute-start.20) | collective-permute-done | bytes 16416 | tf_op jit(solution)/shard_map/ppermute | solution.py:322
  78.1 5.2 %collective-permute-done.21 = f32[4,8,128]{2,1,0:T(8,128)S(1)} collective-permute-done((f32[4,8,128]{2,1,0:T(8,128)S(1)}, f32[4,8,128]{2,1,0:T(8,128)S(1)}, u32[]{:S(2)}, u32[]{:S(2)}) %collective-permute-start.21) | collective-permute-done | bytes 16416 | tf_op jit(solution)/shard_map/ppermute | solution.py:322
  83.3 1.9 %collective-permute-start.24 = (f32[4,8,128]{2,1,0:T(8,128)S(1)}, f32[4,8,128]{2,1,0:T(8,128)S(1)}, u32[]{:S(2)}, u32[]{:S(2)}) collective-permute-start(f32[4,8,128]{2,1,0:T(8,128)S(1)} %add.20), channel_id=1, source_target_pairs={{0,12},{1,13},{2,14},{3,15},{4,8},{5,9},{6,10},{7,11},{8,4},{9,5},... | collective-permute-start | bytes 49160 | tf_op jit(solution)/shard_map/ppermute | solution.py:322
  85.2 2.2 %collective-permute-start.22 = (f32[4,8,128]{2,1,0:T(8,128)S(1)}, f32[4,8,128]{2,1,0:T(8,128)S(1)}, u32[]{:S(2)}, u32[]{:S(2)}) collective-permute-start(f32[4,8,128]{2,1,0:T(8,128)S(1)} %add.20), channel_id=1, source_target_pairs={{0,4},{1,5},{2,6},{3,7},{4,0},{5,1},{6,2},{7,3},{8,12},{9,13},{10,... | collective-permute-start | bytes 49160 | tf_op jit(solution)/shard_map/ppermute | solution.py:322
  87.4 1.0 %collective-permute-done.24 = f32[4,8,128]{2,1,0:T(8,128)S(1)} collective-permute-done((f32[4,8,128]{2,1,0:T(8,128)S(1)}, f32[4,8,128]{2,1,0:T(8,128)S(1)}, u32[]{:S(2)}, u32[]{:S(2)}) %collective-permute-start.24) | collective-permute-done | bytes 16416 | tf_op jit(solution)/shard_map/ppermute | solution.py:322
  88.4 2.1 %collective-permute-done.23 = f32[4,8,128]{2,1,0:T(8,128)S(1)} collective-permute-done((f32[4,8,128]{2,1,0:T(8,128)S(1)}, f32[4,8,128]{2,1,0:T(8,128)S(1)}, u32[]{:S(2)}, u32[]{:S(2)}) %collective-permute-start.23) | collective-permute-done | bytes 16416 | tf_op jit(solution)/shard_map/ppermute | solution.py:322
  90.5 0.7 fusion.1
  (42 shorter events, 0.2 us)
Async XLA Ops:
  2.7 10.9 %copy-start.13 = (bf16[256,256]{1,0:T(8,128)(2,1)S(1)}, bf16[256,256]{1,0:T(8,128)(2,1)}, u32[]{:S(2)}) copy-start(bf16[256,256]{1,0:T(8,128)(2,1)} %get-tuple-element.40) | copy-start | bytes 393220
  2.7 12.8 %copy-start.7 = (bf16[256,256]{1,0:T(8,128)(2,1)S(1)}, bf16[256,256]{1,0:T(8,128)(2,1)}, u32[]{:S(2)}) copy-start(bf16[256,256]{1,0:T(8,128)(2,1)} %get-tuple-element.26) | copy-start | bytes 393220
  2.8 16.5 %copy-start.6 = (bf16[256,256]{1,0:T(8,128)(2,1)S(1)}, bf16[256,256]{1,0:T(8,128)(2,1)}, u32[]{:S(2)}) copy-start(bf16[256,256]{1,0:T(8,128)(2,1)} %get-tuple-element.37) | copy-start | bytes 393220
  2.8 50.0 %copy-start = (bf16[4,4,256,256]{3,2,1,0:T(8,128)(2,1)S(1)}, bf16[4,4,256,256]{3,2,1,0:T(8,128)(2,1)}, u32[]{:S(2)}) copy-start(bf16[4,4,256,256]{3,2,1,0:T(8,128)(2,1)} %o.3) | copy-start | bytes 6291460
  2.8 50.0 %copy-start.3 = (bf16[768,256]{1,0:T(8,128)(2,1)S(1)}, bf16[768,256]{1,0:T(8,128)(2,1)}, u32[]{:S(2)}) copy-start(bf16[768,256]{1,0:T(8,128)(2,1)} %constant.30.mix) | copy-start | bytes 1179652
  2.8 10.8 %collective-permute-start = (bf16[256,256]{1,0:T(8,128)(2,1)}, bf16[256,256]{1,0:T(8,128)(2,1)S(1)}, u32[]{:S(2)}, u32[]{:S(2)}) collective-permute-start(bf16[256,256]{1,0:T(8,128)(2,1)} %get-tuple-element.27), channel_id=1, source_target_pairs={{0,16},{16,32},{32,48},{48,0},{64,80},{80,96},{96,112},{112,64},{1... | collective-permute-start | bytes 393224 | tf_op jit(solution)/shard_map/ppermute | solution.py:337
  4.4 11.1 %collective-permute-start.1 = (bf16[256,256]{1,0:T(8,128)(2,1)}, bf16[256,256]{1,0:T(8,128)(2,1)S(1)}, u32[]{:S(2)}, u32[]{:S(2)}) collective-permute-start(bf16[256,256]{1,0:T(8,128)(2,1)} %get-tuple-element.28), channel_id=1, source_target_pairs={{0,32},{16,48},{32,0},{48,16},{64,96},{80,112},{96,64},{112,80},{1... | collective-permute-start | bytes 393224 | tf_op jit(solution)/shard_map/ppermute | solution.py:337
  7.2 8.3 %collective-permute-start.2 = (bf16[256,256]{1,0:T(8,128)(2,1)}, bf16[256,256]{1,0:T(8,128)(2,1)S(1)}, u32[]{:S(2)}, u32[]{:S(2)}) collective-permute-start(bf16[256,256]{1,0:T(8,128)(2,1)} %get-tuple-element.29), channel_id=1, source_target_pairs={{0,48},{16,0},{32,16},{48,32},{64,112},{80,64},{96,80},{112,96},{1... | collective-permute-start | bytes 393224 | tf_op jit(solution)/shard_map/ppermute | solution.py:337
  8.6 8.6 %collective-permute-start.9 = (bf16[256,256]{1,0:T(8,128)(2,1)}, bf16[256,256]{1,0:T(8,128)(2,1)S(1)}, u32[]{:S(2)}, u32[]{:S(2)}) collective-permute-start(bf16[256,256]{1,0:T(8,128)(2,1)} %get-tuple-element.38), channel_id=1, source_target_pairs={{0,16},{16,32},{32,48},{48,0},{64,80},{80,96},{96,112},{112,64},{1... | collective-permute-start | bytes 393224 | tf_op jit(solution)/shard_map/ppermute | solution.py:337
  9.2 9.8 %collective-permute-start.10 = (bf16[256,256]{1,0:T(8,128)(2,1)}, bf16[256,256]{1,0:T(8,128)(2,1)S(1)}, u32[]{:S(2)}, u32[]{:S(2)}) collective-permute-start(bf16[256,256]{1,0:T(8,128)(2,1)} %get-tuple-element.39), channel_id=1, source_target_pairs={{0,32},{16,48},{32,0},{48,16},{64,96},{80,112},{96,64},{112,80},{1... | collective-permute-start | bytes 393224 | tf_op jit(solution)/shard_map/ppermute | solution.py:337
  13.6 5.6 %collective-permute-start.11 = (bf16[256,256]{1,0:T(8,128)(2,1)S(1)}, bf16[256,256]{1,0:T(8,128)(2,1)S(1)}, u32[]{:S(2)}, u32[]{:S(2)}) collective-permute-start(bf16[256,256]{1,0:T(8,128)(2,1)S(1)} %copy-done.13), channel_id=1, source_target_pairs={{0,48},{16,0},{32,16},{48,32},{64,112},{80,64},{96,80},{112,96},{1... | collective-permute-start | bytes 393224 | tf_op jit(solution)/shard_map/ppermute | solution.py:337
  15.5 10.8 %collective-permute-start.3 = (bf16[256,256]{1,0:T(8,128)(2,1)S(1)}, bf16[256,256]{1,0:T(8,128)(2,1)S(1)}, u32[]{:S(2)}, u32[]{:S(2)}) collective-permute-start(bf16[256,256]{1,0:T(8,128)(2,1)S(1)} %select_select_fusion.1), channel_id=1, source_target_pairs={{0,64},{16,80},{32,96},{48,112},{64,0},{80,16},{96,32},{112,48},{1... | collective-permute-start | bytes 393224 | tf_op jit(solution)/shard_map/ppermute | solution.py:338
  19.3 11.2 %collective-permute-start.12 = (bf16[256,256]{1,0:T(8,128)(2,1)S(1)}, bf16[256,256]{1,0:T(8,128)(2,1)S(1)}, u32[]{:S(2)}, u32[]{:S(2)}) collective-permute-start(bf16[256,256]{1,0:T(8,128)(2,1)S(1)} %select_select_fusion), channel_id=1, source_target_pairs={{0,64},{16,80},{32,96},{48,112},{64,0},{80,16},{96,32},{112,48},{1... | collective-permute-start | bytes 393224 | tf_op jit(solution)/shard_map/ppermute | solution.py:338
  21.0 16.8 %collective-permute-start.7 = (bf16[4,1,256,256]{3,2,1,0:T(8,128)(2,1)}, bf16[4,1,256,256]{3,2,1,0:T(8,128)(2,1)S(1)}, u32[]{:S(2)}, u32[]{:S(2)}) collective-permute-start(bf16[4,1,256,256]{3,2,1,0:T(8,128)(2,1)} %get-tuple-element.31), channel_id=1, source_target_pairs={{0,1},{1,2},{2,3},{3,4},{4,5},{5,6},{6,7},{7,8},{8,9},{9,10},{10,1... | collective-permute-start | bytes 1572872 | tf_op jit(solution)/shard_map/ppermute | solution.py:335
  21.0 16.8 %collective-permute-start.8 = (bf16[4,1,256,256]{3,2,1,0:T(8,128)(2,1)}, bf16[4,1,256,256]{3,2,1,0:T(8,128)(2,1)S(1)}, u32[]{:S(2)}, u32[]{:S(2)}) collective-permute-start(bf16[4,1,256,256]{3,2,1,0:T(8,128)(2,1)} %get-tuple-element.32), channel_id=1, source_target_pairs={{0,15},{1,0},{2,1},{3,2},{4,3},{5,4},{6,5},{7,6},{8,7},{9,8},{10,9... | collective-permute-start | bytes 1572872 | tf_op jit(solution)/shard_map/ppermute | solution.py:336
  26.4 11.5 %copy-start.4 = (bf16[256,256]{1,0:T(8,128)(2,1)}, bf16[256,256]{1,0:T(8,128)(2,1)S(1)}, u32[]{:S(2)}) copy-start(bf16[256,256]{1,0:T(8,128)(2,1)S(1)} %broadcast_select_fusion.1.refs_0_) | copy-start | bytes 393220
  26.4 5.7 %collective-permute-start.6 = (bf16[256,256]{1,0:T(8,128)(2,1)S(1)}, bf16[256,256]{1,0:T(8,128)(2,1)S(1)}, u32[]{:S(2)}, u32[]{:S(2)}) collective-permute-start(bf16[256,256]{1,0:T(8,128)(2,1)S(1)} %broadcast_select_fusion.1.refs_0_), channel_id=1, source_target_pairs={{0,48},{16,0},{32,16},{48,32},{64,112},{80,64},{96,80},{112,96},{1... | collective-permute-start | bytes 393224 | tf_op jit(solution)/shard_map/ppermute | solution.py:337
  28.8 7.1 %collective-permute-start.5 = (bf16[256,256]{1,0:T(8,128)(2,1)S(1)}, bf16[256,256]{1,0:T(8,128)(2,1)S(1)}, u32[]{:S(2)}, u32[]{:S(2)}) collective-permute-start(bf16[256,256]{1,0:T(8,128)(2,1)S(1)} %broadcast_select_fusion.1.refs_0_), channel_id=1, source_target_pairs={{0,32},{16,48},{32,0},{48,16},{64,96},{80,112},{96,64},{112,80},{1... | collective-permute-start | bytes 393224 | tf_op jit(solution)/shard_map/ppermute | solution.py:337
  30.6 7.0 %collective-permute-start.4 = (bf16[256,256]{1,0:T(8,128)(2,1)S(1)}, bf16[256,256]{1,0:T(8,128)(2,1)S(1)}, u32[]{:S(2)}, u32[]{:S(2)}) collective-permute-start(bf16[256,256]{1,0:T(8,128)(2,1)S(1)} %broadcast_select_fusion.1.refs_0_), channel_id=1, source_target_pairs={{0,16},{16,32},{32,48},{48,0},{64,80},{80,96},{96,112},{112,64},{1... | collective-permute-start | bytes 393224 | tf_op jit(solution)/shard_map/ppermute | solution.py:337
  30.6 7.2 %copy-start.5 = (bf16[256,256]{1,0:T(8,128)(2,1)}, bf16[256,256]{1,0:T(8,128)(2,1)S(1)}, u32[]{:S(2)}) copy-start(bf16[256,256]{1,0:T(8,128)(2,1)S(1)} %broadcast_select_fusion.refs_4_) | copy-start | bytes 393220
  32.1 11.2 %copy-start.8 = (bf16[256,256]{1,0:T(8,128)(2,1)}, bf16[256,256]{1,0:T(8,128)(2,1)S(1)}, u32[]{:S(2)}) copy-start(bf16[256,256]{1,0:T(8,128)(2,1)S(1)} %collective-permute-done.6.refs_3_) | copy-start | bytes 393220
  32.1 11.2 %collective-permute-start.15 = (bf16[256,256]{1,0:T(8,128)(2,1)S(1)}, bf16[256,256]{1,0:T(8,128)(2,1)S(1)}, u32[]{:S(2)}, u32[]{:S(2)}) collective-permute-start(bf16[256,256]{1,0:T(8,128)(2,1)S(1)} %broadcast_select_fusion.refs_4_), channel_id=1, source_target_pairs={{0,48},{16,0},{32,16},{48,32},{64,112},{80,64},{96,80},{112,96},{1... | collective-permute-start | bytes 393224 | tf_op jit(solution)/shard_map/ppermute | solution.py:337
  35.9 7.4 %copy-start.9 = (bf16[256,256]{1,0:T(8,128)(2,1)}, bf16[256,256]{1,0:T(8,128)(2,1)S(1)}, u32[]{:S(2)}) copy-start(bf16[256,256]{1,0:T(8,128)(2,1)S(1)} %collective-permute-done.5.refs_2_) | copy-start | bytes 393220
  35.9 7.4 %collective-permute-start.14 = (bf16[256,256]{1,0:T(8,128)(2,1)S(1)}, bf16[256,256]{1,0:T(8,128)(2,1)S(1)}, u32[]{:S(2)}, u32[]{:S(2)}) collective-permute-start(bf16[256,256]{1,0:T(8,128)(2,1)S(1)} %broadcast_select_fusion.refs_4_), channel_id=1, source_target_pairs={{0,32},{16,48},{32,0},{48,16},{64,96},{80,112},{96,64},{112,80},{1... | collective-permute-start | bytes 393224 | tf_op jit(solution)/shard_map/ppermute | solution.py:337
  37.6 5.7 %copy-start.10 = (bf16[256,256]{1,0:T(8,128)(2,1)}, bf16[256,256]{1,0:T(8,128)(2,1)S(1)}, u32[]{:S(2)}) copy-start(bf16[256,256]{1,0:T(8,128)(2,1)S(1)} %collective-permute-done.4.refs_1_) | copy-start | bytes 393220
  37.6 7.0 %collective-permute-start.13 = (bf16[256,256]{1,0:T(8,128)(2,1)S(1)}, bf16[256,256]{1,0:T(8,128)(2,1)}, u32[]{:S(2)}, u32[]{:S(2)}) collective-permute-start(bf16[256,256]{1,0:T(8,128)(2,1)S(1)} %broadcast_select_fusion.refs_4_), channel_id=1, source_target_pairs={{0,16},{16,32},{32,48},{48,0},{64,80},{80,96},{96,112},{112,64},{1... | collective-permute-start | bytes 393224 | tf_op jit(solution)/shard_map/ppermute | solution.py:337
  37.8 30.1 %collective-permute-start.16 = (bf16[4,1,256,256]{3,2,1,0:T(8,128)(2,1)}, bf16[4,1,256,256]{3,2,1,0:T(8,128)(2,1)}, u32[]{:S(2)}, u32[]{:S(2)}) collective-permute-start(bf16[4,1,256,256]{3,2,1,0:T(8,128)(2,1)} %get-tuple-element.43), channel_id=1, source_target_pairs={{0,1},{1,2},{2,3},{3,4},{4,5},{5,6},{6,7},{7,8},{8,9},{9,10},{10,1... | collective-permute-start | bytes 1572872 | tf_op jit(solution)/shard_map/ppermute | solution.py:335
  38.1 29.8 %collective-permute-start.17 = (bf16[4,1,256,256]{3,2,1,0:T(8,128)(2,1)}, bf16[4,1,256,256]{3,2,1,0:T(8,128)(2,1)}, u32[]{:S(2)}, u32[]{:S(2)}) collective-permute-start(bf16[4,1,256,256]{3,2,1,0:T(8,128)(2,1)} %get-tuple-element.45), channel_id=1, source_target_pairs={{0,15},{1,0},{2,1},{3,2},{4,3},{5,4},{6,5},{7,6},{8,7},{9,8},{10,9... | collective-permute-start | bytes 1572872 | tf_op jit(solution)/shard_map/ppermute | solution.py:336
  43.3 0.7 copy-start.11
  43.9 0.7 copy-start.12
  47.3 20.6 %collective-permute-start.18 = (bf16[2,2,256,256]{3,2,1,0:T(8,128)(2,1)}, bf16[2,2,256,256]{3,2,1,0:T(8,128)(2,1)S(1)}, u32[]{:S(2)}, u32[]{:S(2)}) collective-permute-start(bf16[2,2,256,256]{3,2,1,0:T(8,128)(2,1)} %get-tuple-element.46), channel_id=1, source_target_pairs={{0,1},{1,2},{2,3},{3,4},{4,5},{5,6},{6,7},{7,8},{8,9},{9,10},{10,1... | collective-permute-start | bytes 1572872 | tf_op jit(solution)/shard_map/ppermute | solution.py:335
  47.4 20.5 %collective-permute-start.19 = (bf16[2,2,256,256]{3,2,1,0:T(8,128)(2,1)}, bf16[2,2,256,256]{3,2,1,0:T(8,128)(2,1)S(1)}, u32[]{:S(2)}, u32[]{:S(2)}) collective-permute-start(bf16[2,2,256,256]{3,2,1,0:T(8,128)(2,1)} %get-tuple-element.47), channel_id=1, source_target_pairs={{0,15},{1,0},{2,1},{3,2},{4,3},{5,4},{6,5},{7,6},{8,7},{9,8},{10,9... | collective-permute-start | bytes 1572872 | tf_op jit(solution)/shard_map/ppermute | solution.py:336
  52.8 1.2 %copy-start.1 = (bf16[2,4,256,256]{3,2,1,0:T(8,128)(2,1)S(1)}, bf16[2,4,256,256]{3,2,1,0:T(8,128)(2,1)}, u32[]{:S(2)}) copy-start(bf16[2,4,256,256]{3,2,1,0:T(8,128)(2,1)} %get-tuple-element.41.p) | copy-start | bytes 3145732
  54.0 13.9 %copy-start.2 = (bf16[2,4,256,256]{3,2,1,0:T(8,128)(2,1)S(1)}, bf16[2,4,256,256]{3,2,1,0:T(8,128)(2,1)}, u32[]{:S(2)}) copy-start(bf16[2,4,256,256]{3,2,1,0:T(8,128)(2,1)} %get-tuple-element.41.p) | copy-start | bytes 3145732
  76.9 1.2 %collective-permute-start.20 = (f32[4,8,128]{2,1,0:T(8,128)S(1)}, f32[4,8,128]{2,1,0:T(8,128)S(1)}, u32[]{:S(2)}, u32[]{:S(2)}) collective-permute-start(f32[4,8,128]{2,1,0:T(8,128)S(1)} %get-tuple-element.49), channel_id=1, source_target_pairs={{0,1},{1,0},{2,3},{3,2},{4,5},{5,4},{6,7},{7,6},{8,9},{9,8},{10,11... | collective-permute-start | bytes 49160 | tf_op jit(solution)/shard_map/ppermute | solution.py:322
  78.1 5.2 %collective-permute-start.21 = (f32[4,8,128]{2,1,0:T(8,128)S(1)}, f32[4,8,128]{2,1,0:T(8,128)S(1)}, u32[]{:S(2)}, u32[]{:S(2)}) collective-permute-start(f32[4,8,128]{2,1,0:T(8,128)S(1)} %add.19), channel_id=1, source_target_pairs={{0,2},{1,3},{2,0},{3,1},{4,6},{5,7},{6,4},{7,5},{8,10},{9,11},{10,... | collective-permute-start | bytes 49160 | tf_op jit(solution)/shard_map/ppermute | solution.py:322
  83.3 5.1 %collective-permute-start.24 = (f32[4,8,128]{2,1,0:T(8,128)S(1)}, f32[4,8,128]{2,1,0:T(8,128)S(1)}, u32[]{:S(2)}, u32[]{:S(2)}) collective-permute-start(f32[4,8,128]{2,1,0:T(8,128)S(1)} %add.20), channel_id=1, source_target_pairs={{0,12},{1,13},{2,14},{3,15},{4,8},{5,9},{6,10},{7,11},{8,4},{9,5},... | collective-permute-start | bytes 49160 | tf_op jit(solution)/shard_map/ppermute | solution.py:322
  85.2 5.2 %collective-permute-start.23 = (f32[4,8,128]{2,1,0:T(8,128)S(1)}, f32[4,8,128]{2,1,0:T(8,128)S(1)}, u32[]{:S(2)}, u32[]{:S(2)}) collective-permute-start(f32[4,8,128]{2,1,0:T(8,128)S(1)} %add.20), channel_id=1, source_target_pairs={{0,8},{1,9},{2,10},{3,11},{4,12},{5,13},{6,14},{7,15},{8,0},{9,1},... | collective-permute-start | bytes 49160 | tf_op jit(solution)/shard_map/ppermute | solution.py:322
  85.2 5.2 %collective-permute-start.22 = (f32[4,8,128]{2,1,0:T(8,128)S(1)}, f32[4,8,128]{2,1,0:T(8,128)S(1)}, u32[]{:S(2)}, u32[]{:S(2)}) collective-permute-start(f32[4,8,128]{2,1,0:T(8,128)S(1)} %add.20), channel_id=1, source_target_pairs={{0,4},{1,5},{2,6},{3,7},{4,0},{5,1},{6,2},{7,3},{8,12},{9,13},{10,... | collective-permute-start | bytes 49160 | tf_op jit(solution)/shard_map/ppermute | solution.py:322

commit v3 on v2

v3 whole, which is shorter than its diff:
```python
import math

import jax
import jax.numpy as jnp
import numpy as np
from jax import lax
from jax.experimental import pallas as pl
from jax.experimental.pallas import tpu as pltpu
from jax.sharding import PartitionSpec as P

PANEL, SWEEPS, SCREEN = 2, 3, 0.1
PAD = 8
STRIP = 32


def polynomial():
    d = 6.0 + SCREEN
    w = [1.0 / (1.0 + 6.0 / d * math.cos(math.pi * (2 * k + 1) / (2 * SWEEPS))) for k in range(SWEEPS)]
    p = [w[0] / d]
    for k in range(1, SWEEPS):
        n = [0.0] * (len(p) + 1)
        for i, c in enumerate(p):
            n[i] += c * (1.0 - w[k])
            n[i + 1] += c * w[k] / d
        n[0] += w[k] / d
        p = n
    return p


def mixing(nz, beta):
    near = np.zeros((nz, nz), np.float32)
    far = np.zeros((nz, nz), np.float32)
    for z in range(nz):
        for s, m in ((1, near), (2, far)):
            m[(z - s) % nz, z] += 1.0
            m[(z + s) % nz, z] += 1.0
    return jnp.asarray(np.concatenate([near, near, beta * far], 0)).astype(jnp.bfloat16)


LANES = 128


def at(ref, idx, start, size, h):
    return ref[(*idx, slice(start, start + size), slice(h * LANES, (h + 1) * LANES))]


def sp(ref, idx, start, size, h):
    return ref[(*idx, h, slice(start, start + size), slice(None))]


def wrap(ref, idx, halves, ny, width):
    for h in range(halves):
        ref[(*idx, h, slice(PAD - width, PAD), slice(None))] = sp(ref, idx, PAD + ny - width, width, h)
        ref[(*idx, h, slice(PAD + ny, PAD + ny + width), slice(None))] = sp(ref, idx, PAD, width, h)


def split(left, rows, nz, h, v):
    hi = v.astype(jnp.bfloat16)
    left[rows, h * LANES:(h + 1) * LANES] = hi
    left[rows, nz + h * LANES:nz + (h + 1) * LANES] = (v - hi.astype(jnp.float32)).astype(jnp.bfloat16)


def inner_kernel(o, p, mix, e, rho, *scratch):
    g0, g1, g2 = polynomial()
    beta = g2 / g1
    kappa = g0 / g1 + 6.0 * beta
    na, nx, ny, nz = p.shape
    steps, halves = ny // STRIP, nz // LANES
    f32, bf = jnp.float32, jnp.bfloat16
    sigs, lefts, bases = scratch[0:2], scratch[2:4], scratch[4:6]

    for x in range(nx):
        for i in range(steps):
            for h in range(halves):
                ov = at(o, (0, x), i * STRIP, STRIP, h).astype(f32)
                for a in range(na):
                    rho[a, x, h, PAD + i * STRIP:PAD + (i + 1) * STRIP, :] = at(p, (a, x), i * STRIP, STRIP, h).astype(f32) * ov
        for a in range(na):
            wrap(rho, (a, x), halves, ny, 2)

    def prepare(x):
        sig, left, base = sigs[x % 2], lefts[x % 2], bases[x % 2]
        near = [n for n in (x - 1, x + 1) if 0 <= n < nx]
        apart = [n for n in (x - 2, x + 2) if 0 <= n < nx]
        if len(near) > 1:
            for a in range(na):
                for h in range(halves):
                    for r in range(0, ny + 2 * PAD, 16):
                        sig[a, h, r:r + 16, :] = sp(rho, (a, near[0]), r, 16, h) + sp(rho, (a, near[1]), r, 16, h)
        for a in range(na):
            s_ref, s_idx = (sig, (a,)) if len(near) > 1 else (rho, (a, near[0]))
            for i in range(steps):
                for h in range(halves):
                    r = PAD + i * STRIP
                    rows = slice(i * STRIP, (i + 1) * STRIP)
                    c = sp(rho, (a, x), r, STRIP, h)
                    q = sp(s_ref, s_idx, r, STRIP, h) + (sp(rho, (a, x), r - 1, STRIP, h) + sp(rho, (a, x), r + 1, STRIP, h))
                    far = sp(rho, (a, x), r - 2, STRIP, h) + sp(rho, (a, x), r + 2, STRIP, h)
                    for n in apart:
                        far = far + sp(rho, (a, n), r, STRIP, h)
                    side = sp(s_ref, s_idx, r - 1, STRIP, h) + sp(s_ref, s_idx, r + 1, STRIP, h)
                    split(left.at[a], rows, nz, h, c + (2.0 * beta) * q)
                    left[a, rows, 2 * nz + h * LANES:2 * nz + (h + 1) * LANES] = c.astype(bf)
                    base[a, rows, h * LANES:(h + 1) * LANES] = (kappa * c + q) + beta * (far + (side + side))

    def finish(x):
        left, base = lefts[x % 2], bases[x % 2]
        mixed = [jnp.dot(left[a], mix[...], preferred_element_type=f32) for a in range(na)]
        for i in range(steps):
            rows = slice(i * STRIP, (i + 1) * STRIP)
            total = None
            for a in range(na):
                w = p[a, x, rows, :].astype(f32) * (base[a, rows, :] + mixed[a][rows])
                total = w if total is None else total + w
            e[pl.program_id(0), x, rows, :] = total * (-g1)

    prepare(0)
    for x in range(1, nx):
        prepare(x)
        finish(x - 1)
    finish(nx - 1)


def inner(o, p):
    nj, nx, ny, nz = o.shape
    na = p.shape[0]
    g = polynomial()
    f32, bf = jnp.float32, jnp.bfloat16
    mix = mixing(nz, g[2] / g[1])
    return pl.pallas_call(
        inner_kernel,
        grid=(nj,),
        out_shape=pltpu.VMEM((nj, nx, ny, nz), f32),
        in_specs=[
            pl.BlockSpec((1, nx, ny, nz), lambda j: (j, 0, 0, 0)),
            pl.BlockSpec(memory_space=pltpu.VMEM),
            pl.BlockSpec(mix.shape, lambda j: (0, 0)),
        ],
        out_specs=pl.BlockSpec(memory_space=pltpu.VMEM),
        scratch_shapes=[pltpu.VMEM((na, nx, nz // LANES, ny + 2 * PAD, LANES), f32)]
        + [pltpu.VMEM((na, nz // LANES, ny + 2 * PAD, LANES), f32)] * 2
        + [pltpu.VMEM((na, ny, 3 * nz), bf)] * 2
        + [pltpu.VMEM((na, ny, nz), f32)] * 2,
        compiler_params=pltpu.CompilerParams(vmem_limit_bytes=20 * 2**20),
        cost_estimate=pl.CostEstimate(flops=6 * 10**9, bytes_accessed=8 * 2**20, transcendentals=0),
        name="inner_field",
    )(o, p, mix)


def outer_kernel(e_in, o, halo_low, halo_high, p, plo, phi, mix, e, ace, *scratch):
    g0, g1, g2 = polynomial()
    beta = g2 / g1
    na, nx, ny, nz = p.shape
    nj = o.shape[0]
    steps, halves = ny // STRIP, nz // LANES
    f32, bf = jnp.float32, jnp.bfloat16
    rhos, lefts, bases = scratch[0:2], scratch[2:4], scratch[4:6]
    sides = ((0, halo_low, plo, 1, 0, 0, 1), (1, halo_high, phi, 0, 1, nx - 1, nx - 2))

    def prepare(s, halo, ph, h1, h2, t0, t1):
        rho, left, base = rhos[s], lefts[s], bases[s]
        for i in range(steps):
            for h in range(halves):
                ov = at(halo, (0, h1), i * STRIP, STRIP, h).astype(f32)
                for a in range(na):
                    rho[a, h, PAD + i * STRIP:PAD + (i + 1) * STRIP, :] = at(ph, (a, h1), i * STRIP, STRIP, h).astype(f32) * ov
        for a in range(na):
            wrap(rho, (a,), halves, ny, 1)
        for i in range(steps):
            for h in range(halves):
                r = PAD + i * STRIP
                rows = slice(i * STRIP, (i + 1) * STRIP)
                lanes = slice(h * LANES, (h + 1) * LANES)
                ov = at(halo, (0, h2), i * STRIP, STRIP, h).astype(f32)
                step = None
                for a in range(na):
                    c = sp(rho, (a,), r, STRIP, h)
                    split(left.at[a], rows, nz, h, c)
                    y = sp(rho, (a,), r - 1, STRIP, h) + sp(rho, (a,), r + 1, STRIP, h)
                    base[a, rows, lanes] = (c + beta * (at(ph, (a, h2), i * STRIP, STRIP, h).astype(f32) * ov)) + (2.0 * beta) * y
                    w = at(p, (a, t1), i * STRIP, STRIP, h).astype(f32) * c
                    step = w if step is None else step + w
                e[0, t1, rows, lanes] = at(e_in, (pl.program_id(0), t1), i * STRIP, STRIP, h) + step * (-g1 * beta)

    def finish(s, halo, ph, h1, h2, t0, t1):
        left, base = lefts[s], bases[s]
        mixed = [jnp.dot(left[a], mix[:2 * nz, :], preferred_element_type=f32) for a in range(na)]
        for i in range(steps):
            rows = slice(i * STRIP, (i + 1) * STRIP)
            step = None
            for a in range(na):
                w = p[a, t0, rows, :].astype(f32) * (base[a, rows, :] + (2.0 * beta) * mixed[a][rows])
                step = w if step is None else step + w
            e[0, t0, rows, :] = e_in[pl.program_id(0), t0, rows, :] + step * (-g1)

    prepare(*sides[0])
    prepare(*sides[1])
    finish(*sides[0])
    finish(*sides[1])

    def project(x, acc):
        acc = list(acc)
        for i in range(steps):
            rows = slice(i * STRIP, (i + 1) * STRIP)
            field = e[0, x, rows, :]
            for s in range(na + nj):
                source = p[s, x, rows, :] if s < na else o[s - na, x, rows, :]
                m = source.astype(f32) * field
                m = m[:, :128] + m[:, 128:]
                acc[s] = acc[s] + jnp.sum(m.reshape(STRIP // 8, 8, 128), axis=0)
        return tuple(acc)

    acc = lax.fori_loop(0, nx, project, tuple(jnp.zeros((8, 128), f32) for _ in range(na + nj)))
    sums = [jnp.sum(a, axis=0, keepdims=True) for a in acc]
    tile = jnp.concatenate(sums + [jnp.zeros((8 - na - nj, LANES), f32)], axis=0)
    share = LANES // nj
    width = LANES // 2
    while width >= share:
        tile = tile + pltpu.roll(tile, width, 1)
        width //= 2
    j = pl.program_id(0)
    lane = lax.broadcasted_iota(jnp.int32, (8, LANES), 1)
    tile = jnp.where((lane >= j * share) & (lane < (j + 1) * share), tile, jnp.where(j == 0, 0.0, ace[...]))
    ace[...] = tile


def outer(e, o, halo, p, plo, phi):
    nj, nx, ny, nz = o.shape
    na = p.shape[0]
    g = polynomial()
    f32, bf = jnp.float32, jnp.bfloat16
    mix = mixing(nz, g[2] / g[1])
    each = lambda shape: pl.BlockSpec((1, *shape[1:]), lambda j: (j, *(0,) * (len(shape) - 1)))
    whole = lambda shape: pl.BlockSpec(shape, lambda j: (0,) * len(shape))
    return pl.pallas_call(
        outer_kernel,
        grid=(nj,),
        out_shape=(jax.ShapeDtypeStruct(e.shape, f32), jax.ShapeDtypeStruct((8, LANES), f32)),
        in_specs=[pl.BlockSpec(memory_space=pltpu.VMEM), whole(o.shape), *[each(h.shape) for h in halo], pl.BlockSpec(memory_space=pltpu.VMEM), whole(plo.shape), whole(phi.shape), whole(mix.shape)],
        out_specs=(each(e.shape), pl.BlockSpec((8, LANES), lambda j: (0, 0))),
        scratch_shapes=[pltpu.VMEM((na, nz // LANES, ny + 2 * PAD, LANES), f32)] * 2
        + [pltpu.VMEM((na, ny, 2 * nz), bf)] * 2
        + [pltpu.VMEM((na, ny, nz), f32)] * 2,
        compiler_params=pltpu.CompilerParams(vmem_limit_bytes=24 * 2**20),
        cost_estimate=pl.CostEstimate(flops=3 * 10**9, bytes_accessed=14 * 2**20, transcendentals=0),
        name="outer_field",
    )(e, o, *halo, p, plo, phi, mix)


def cut_kernel(row, orbitals, *refs):
    parts = refs[:PANEL * row]
    held, loaded, stored = refs[PANEL * row:]
    x = lax.rem(lax.axis_index("band"), row)
    loads = [pltpu.make_async_copy(orbitals.at[a], held.at[a], loaded.at[a]) for a in range(PANEL)]
    stores = [
        pltpu.make_async_copy(held.at[a, lax.rem(x + k, row)], parts[a * row + k], stored.at[a * row + k])
        for a in range(PANEL)
        for k in range(row)
    ]
    for a in range(PANEL):
        loads[a].start()
    for a in range(PANEL):
        loads[a].wait()
        for k in range(row):
            stores[a * row + k].start()
    for c in stores:
        c.wait()


def cut(orbitals):
    row, ny, nz = orbitals.shape[1:]
    part = jax.ShapeDtypeStruct((ny, nz), orbitals.dtype)
    hbm = pl.BlockSpec(memory_space=pltpu.HBM)
    parts = pl.pallas_call(
        lambda *refs: cut_kernel(row, *refs),
        out_shape=(part,) * (PANEL * row),
        in_specs=[hbm],
        out_specs=(hbm,) * (PANEL * row),
        scratch_shapes=[
            pltpu.VMEM((PANEL, row, ny, nz), orbitals.dtype),
            pltpu.SemaphoreType.DMA((PANEL,)),
            pltpu.SemaphoreType.DMA((PANEL * row,)),
        ],
        name="cut_panel",
    )(orbitals)
    return [parts[a * row:(a + 1) * row] for a in range(PANEL)]


def edges_kernel(orbitals, top, bottom, held, loaded, stored):
    nx = orbitals.shape[1]
    loads = [pltpu.make_async_copy(orbitals.at[:, a:a + 2], held.at[n], loaded.at[n]) for n, a in enumerate((nx - 2, 0))]
    stores = [pltpu.make_async_copy(held.at[n], out, stored.at[n]) for n, out in enumerate((top, bottom))]
    for c in loads:
        c.start()
    for load, store in zip(loads, stores):
        load.wait()
        store.start()
    for c in stores:
        c.wait()


def edges(orbitals):
    nj, _, ny, nz = orbitals.shape
    hbm = pl.BlockSpec(memory_space=pltpu.HBM)
    return pl.pallas_call(
        edges_kernel,
        out_shape=(jax.ShapeDtypeStruct((nj, 2, ny, nz), orbitals.dtype),) * 2,
        in_specs=[hbm],
        out_specs=(hbm, hbm),
        scratch_shapes=[pltpu.VMEM((2, nj, 2, ny, nz), orbitals.dtype), pltpu.SemaphoreType.DMA((2,)), pltpu.SemaphoreType.DMA((2,))],
        name="edge_planes",
    )(orbitals)


def join_kernel(row, *refs):
    parts, (panel, top, bottom, loaded, stored) = refs[:PANEL * row], refs[PANEL * row:]
    x = lax.rem(lax.axis_index("band"), row)
    loads = [
        pltpu.make_async_copy(parts[a * row + k], panel.at[a, lax.rem(x + row - k, row)], loaded.at[a * row + k])
        for a in range(PANEL)
        for k in range(row)
    ]
    stores = [
        pltpu.make_async_copy(panel.at[:, row - 2:], top, stored.at[0]),
        pltpu.make_async_copy(panel.at[:, :2], bottom, stored.at[1]),
    ]
    for c in loads:
        c.start()
    for c in loads:
        c.wait()
    for c in stores:
        c.start()
    for c in stores:
        c.wait()


def join(parts):
    row = len(parts) // PANEL
    ny, nz = parts[0].shape
    dtype = parts[0].dtype
    hbm = pl.BlockSpec(memory_space=pl.ANY)
    edge = pltpu.VMEM((PANEL, 2, ny, nz), dtype)
    return pl.pallas_call(
        lambda *refs: join_kernel(row, *refs),
        out_shape=(pltpu.VMEM((PANEL, row, ny, nz), dtype), edge, edge),
        in_specs=[hbm] * (PANEL * row),
        out_specs=(pl.BlockSpec(memory_space=pltpu.VMEM),) * 3,
        scratch_shapes=[pltpu.SemaphoreType.DMA((PANEL * row,)), pltpu.SemaphoreType.DMA((2,))],
        name="join_panel",
    )(*parts)


def ring(count, shift):
    return [(i, (i + shift) % count) for i in range(count)]


def rows(shift, row):
    count = lax.axis_size("band")
    return [(i, i // row * row + (i + shift) % row) for i in range(count)]


def total(part):
    count = lax.axis_size("dom")
    for group in ((1,), (2,), (4, 8, 12)):
        moved = [lax.ppermute(part, "dom", [(i, i ^ k) for i in range(count)]) for k in group]
        for m in moved:
            part = part + m
    return part


def local(orbitals, owner_band):
    nj, nx, ny, nz = orbitals.shape
    row = nx
    slabs = lax.axis_size("dom")
    me = lax.axis_index("band")
    owner = owner_band[0]
    behind = lax.rem(me + row - lax.rem(owner, row), row)
    same = lax.div(me, row) == lax.div(owner, row)
    up = lambda v: lax.ppermute(v, "dom", ring(lax.axis_size("dom"), 1))
    down = lambda v: lax.ppermute(v, "dom", ring(lax.axis_size("dom"), -1))
    along = lambda v, k: lax.ppermute(v, "band", rows(k, row))
    across = lambda v: lax.ppermute(v, "band", ring(lax.axis_size("band"), row))

    pieces = cut(orbitals)
    o_top, o_bottom = edges(orbitals)
    got = [[pieces[n][0]] + [along(pieces[n][m], m) for m in range(1, row)] for n in range(PANEL)]
    mine = [lax.select_n(behind, *g) for g in got]
    mine[0], o_top, o_bottom = lax.optimization_barrier((mine[0], o_top, o_bottom))
    halo = (up(o_top), down(o_bottom))
    mine = [jnp.where(same, m, across(m)) for m in mine]
    parts = [[m, *[along(m, n) for n in range(1, row)]] for m in mine]
    panel, top, bottom = join(parts[0] + parts[1])
    low, high = up(top), down(bottom)
    exchange = inner(orbitals, panel)
    exchange, sums = outer(exchange, orbitals, halo, panel, low, high)
    cells = float(nx * slabs * ny * nz)
    ace_block = jnp.sum(total(sums)[:PANEL + nj].reshape(PANEL + nj, nj, -1), axis=2) / cells
    return exchange, ace_block[None]


def solution(mesh):
    placed = (P("band", "dom", None, None), P())
    return jax.shard_map(
        local,
        mesh=mesh,
        in_specs=placed,
        out_specs=(P("band", "dom", None, None), P("band", None, None)),
        check_vma=False,
    )
```

time: 91.4 us -> 86.2 us (0.943)
  starting transfers between devices: 42.7 us -> 36.1 us
  waiting for transfers between devices: 13.1 us -> 17.8 us
  Pallas kernels: 27.7 us -> 25.2 us
  local copies, waits for them, and re-layouts: 5.41 us -> 3.02 us
  other arithmetic: 0.78 us -> 2.01 us
    ppermute x12, waiting for transfers between devices: 3.56 us -> 9.85 us  [local(): along = lambda v, k: lax.ppermute(v, 'band', rows(k, row))]
    ppermute x3 -> x2, starting transfers between devices: 15.9 us -> 10.7 us  [local(): down = lambda v: lax.ppermute(v, 'dom', ring(lax.axis_size('dom'), -1))]
    slice x1 -> x0, local copies, waits for them, and re-layouts: 2.87 us -> none  [local(): plane = lambda v, x: v[:, x:x + 1]]
    pallas_call x2 -> x3, Pallas kernels: 16.6 us -> 14.3 us  [the longest x1 10.2 us: inner(): pl.pallas_call(inner_kernel, grid=(nj,), out_shape=pltpu.VMEM((nj, nx, ny...]
    select_n x2, other arithmetic: 0.07 us -> 1.88 us  [local(): mine = [lax.select_n(behind, *g) for g in got]]
    ppermute x12, starting transfers between devices: 19.1 us -> 17.3 us  [local(): along = lambda v, k: lax.ppermute(v, 'band', rows(k, row))]
    ppermute x5, waiting for transfers between devices: 9.49 us -> 7.95 us  [total(): lax.ppermute(part, 'dom', [(i, i ^ k) for i in range(count)])]
    unnamed x28 -> x20, local copies, waits for them, and re-layouts: 2.54 us -> 2.27 us
  transfers between devices with their start and end apart: 25 -> 23, of which waited for: 7 -> 11; matrix products, arithmetic and copies ran while one was open for 3% -> 2% of each run, Pallas kernels for 18% -> 17%
where the time goes in v3:
time: 86.2 us; the launch traced here: 85.7 us
  starting transfers between devices  36.1 us (42%)
  Pallas kernels  25.2 us (29%)
  waiting for transfers between devices  17.8 us (21%)
  local copies, waits for them, and re-layouts  3.02 us (4%)
  other arithmetic  2.01 us (2%)
  between operations  1.51 us (2%)
    ppermute x12, starting transfers between devices, local(): along = lambda v, k: lax.ppermute(v, 'band', rows(k, row))  17.3 us
    ppermute x2, starting transfers between devices, local(): down = lambda v: lax.ppermute(v, 'dom', ring(lax.axis_size('dom'), -1))  10.7 us
    pallas_call x1, Pallas kernels, inner(): pl.pallas_call(inner_kernel, grid=(nj,), out_shape=pltpu.VMEM((nj, nx, ny...  10.2 us
    ppermute x12, waiting for transfers between devices, local(): along = lambda v, k: lax.ppermute(v, 'band', rows(k, row))  9.85 us
    pallas_call x1, Pallas kernels, outer(): pl.pallas_call(outer_kernel, grid=(nj,), out_shape=(jax.ShapeDtypeStruct(...  8.79 us
    ppermute x5, waiting for transfers between devices, total(): lax.ppermute(part, 'dom', [(i, i ^ k) for i in range(count)])  7.95 us
    ppermute x5, starting transfers between devices, total(): lax.ppermute(part, 'dom', [(i, i ^ k) for i in range(count)])  4.77 us
    ppermute x2, starting transfers between devices, local(): across = lambda v: lax.ppermute(v, 'band', ring(lax.axis_size('band'), row))  3.31 us
  transfers between devices with their start and end apart: 23, of which 11 were waited for; matrix products, arithmetic and copies ran while one was open for 2% of the time, Pallas kernels for 17%

profile of v3, /device:TPU:0, one launch (start us, length us, event | category | flops | bytes accessed | tf_op | source)
XLA Modules:
  0.0 85.7 jit_solution(4906208820281484669)
XLA Ops:
  0.6 0.0 copy-start.2
  0.6 2.1 %cut_panel.1 = (bf16[256,256]{1,0:T(8,128)(2,1)}, bf16[256,256]{1,0:T(8,128)(2,1)}, bf16[256,256]{1,0:T(8,128)(2,1)}, bf16[256,256]{1,0:T(8,128)(2,1)}, bf16[256...) custom-call(bf16[4,4,256,256]{3,2,1,0:T(8,128)(2,1)} %o.3), custom_call_target="tpu_custom_call" | custom-call | tf_op jit(solution)/shard_map/cut_panel/pallas_call | solution.py:274
  2.8 1.6 %collective-permute-start.7 = (bf16[256,256]{1,0:T(8,128)(2,1)}, bf16[256,256]{1,0:T(8,128)(2,1)S(1)}, u32[]{:S(2)}, u32[]{:S(2)}) collective-permute-start(bf16[256,256]{1,0:T(8,128)(2,1)} %get-tuple-element.28), channel_id=1, source_target_pairs={{0,16},{16,32},{32,48},{48,0},{64,80},{80,96},{96,112},{112,64},{1... | collective-permute-start | bytes 393224 | tf_op jit(solution)/shard_map/ppermute | solution.py:381
  4.4 2.7 %collective-permute-start.8 = (bf16[256,256]{1,0:T(8,128)(2,1)}, bf16[256,256]{1,0:T(8,128)(2,1)S(1)}, u32[]{:S(2)}, u32[]{:S(2)}) collective-permute-start(bf16[256,256]{1,0:T(8,128)(2,1)} %get-tuple-element.29), channel_id=1, source_target_pairs={{0,32},{16,48},{32,0},{48,16},{64,96},{80,112},{96,64},{112,80},{1... | collective-permute-start | bytes 393224 | tf_op jit(solution)/shard_map/ppermute | solution.py:381
  7.2 1.4 %collective-permute-start.9 = (bf16[256,256]{1,0:T(8,128)(2,1)}, bf16[256,256]{1,0:T(8,128)(2,1)S(1)}, u32[]{:S(2)}, u32[]{:S(2)}) collective-permute-start(bf16[256,256]{1,0:T(8,128)(2,1)} %get-tuple-element.30), channel_id=1, source_target_pairs={{0,48},{16,0},{32,16},{48,32},{64,112},{80,64},{96,80},{112,96},{1... | collective-permute-start | bytes 393224 | tf_op jit(solution)/shard_map/ppermute | solution.py:381
  8.6 0.6 collective-permute-start
  9.2 0.9 %collective-permute-start.1 = (bf16[256,256]{1,0:T(8,128)(2,1)}, bf16[256,256]{1,0:T(8,128)(2,1)S(1)}, u32[]{:S(2)}, u32[]{:S(2)}) collective-permute-start(bf16[256,256]{1,0:T(8,128)(2,1)} %get-tuple-element.22), channel_id=1, source_target_pairs={{0,32},{16,48},{32,0},{48,16},{64,96},{80,112},{96,64},{112,80},{1... | collective-permute-start | bytes 393224 | tf_op jit(solution)/shard_map/ppermute | solution.py:381
  10.7 2.6 %edge_planes.1 = (bf16[4,2,256,256]{3,2,1,0:T(8,128)(2,1)}, bf16[4,2,256,256]{3,2,1,0:T(8,128)(2,1)}) custom-call(bf16[4,4,256,256]{3,2,1,0:T(8,128)(2,1)} %o.3), custom_call_target="tpu_custom_call" | custom-call | tf_op jit(solution)/shard_map/edge_planes/pallas_call | solution.py:305
  13.4 1.9 %collective-permute-start.2 = (bf16[256,256]{1,0:T(8,128)(2,1)}, bf16[256,256]{1,0:T(8,128)(2,1)S(1)}, u32[]{:S(2)}, u32[]{:S(2)}) collective-permute-start(bf16[256,256]{1,0:T(8,128)(2,1)} %get-tuple-element.23), channel_id=1, source_target_pairs={{0,48},{16,0},{32,16},{48,32},{64,112},{80,64},{96,80},{112,96},{1... | collective-permute-start | bytes 393224 | tf_op jit(solution)/shard_map/ppermute | solution.py:381
  15.2 0.0 collective-permute-done.8
  15.2 0.9 %select_select_fusion = bf16[256,256]{1,0:T(8,128)(2,1)S(1)} fusion(bf16[256,256]{1,0:T(8,128)(2,1)S(1)} %collective-permute-done.8, bf16[256,256]{1,0:T(8,128)(2,1)S(1)} %collective-permute-done.9, bf16[256,256]{1,0:T(8,128)(2,1)} %get-tuple-element.27, bf16[256,256]{1,0:T(8,128)(2,1)S(1)} %collective-permute-done.7, pred[]{:T(512)S(6)} %select_n.60, ...), kind=kLoop, calls=%fused_computation | loop fusion | flops 196608 | bytes 655363 | tf_op jit(solution)/shard_map/select_n | solution.py:387
  16.2 1.7 %collective-permute-start.10 = (bf16[256,256]{1,0:T(8,128)(2,1)S(1)}, bf16[256,256]{1,0:T(8,128)(2,1)S(1)}, u32[]{:S(2)}, u32[]{:S(2)}) collective-permute-start(bf16[256,256]{1,0:T(8,128)(2,1)S(1)} %select_select_fusion), channel_id=1, source_target_pairs={{0,64},{16,80},{32,96},{48,112},{64,0},{80,16},{96,32},{112,48},{1... | collective-permute-start | bytes 393224 | tf_op jit(solution)/shard_map/ppermute | solution.py:382
  17.8 0.0 collective-permute-done
  17.8 1.2 %collective-permute-done.1 = bf16[256,256]{1,0:T(8,128)(2,1)S(1)} collective-permute-done((bf16[256,256]{1,0:T(8,128)(2,1)}, bf16[256,256]{1,0:T(8,128)(2,1)S(1)}, u32[]{:S(2)}, u32[]{:S(2)}) %collective-permute-start.1) | collective-permute-done | bytes 131104 | tf_op jit(solution)/shard_map/ppermute | solution.py:381
  19.0 0.2 collective-permute-done.2
  19.2 0.9 %select_select_fusion.1 = bf16[256,256]{1,0:T(8,128)(2,1)S(1)} fusion(bf16[256,256]{1,0:T(8,128)(2,1)S(1)} %collective-permute-done.1, bf16[256,256]{1,0:T(8,128)(2,1)S(1)} %collective-permute-done.2, bf16[256,256]{1,0:T(8,128)(2,1)} %get-tuple-element.20, bf16[256,256]{1,0:T(8,128)(2,1)S(1)} %collective-permute-done, pred[]{:T(512)S(6)} %select_n.60, ...), kind=kLoop, calls=%fused_computation.1 | loop fusion | flops 196608 | bytes 655363 | tf_op jit(solution)/shard_map/select_n | solution.py:387
  20.2 1.7 %collective-permute-start.3 = (bf16[256,256]{1,0:T(8,128)(2,1)S(1)}, bf16[256,256]{1,0:T(8,128)(2,1)S(1)}, u32[]{:S(2)}, u32[]{:S(2)}) collective-permute-start(bf16[256,256]{1,0:T(8,128)(2,1)S(1)} %select_select_fusion.1), channel_id=1, source_target_pairs={{0,64},{16,80},{32,96},{48,112},{64,0},{80,16},{96,32},{112,48},{1... | collective-permute-start | bytes 393224 | tf_op jit(solution)/shard_map/ppermute | solution.py:382
  21.8 0.0 collective-permute-start.14
  21.8 5.4 %collective-permute-start.15 = (bf16[4,2,256,256]{3,2,1,0:T(8,128)(2,1)}, bf16[4,2,256,256]{3,2,1,0:T(8,128)(2,1)}, u32[]{:S(2)}, u32[]{:S(2)}) collective-permute-start(bf16[4,2,256,256]{3,2,1,0:T(8,128)(2,1)} %get-tuple-element.33), channel_id=1, source_target_pairs={{0,15},{1,0},{2,1},{3,2},{4,3},{5,4},{6,5},{7,6},{8,7},{9,8},{10,9... | collective-permute-start | bytes 3145736 | tf_op jit(solution)/shard_map/ppermute | solution.py:380
  27.2 0.0 collective-permute-done.10
  27.2 1.6 %collective-permute-start.13 = (bf16[256,256]{1,0:T(8,128)(2,1)S(1)}, bf16[256,256]{1,0:T(8,128)(2,1)S(1)}, u32[]{:S(2)}, u32[]{:S(2)}) collective-permute-start(bf16[256,256]{1,0:T(8,128)(2,1)S(1)} %broadcast_select_fusion.refs_4_), channel_id=1, source_target_pairs={{0,48},{16,0},{32,16},{48,32},{64,112},{80,64},{96,80},{112,96},{1... | collective-permute-start | bytes 393224 | tf_op jit(solution)/shard_map/ppermute | solution.py:381
  28.8 1.7 %collective-permute-start.12 = (bf16[256,256]{1,0:T(8,128)(2,1)S(1)}, bf16[256,256]{1,0:T(8,128)(2,1)S(1)}, u32[]{:S(2)}, u32[]{:S(2)}) collective-permute-start(bf16[256,256]{1,0:T(8,128)(2,1)S(1)} %broadcast_select_fusion.refs_4_), channel_id=1, source_target_pairs={{0,32},{16,48},{32,0},{48,16},{64,96},{80,112},{96,64},{112,80},{1... | collective-permute-start | bytes 393224 | tf_op jit(solution)/shard_map/ppermute | solution.py:381
  30.6 2.3 %collective-permute-done.13.refs_7_ = bf16[256,256]{1,0:T(8,128)(2,1)S(1)} collective-permute-done((bf16[256,256]{1,0:T(8,128)(2,1)S(1)}, bf16[256,256]{1,0:T(8,128)(2,1)S(1)}, u32[]{:S(2)}, u32[]{:S(2)}) %collective-permute-start.13) | collective-permute-done | bytes 131104 | tf_op jit(solution)/shard_map/ppermute | solution.py:381
  32.9 2.1 %collective-permute-start.6 = (bf16[256,256]{1,0:T(8,128)(2,1)S(1)}, bf16[256,256]{1,0:T(8,128)(2,1)S(1)}, u32[]{:S(2)}, u32[]{:S(2)}) collective-permute-start(bf16[256,256]{1,0:T(8,128)(2,1)S(1)} %broadcast_select_fusion.1.refs_0_), channel_id=1, source_target_pairs={{0,48},{16,0},{32,16},{48,32},{64,112},{80,64},{96,80},{112,96},{1... | collective-permute-start | bytes 393224 | tf_op jit(solution)/shard_map/ppermute | solution.py:381
  35.0 0.3 collective-permute-done.12.refs_6_
  35.3 1.8 %collective-permute-start.5 = (bf16[256,256]{1,0:T(8,128)(2,1)S(1)}, bf16[256,256]{1,0:T(8,128)(2,1)S(1)}, u32[]{:S(2)}, u32[]{:S(2)}) collective-permute-start(bf16[256,256]{1,0:T(8,128)(2,1)S(1)} %broadcast_select_fusion.1.refs_0_), channel_id=1, source_target_pairs={{0,32},{16,48},{32,0},{48,16},{64,96},{80,112},{96,64},{112,80},{1... | collective-permute-start | bytes 393224 | tf_op jit(solution)/shard_map/ppermute | solution.py:381
  37.1 1.1 %collective-permute-done.11.refs_5_ = bf16[256,256]{1,0:T(8,128)(2,1)S(1)} collective-permute-done((bf16[256,256]{1,0:T(8,128)(2,1)S(1)}, bf16[256,256]{1,0:T(8,128)(2,1)S(1)}, u32[]{:S(2)}, u32[]{:S(2)}) %collective-permute-start.11) | collective-permute-done | bytes 131104 | tf_op jit(solution)/shard_map/ppermute | solution.py:381
  38.3 0.9 %collective-permute-start.4 = (bf16[256,256]{1,0:T(8,128)(2,1)S(1)}, bf16[256,256]{1,0:T(8,128)(2,1)}, u32[]{:S(2)}, u32[]{:S(2)}) collective-permute-start(bf16[256,256]{1,0:T(8,128)(2,1)S(1)} %broadcast_select_fusion.1.refs_0_), channel_id=1, source_target_pairs={{0,16},{16,32},{32,48},{48,0},{64,80},{80,96},{96,112},{112,64},{1... | collective-permute-start | bytes 393224 | tf_op jit(solution)/shard_map/ppermute | solution.py:381
  39.1 2.6 %collective-permute-done.5.refs_2_ = bf16[256,256]{1,0:T(8,128)(2,1)S(1)} collective-permute-done((bf16[256,256]{1,0:T(8,128)(2,1)S(1)}, bf16[256,256]{1,0:T(8,128)(2,1)S(1)}, u32[]{:S(2)}, u32[]{:S(2)}) %collective-permute-start.5) | collective-permute-done | bytes 131104 | tf_op jit(solution)/shard_map/ppermute | solution.py:381
  41.8 0.6 copy-done.9
  42.4 2.1 %collective-permute-done.4.refs_1_ = bf16[256,256]{1,0:T(8,128)(2,1)} collective-permute-done((bf16[256,256]{1,0:T(8,128)(2,1)S(1)}, bf16[256,256]{1,0:T(8,128)(2,1)}, u32[]{:S(2)}, u32[]{:S(2)}) %collective-permute-start.4) | collective-permute-done | bytes 131104 | tf_op jit(solution)/shard_map/ppermute | solution.py:381
  44.5 1.4 %join_panel.1 = (bf16[2,4,256,256]{3,2,1,0:T(8,128)(2,1)S(1)}, bf16[2,2,256,256]{3,2,1,0:T(8,128)(2,1)S(1)}, bf16[2,2,256,256]{3,2,1,0:T(8,128)(2,1)S(1)}) custom-call(bf16[256,256]{1,0:T(8,128)(2,1)} %copy-done.4, bf16[256,256]{1,0:T(8,128)(2,1)} %collective-permute-done.4.refs_1_, bf16[256,256]{1,0:T(8,128)(2,1)} %copy-done.9, bf16[256,256]{1,0:T(8,128)(2,1)} %copy-done.8, ...), custom_call_target="tpu_custom_call" | custom-call | tf_op jit(solution)/shard_map/join_panel/pallas_call | solution.py:343
  46.0 0.1 collective-permute-start.16
  46.1 5.3 %collective-permute-start.17 = (bf16[2,2,256,256]{3,2,1,0:T(8,128)(2,1)S(1)}, bf16[2,2,256,256]{3,2,1,0:T(8,128)(2,1)S(1)}, u32[]{:S(2)}, u32[]{:S(2)}) collective-permute-start(bf16[2,2,256,256]{3,2,1,0:T(8,128)(2,1)S(1)} %get-tuple-element.35), channel_id=1, source_target_pairs={{0,15},{1,0},{2,1},{3,2},{4,3},{5,4},{6,5},{7,6},{8,7},{9,8},{10,9... | collective-permute-start | bytes 1572872 | tf_op jit(solution)/shard_map/ppermute | solution.py:380
  51.4 1.6 %copy-done = bf16[4,4,256,256]{3,2,1,0:T(8,128)(2,1)S(1)} copy-done((bf16[4,4,256,256]{3,2,1,0:T(8,128)(2,1)S(1)}, bf16[4,4,256,256]{3,2,1,0:T(8,128)(2,1)}, u32[]{:S(2)}) %copy-start) | copy-done | bytes 2097176
  53.0 10.2 %inner_field.1.e_in = f32[4,4,256,256]{3,2,1,0:T(8,128)S(1)} custom-call(bf16[4,4,256,256]{3,2,1,0:T(8,128)(2,1)S(1)} %copy-done, bf16[2,4,256,256]{3,2,1,0:T(8,128)(2,1)S(1)} %get-tuple-element.31.p, bf16[768,256]{1,0:T(8,128)(2,1)S(1)} %copy-done.2), custom_call_target="tpu_custom_call" | custom-call | flops 6000000000 | bytes 8388608 | tf_op jit(solution)/shard_map/inner_field/pallas_call | solution.py:130
  63.3 8.8 %outer_field.1 = (f32[4,4,256,256]{3,2,1,0:T(8,128)}, f32[8,128]{1,0:T(8,128)S(1)}) custom-call(f32[4,4,256,256]{3,2,1,0:T(8,128)S(1)} %inner_field.1.e_in, bf16[4,4,256,256]{3,2,1,0:T(8,128)(2,1)S(1)} %copy-done.1, bf16[4,2,256,256]{3,2,1,0:T(8,128)(2,1)S(1)} %collective-permute-done.14.halo_low, ...), custom_call_target="tpu_custom_call" | custom-call | flops 3000000000 | bytes 14680064 | tf_op jit(solution)/shard_map/outer_field/pallas_call | solution.py:235
  72.1 1.2 %collective-permute-done.18 = f32[8,128]{1,0:T(8,128)S(1)} collective-permute-done((f32[8,128]{1,0:T(8,128)S(1)}, f32[8,128]{1,0:T(8,128)S(1)}, u32[]{:S(2)}, u32[]{:S(2)}) %collective-permute-start.18) | collective-permute-done | bytes 4128 | tf_op jit(solution)/shard_map/ppermute | solution.py:365
  73.3 0.7 collective-permute-start.19
  73.9 4.4 %collective-permute-done.19 = f32[8,128]{1,0:T(8,128)S(1)} collective-permute-done((f32[8,128]{1,0:T(8,128)S(1)}, f32[8,128]{1,0:T(8,128)S(1)}, u32[]{:S(2)}, u32[]{:S(2)}) %collective-permute-start.19) | collective-permute-done | bytes 4128 | tf_op jit(solution)/shard_map/ppermute | solution.py:365
  78.4 1.3 %collective-permute-start.22 = (f32[8,128]{1,0:T(8,128)S(1)}, f32[8,128]{1,0:T(8,128)S(1)}, u32[]{:S(2)}, u32[]{:S(2)}) collective-permute-start(f32[8,128]{1,0:T(8,128)S(1)} %add.20), channel_id=1, source_target_pairs={{0,12},{1,13},{2,14},{3,15},{4,8},{5,9},{6,10},{7,11},{8,4},{9,5},... | collective-permute-start | bytes 12296 | tf_op jit(solution)/shard_map/ppermute | solution.py:365
  79.7 0.5 collective-permute-start.21
  80.2 2.3 %collective-permute-start.20 = (f32[8,128]{1,0:T(8,128)S(1)}, f32[8,128]{1,0:T(8,128)S(1)}, u32[]{:S(2)}, u32[]{:S(2)}) collective-permute-start(f32[8,128]{1,0:T(8,128)S(1)} %add.20), channel_id=1, source_target_pairs={{0,4},{1,5},{2,6},{3,7},{4,0},{5,1},{6,2},{7,3},{8,12},{9,13},{10,... | collective-permute-start | bytes 12296 | tf_op jit(solution)/shard_map/ppermute | solution.py:365
  82.5 0.7 collective-permute-done.22
  83.2 1.6 %collective-permute-done.21 = f32[8,128]{1,0:T(8,128)S(1)} collective-permute-done((f32[8,128]{1,0:T(8,128)S(1)}, f32[8,128]{1,0:T(8,128)S(1)}, u32[]{:S(2)}, u32[]{:S(2)}) %collective-permute-start.21) | collective-permute-done | bytes 4128 | tf_op jit(solution)/shard_map/ppermute | solution.py:365
  84.8 0.1 reshape.16
  84.9 0.1 reduce_sum.9
  85.0 0.7 copy.6
  (34 shorter events, 0.1 us)
Async XLA Ops:
  0.6 50.8 %copy-start.2 = (bf16[768,256]{1,0:T(8,128)(2,1)S(1)}, bf16[768,256]{1,0:T(8,128)(2,1)}, u32[]{:S(2)}) copy-start(bf16[768,256]{1,0:T(8,128)(2,1)} %constant.32.mix) | copy-start | bytes 1179652
  2.8 10.6 %collective-permute-start.7 = (bf16[256,256]{1,0:T(8,128)(2,1)}, bf16[256,256]{1,0:T(8,128)(2,1)S(1)}, u32[]{:S(2)}, u32[]{:S(2)}) collective-permute-start(bf16[256,256]{1,0:T(8,128)(2,1)} %get-tuple-element.28), channel_id=1, source_target_pairs={{0,16},{16,32},{32,48},{48,0},{64,80},{80,96},{96,112},{112,64},{1... | collective-permute-start | bytes 393224 | tf_op jit(solution)/shard_map/ppermute | solution.py:381
  4.4 10.8 %collective-permute-start.8 = (bf16[256,256]{1,0:T(8,128)(2,1)}, bf16[256,256]{1,0:T(8,128)(2,1)S(1)}, u32[]{:S(2)}, u32[]{:S(2)}) collective-permute-start(bf16[256,256]{1,0:T(8,128)(2,1)} %get-tuple-element.29), channel_id=1, source_target_pairs={{0,32},{16,48},{32,0},{48,16},{64,96},{80,112},{96,64},{112,80},{1... | collective-permute-start | bytes 393224 | tf_op jit(solution)/shard_map/ppermute | solution.py:381
  7.2 8.1 %collective-permute-start.9 = (bf16[256,256]{1,0:T(8,128)(2,1)}, bf16[256,256]{1,0:T(8,128)(2,1)S(1)}, u32[]{:S(2)}, u32[]{:S(2)}) collective-permute-start(bf16[256,256]{1,0:T(8,128)(2,1)} %get-tuple-element.30), channel_id=1, source_target_pairs={{0,48},{16,0},{32,16},{48,32},{64,112},{80,64},{96,80},{112,96},{1... | collective-permute-start | bytes 393224 | tf_op jit(solution)/shard_map/ppermute | solution.py:381
  8.6 9.2 %collective-permute-start = (bf16[256,256]{1,0:T(8,128)(2,1)}, bf16[256,256]{1,0:T(8,128)(2,1)S(1)}, u32[]{:S(2)}, u32[]{:S(2)}) collective-permute-start(bf16[256,256]{1,0:T(8,128)(2,1)} %get-tuple-element.21), channel_id=1, source_target_pairs={{0,16},{16,32},{32,48},{48,0},{64,80},{80,96},{96,112},{112,64},{1... | collective-permute-start | bytes 393224 | tf_op jit(solution)/shard_map/ppermute | solution.py:381
  9.2 9.8 %collective-permute-start.1 = (bf16[256,256]{1,0:T(8,128)(2,1)}, bf16[256,256]{1,0:T(8,128)(2,1)S(1)}, u32[]{:S(2)}, u32[]{:S(2)}) collective-permute-start(bf16[256,256]{1,0:T(8,128)(2,1)} %get-tuple-element.22), channel_id=1, source_target_pairs={{0,32},{16,48},{32,0},{48,16},{64,96},{80,112},{96,64},{112,80},{1... | collective-permute-start | bytes 393224 | tf_op jit(solution)/shard_map/ppermute | solution.py:381
  13.4 5.9 %collective-permute-start.2 = (bf16[256,256]{1,0:T(8,128)(2,1)}, bf16[256,256]{1,0:T(8,128)(2,1)S(1)}, u32[]{:S(2)}, u32[]{:S(2)}) collective-permute-start(bf16[256,256]{1,0:T(8,128)(2,1)} %get-tuple-element.23), channel_id=1, source_target_pairs={{0,48},{16,0},{32,16},{48,32},{64,112},{80,64},{96,80},{112,96},{1... | collective-permute-start | bytes 393224 | tf_op jit(solution)/shard_map/ppermute | solution.py:381
  16.2 11.0 %collective-permute-start.10 = (bf16[256,256]{1,0:T(8,128)(2,1)S(1)}, bf16[256,256]{1,0:T(8,128)(2,1)S(1)}, u32[]{:S(2)}, u32[]{:S(2)}) collective-permute-start(bf16[256,256]{1,0:T(8,128)(2,1)S(1)} %select_select_fusion), channel_id=1, source_target_pairs={{0,64},{16,80},{32,96},{48,112},{64,0},{80,16},{96,32},{112,48},{1... | collective-permute-start | bytes 393224 | tf_op jit(solution)/shard_map/ppermute | solution.py:382
  20.2 10.4 %collective-permute-start.3 = (bf16[256,256]{1,0:T(8,128)(2,1)S(1)}, bf16[256,256]{1,0:T(8,128)(2,1)S(1)}, u32[]{:S(2)}, u32[]{:S(2)}) collective-permute-start(bf16[256,256]{1,0:T(8,128)(2,1)S(1)} %select_select_fusion.1), channel_id=1, source_target_pairs={{0,64},{16,80},{32,96},{48,112},{64,0},{80,16},{96,32},{112,48},{1... | collective-permute-start | bytes 393224 | tf_op jit(solution)/shard_map/ppermute | solution.py:382
  21.8 41.4 %collective-permute-start.14 = (bf16[4,2,256,256]{3,2,1,0:T(8,128)(2,1)}, bf16[4,2,256,256]{3,2,1,0:T(8,128)(2,1)S(1)}, u32[]{:S(2)}, u32[]{:S(2)}) collective-permute-start(bf16[4,2,256,256]{3,2,1,0:T(8,128)(2,1)} %get-tuple-element.32), channel_id=1, source_target_pairs={{0,1},{1,2},{2,3},{3,4},{4,5},{5,6},{6,7},{7,8},{8,9},{9,10},{10,1... | collective-permute-start | bytes 3145736 | tf_op jit(solution)/shard_map/ppermute | solution.py:379
  21.8 41.5 %collective-permute-start.15 = (bf16[4,2,256,256]{3,2,1,0:T(8,128)(2,1)}, bf16[4,2,256,256]{3,2,1,0:T(8,128)(2,1)}, u32[]{:S(2)}, u32[]{:S(2)}) collective-permute-start(bf16[4,2,256,256]{3,2,1,0:T(8,128)(2,1)} %get-tuple-element.33), channel_id=1, source_target_pairs={{0,15},{1,0},{2,1},{3,2},{4,3},{5,4},{6,5},{7,6},{8,7},{9,8},{10,9... | collective-permute-start | bytes 3145736 | tf_op jit(solution)/shard_map/ppermute | solution.py:380
  27.2 14.5 %copy-start.3 = (bf16[256,256]{1,0:T(8,128)(2,1)}, bf16[256,256]{1,0:T(8,128)(2,1)S(1)}, u32[]{:S(2)}) copy-start(bf16[256,256]{1,0:T(8,128)(2,1)S(1)} %broadcast_select_fusion.refs_4_) | copy-start | bytes 393220
  27.2 5.7 %collective-permute-start.13 = (bf16[256,256]{1,0:T(8,128)(2,1)S(1)}, bf16[256,256]{1,0:T(8,128)(2,1)S(1)}, u32[]{:S(2)}, u32[]{:S(2)}) collective-permute-start(bf16[256,256]{1,0:T(8,128)(2,1)S(1)} %broadcast_select_fusion.refs_4_), channel_id=1, source_target_pairs={{0,48},{16,0},{32,16},{48,32},{64,112},{80,64},{96,80},{112,96},{1... | collective-permute-start | bytes 393224 | tf_op jit(solution)/shard_map/ppermute | solution.py:381
  28.8 6.5 %collective-permute-start.12 = (bf16[256,256]{1,0:T(8,128)(2,1)S(1)}, bf16[256,256]{1,0:T(8,128)(2,1)S(1)}, u32[]{:S(2)}, u32[]{:S(2)}) collective-permute-start(bf16[256,256]{1,0:T(8,128)(2,1)S(1)} %broadcast_select_fusion.refs_4_), channel_id=1, source_target_pairs={{0,32},{16,48},{32,0},{48,16},{64,96},{80,112},{96,64},{112,80},{1... | collective-permute-start | bytes 393224 | tf_op jit(solution)/shard_map/ppermute | solution.py:381
  30.5 7.7 %collective-permute-start.11 = (bf16[256,256]{1,0:T(8,128)(2,1)S(1)}, bf16[256,256]{1,0:T(8,128)(2,1)S(1)}, u32[]{:S(2)}, u32[]{:S(2)}) collective-permute-start(bf16[256,256]{1,0:T(8,128)(2,1)S(1)} %broadcast_select_fusion.refs_4_), channel_id=1, source_target_pairs={{0,16},{16,32},{32,48},{48,0},{64,80},{80,96},{96,112},{112,64},{1... | collective-permute-start | bytes 393224 | tf_op jit(solution)/shard_map/ppermute | solution.py:381
  30.6 11.2 %copy-start.4 = (bf16[256,256]{1,0:T(8,128)(2,1)}, bf16[256,256]{1,0:T(8,128)(2,1)S(1)}, u32[]{:S(2)}) copy-start(bf16[256,256]{1,0:T(8,128)(2,1)S(1)} %broadcast_select_fusion.1.refs_0_) | copy-start | bytes 393220
  32.9 8.9 %copy-start.5 = (bf16[256,256]{1,0:T(8,128)(2,1)}, bf16[256,256]{1,0:T(8,128)(2,1)S(1)}, u32[]{:S(2)}) copy-start(bf16[256,256]{1,0:T(8,128)(2,1)S(1)} %collective-permute-done.13.refs_7_) | copy-start | bytes 393220
  32.9 6.3 %collective-permute-start.6 = (bf16[256,256]{1,0:T(8,128)(2,1)S(1)}, bf16[256,256]{1,0:T(8,128)(2,1)S(1)}, u32[]{:S(2)}, u32[]{:S(2)}) collective-permute-start(bf16[256,256]{1,0:T(8,128)(2,1)S(1)} %broadcast_select_fusion.1.refs_0_), channel_id=1, source_target_pairs={{0,48},{16,0},{32,16},{48,32},{64,112},{80,64},{96,80},{112,96},{1... | collective-permute-start | bytes 393224 | tf_op jit(solution)/shard_map/ppermute | solution.py:381
  35.3 6.5 %copy-start.6 = (bf16[256,256]{1,0:T(8,128)(2,1)}, bf16[256,256]{1,0:T(8,128)(2,1)S(1)}, u32[]{:S(2)}) copy-start(bf16[256,256]{1,0:T(8,128)(2,1)S(1)} %collective-permute-done.12.refs_6_) | copy-start | bytes 393220
  35.3 6.5 %collective-permute-start.5 = (bf16[256,256]{1,0:T(8,128)(2,1)S(1)}, bf16[256,256]{1,0:T(8,128)(2,1)S(1)}, u32[]{:S(2)}, u32[]{:S(2)}) collective-permute-start(bf16[256,256]{1,0:T(8,128)(2,1)S(1)} %broadcast_select_fusion.1.refs_0_), channel_id=1, source_target_pairs={{0,32},{16,48},{32,0},{48,16},{64,96},{80,112},{96,64},{112,80},{1... | collective-permute-start | bytes 393224 | tf_op jit(solution)/shard_map/ppermute | solution.py:381
  38.3 3.5 %copy-start.7 = (bf16[256,256]{1,0:T(8,128)(2,1)}, bf16[256,256]{1,0:T(8,128)(2,1)S(1)}, u32[]{:S(2)}) copy-start(bf16[256,256]{1,0:T(8,128)(2,1)S(1)} %collective-permute-done.11.refs_5_) | copy-start | bytes 393220
  38.3 6.3 %collective-permute-start.4 = (bf16[256,256]{1,0:T(8,128)(2,1)S(1)}, bf16[256,256]{1,0:T(8,128)(2,1)}, u32[]{:S(2)}, u32[]{:S(2)}) collective-permute-start(bf16[256,256]{1,0:T(8,128)(2,1)S(1)} %broadcast_select_fusion.1.refs_0_), channel_id=1, source_target_pairs={{0,16},{16,32},{32,48},{48,0},{64,80},{80,96},{96,112},{112,64},{1... | collective-permute-start | bytes 393224 | tf_op jit(solution)/shard_map/ppermute | solution.py:381
  39.1 2.6 %copy-start.8 = (bf16[256,256]{1,0:T(8,128)(2,1)}, bf16[256,256]{1,0:T(8,128)(2,1)S(1)}, u32[]{:S(2)}) copy-start(bf16[256,256]{1,0:T(8,128)(2,1)S(1)} %collective-permute-done.6.refs_3_) | copy-start | bytes 393220
  41.8 0.7 copy-start.9
  46.0 17.3 %collective-permute-start.16 = (bf16[2,2,256,256]{3,2,1,0:T(8,128)(2,1)S(1)}, bf16[2,2,256,256]{3,2,1,0:T(8,128)(2,1)S(1)}, u32[]{:S(2)}, u32[]{:S(2)}) collective-permute-start(bf16[2,2,256,256]{3,2,1,0:T(8,128)(2,1)S(1)} %get-tuple-element.34), channel_id=1, source_target_pairs={{0,1},{1,2},{2,3},{3,4},{4,5},{5,6},{6,7},{7,8},{8,9},{9,10},{10,1... | collective-permute-start | bytes 1572872 | tf_op jit(solution)/shard_map/ppermute | solution.py:379
  46.1 17.2 %collective-permute-start.17 = (bf16[2,2,256,256]{3,2,1,0:T(8,128)(2,1)S(1)}, bf16[2,2,256,256]{3,2,1,0:T(8,128)(2,1)S(1)}, u32[]{:S(2)}, u32[]{:S(2)}) collective-permute-start(bf16[2,2,256,256]{3,2,1,0:T(8,128)(2,1)S(1)} %get-tuple-element.35), channel_id=1, source_target_pairs={{0,15},{1,0},{2,1},{3,2},{4,3},{5,4},{6,5},{7,6},{8,7},{9,8},{10,9... | collective-permute-start | bytes 1572872 | tf_op jit(solution)/shard_map/ppermute | solution.py:380
  51.4 1.6 %copy-start = (bf16[4,4,256,256]{3,2,1,0:T(8,128)(2,1)S(1)}, bf16[4,4,256,256]{3,2,1,0:T(8,128)(2,1)}, u32[]{:S(2)}) copy-start(bf16[4,4,256,256]{3,2,1,0:T(8,128)(2,1)} %o.3) | copy-start | bytes 6291460
  53.0 10.3 %copy-start.1 = (bf16[4,4,256,256]{3,2,1,0:T(8,128)(2,1)S(1)}, bf16[4,4,256,256]{3,2,1,0:T(8,128)(2,1)}, u32[]{:S(2)}) copy-start(bf16[4,4,256,256]{3,2,1,0:T(8,128)(2,1)} %o.3) | copy-start | bytes 6291460
  72.1 1.2 %collective-permute-start.18 = (f32[8,128]{1,0:T(8,128)S(1)}, f32[8,128]{1,0:T(8,128)S(1)}, u32[]{:S(2)}, u32[]{:S(2)}) collective-permute-start(f32[8,128]{1,0:T(8,128)S(1)} %get-tuple-element.37), channel_id=1, source_target_pairs={{0,1},{1,0},{2,3},{3,2},{4,5},{5,4},{6,7},{7,6},{8,9},{9,8},{10,11... | collective-permute-start | bytes 12296 | tf_op jit(solution)/shard_map/ppermute | solution.py:365
  73.3 5.1 %collective-permute-start.19 = (f32[8,128]{1,0:T(8,128)S(1)}, f32[8,128]{1,0:T(8,128)S(1)}, u32[]{:S(2)}, u32[]{:S(2)}) collective-permute-start(f32[8,128]{1,0:T(8,128)S(1)} %add.19), channel_id=1, source_target_pairs={{0,2},{1,3},{2,0},{3,1},{4,6},{5,7},{6,4},{7,5},{8,10},{9,11},{10,... | collective-permute-start | bytes 12296 | tf_op jit(solution)/shard_map/ppermute | solution.py:365
  78.4 4.8 %collective-permute-start.22 = (f32[8,128]{1,0:T(8,128)S(1)}, f32[8,128]{1,0:T(8,128)S(1)}, u32[]{:S(2)}, u32[]{:S(2)}) collective-permute-start(f32[8,128]{1,0:T(8,128)S(1)} %add.20), channel_id=1, source_target_pairs={{0,12},{1,13},{2,14},{3,15},{4,8},{5,9},{6,10},{7,11},{8,4},{9,5},... | collective-permute-start | bytes 12296 | tf_op jit(solution)/shard_map/ppermute | solution.py:365
  79.7 5.1 %collective-permute-start.21 = (f32[8,128]{1,0:T(8,128)S(1)}, f32[8,128]{1,0:T(8,128)S(1)}, u32[]{:S(2)}, u32[]{:S(2)}) collective-permute-start(f32[8,128]{1,0:T(8,128)S(1)} %add.20), channel_id=1, source_target_pairs={{0,8},{1,9},{2,10},{3,11},{4,12},{5,13},{6,14},{7,15},{8,0},{9,1},... | collective-permute-start | bytes 12296 | tf_op jit(solution)/shard_map/ppermute | solution.py:365
  80.2 4.6 %collective-permute-start.20 = (f32[8,128]{1,0:T(8,128)S(1)}, f32[8,128]{1,0:T(8,128)S(1)}, u32[]{:S(2)}, u32[]{:S(2)}) collective-permute-start(f32[8,128]{1,0:T(8,128)S(1)} %add.20), channel_id=1, source_target_pairs={{0,4},{1,5},{2,6},{3,7},{4,0},{5,1},{6,2},{7,3},{8,12},{9,13},{10,... | collective-permute-start | bytes 12296 | tf_op jit(solution)/shard_map/ppermute | solution.py:365

commit v4 on v3

--- a/solution.py
+++ b/solution.py
@@ -60,7 +60,8 @@
     left[rows, nz + h * LANES:nz + (h + 1) * LANES] = (v - hi.astype(jnp.float32)).astype(jnp.bfloat16)
 
 
-def inner_kernel(o, p, mix, e, rho, *scratch):
+def inner_kernel(o, p, mix, e, o_wide, p_wide, rho, *scratch):
+    j = pl.program_id(0)
     g0, g1, g2 = polynomial()
     beta = g2 / g1
     kappa = g0 / g1 + 6.0 * beta
@@ -73,10 +74,19 @@
         for i in range(steps):
             for h in range(halves):
                 ov = at(o, (0, x), i * STRIP, STRIP, h).astype(f32)
+                o_wide[j, x, i * STRIP:(i + 1) * STRIP, h * LANES:(h + 1) * LANES] = ov
                 for a in range(na):
                     rho[a, x, h, PAD + i * STRIP:PAD + (i + 1) * STRIP, :] = at(p, (a, x), i * STRIP, STRIP, h).astype(f32) * ov
         for a in range(na):
             wrap(rho, (a, x), halves, ny, 2)
+
+    @pl.when(j == 0)
+    def _():
+        for a in range(na):
+            for x in range(nx):
+                for i in range(steps):
+                    rows = slice(i * STRIP, (i + 1) * STRIP)
+                    p_wide[a, x, rows, :] = p[a, x, rows, :].astype(f32)
 
     def prepare(x):
         sig, left, base = sigs[x % 2], lefts[x % 2], bases[x % 2]
@@ -130,13 +140,13 @@
     return pl.pallas_call(
         inner_kernel,
         grid=(nj,),
-        out_shape=pltpu.VMEM((nj, nx, ny, nz), f32),
+        out_shape=(pltpu.VMEM((nj, nx, ny, nz), f32), pltpu.VMEM((nj, nx, ny, nz), f32), pltpu.VMEM((na, nx, ny, nz), f32)),
         in_specs=[
             pl.BlockSpec((1, nx, ny, nz), lambda j: (j, 0, 0, 0)),
             pl.BlockSpec(memory_space=pltpu.VMEM),
             pl.BlockSpec(mix.shape, lambda j: (0, 0)),
         ],
-        out_specs=pl.BlockSpec(memory_space=pltpu.VMEM),
+        out_specs=(pl.BlockSpec(memory_space=pltpu.VMEM),) * 3,
         scratch_shapes=[pltpu.VMEM((na, nx, nz // LANES, ny + 2 * PAD, LANES), f32)]
         + [pltpu.VMEM((na, nz // LANES, ny + 2 * PAD, LANES), f32)] * 2
         + [pltpu.VMEM((na, ny, 3 * nz), bf)] * 2
@@ -198,30 +208,38 @@
     finish(*sides[0])
     finish(*sides[1])
 
-    def project(x, acc):
-        acc = list(acc)
-        for i in range(steps):
-            rows = slice(i * STRIP, (i + 1) * STRIP)
-            field = e[0, x, rows, :]
-            for s in range(na + nj):
-                source = p[s, x, rows, :] if s < na else o[s - na, x, rows, :]
-                m = source.astype(f32) * field
-                m = m[:, :128] + m[:, 128:]
-                acc[s] = acc[s] + jnp.sum(m.reshape(STRIP // 8, 8, 128), axis=0)
-        return tuple(acc)
-
-    acc = lax.fori_loop(0, nx, project, tuple(jnp.zeros((8, 128), f32) for _ in range(na + nj)))
-    sums = [jnp.sum(a, axis=0, keepdims=True) for a in acc]
-    tile = jnp.concatenate(sums + [jnp.zeros((8 - na - nj, LANES), f32)], axis=0)
-    share = LANES // nj
-    width = LANES // 2
-    while width >= share:
-        tile = tile + pltpu.roll(tile, width, 1)
-        width //= 2
-    j = pl.program_id(0)
-    lane = lax.broadcasted_iota(jnp.int32, (8, LANES), 1)
-    tile = jnp.where((lane >= j * share) & (lane < (j + 1) * share), tile, jnp.where(j == 0, 0.0, ace[...]))
-    ace[...] = tile
+    def project(residents):
+        sources = [(p, a) for a in range(na)] + [(o, i) for i in range(residents)]
+
+        def one_plane(x, acc):
+            acc = list(acc)
+            for i in range(steps):
+                rows = slice(i * STRIP, (i + 1) * STRIP)
+                field = e[0, x, rows, :]
+                for s, (ref, n) in enumerate(sources):
+                    m = ref[n, x, rows, :].astype(f32) * field
+                    m = m[:, :LANES] + m[:, LANES:]
+                    acc[s] = acc[s] + jnp.sum(m.reshape(STRIP // 8, 8, LANES), axis=0)
+            return tuple(acc)
+
+        acc = lax.fori_loop(0, nx, one_plane, tuple(jnp.zeros((8, LANES), f32) for _ in sources))
+        sums = [jnp.sum(a, axis=0, keepdims=True) for a in acc]
+        tile = jnp.concatenate(sums + [jnp.zeros((8 - len(sums), LANES), f32)], axis=0)
+        share = LANES // nj
+        width = LANES // 2
+        while width >= share:
+            tile = tile + pltpu.roll(tile, width, 1)
+            width //= 2
+        j = residents - 1
+        group = lax.broadcasted_iota(jnp.int32, (8, LANES), 1) // share
+        row = lax.broadcasted_iota(jnp.int32, (8, LANES), 0)
+        out = jnp.where(group == j, tile, jnp.zeros_like(tile) if j == 0 else ace[...])
+        for i in range(j):
+            out = jnp.where((group == i) & (row == na + j), tile[na + i:na + i + 1], out)
+        ace[...] = out
+
+    for j in range(nj):
+        pl.when(pl.program_id(0) == j)(lambda j=j: project(j + 1))
 
 
 def outer(e, o, halo, p, plo, phi):
@@ -236,7 +254,7 @@
         outer_kernel,
         grid=(nj,),
         out_shape=(jax.ShapeDtypeStruct(e.shape, f32), jax.ShapeDtypeStruct((8, LANES), f32)),
-        in_specs=[pl.BlockSpec(memory_space=pltpu.VMEM), whole(o.shape), *[each(h.shape) for h in halo], pl.BlockSpec(memory_space=pltpu.VMEM), whole(plo.shape), whole(phi.shape), whole(mix.shape)],
+        in_specs=[pl.BlockSpec(memory_space=pltpu.VMEM), pl.BlockSpec(memory_space=pltpu.VMEM), *[each(h.shape) for h in halo], pl.BlockSpec(memory_space=pltpu.VMEM), whole(plo.shape), whole(phi.shape), whole(mix.shape)],
         out_specs=(each(e.shape), pl.BlockSpec((8, LANES), lambda j: (0, 0))),
         scratch_shapes=[pltpu.VMEM((na, nz // LANES, ny + 2 * PAD, LANES), f32)] * 2
         + [pltpu.VMEM((na, ny, 2 * nz), bf)] * 2
@@ -391,8 +409,8 @@
     parts = [[m, *[along(m, n) for n in range(1, row)]] for m in mine]
     panel, top, bottom = join(parts[0] + parts[1])
     low, high = up(top), down(bottom)
-    exchange = inner(orbitals, panel)
-    exchange, sums = outer(exchange, orbitals, halo, panel, low, high)
+    exchange, o_wide, p_wide = inner(orbitals, panel)
+    exchange, sums = outer(exchange, o_wide, halo, p_wide, low, high)
     cells = float(nx * slabs * ny * nz)
     ace_block = jnp.sum(total(sums)[:PANEL + nj].reshape(PANEL + nj, nj, -1), axis=2) / cells
     return exchange, ace_block[None]

time: 86.2 us -> 85.4 us (level)
  waiting for transfers between devices: 17.8 us -> 19.6 us
  other arithmetic: 2.01 us -> 0.21 us
  Pallas kernels: 25.2 us -> 24.2 us
    select_n x2, other arithmetic: 1.88 us -> 0.07 us  [local(): mine = [lax.select_n(behind, *g) for g in got]]
    pallas_call x1, Pallas kernels: 8.79 us -> 7.68 us  [outer(): pl.pallas_call(outer_kernel, grid=(nj,), out_shape=(jax.ShapeDtypeStruct(...]
    ppermute x12, starting transfers between devices: 17.3 us -> 18.3 us  [local(): along = lambda v, k: lax.ppermute(v, 'band', rows(k, row))]
    ppermute x5, waiting for transfers between devices: 7.95 us -> 8.93 us  [total(): lax.ppermute(part, 'dom', [(i, i ^ k) for i in range(count)])]
    unnamed x20 -> x18, local copies, waits for them, and re-layouts: 2.27 us -> 2.26 us
  transfers between devices with their start and end apart: 23 -> 23, of which waited for: 11 -> 12; matrix products, arithmetic and copies ran while one was open for 2% -> 0% of each run, Pallas kernels for 17% -> 17%
where the time goes in v4:
time: 85.4 us; the launch traced here: 85.1 us
  starting transfers between devices  36.6 us (43%)
  Pallas kernels  24.2 us (28%)
  waiting for transfers between devices  19.6 us (23%)
  local copies, waits for them, and re-layouts  3.01 us (4%)
  between operations  1.5 us (2%)
    ppermute x12, starting transfers between devices, local(): along = lambda v, k: lax.ppermute(v, 'band', rows(k, row))  18.3 us
    ppermute x2, starting transfers between devices, local(): down = lambda v: lax.ppermute(v, 'dom', ring(lax.axis_size('dom'), -1))  10.7 us
    ppermute x12, waiting for transfers between devices, local(): along = lambda v, k: lax.ppermute(v, 'band', rows(k, row))  10.7 us
    pallas_call x1, Pallas kernels, inner(): pl.pallas_call(inner_kernel, grid=(nj,), out_shape=(pltpu.VMEM((nj, nx, n...  10.3 us
    ppermute x5, waiting for transfers between devices, total(): lax.ppermute(part, 'dom', [(i, i ^ k) for i in range(count)])  8.93 us
    pallas_call x1, Pallas kernels, outer(): pl.pallas_call(outer_kernel, grid=(nj,), out_shape=(jax.ShapeDtypeStruct(...  7.68 us
    ppermute x5, starting transfers between devices, total(): lax.ppermute(part, 'dom', [(i, i ^ k) for i in range(count)])  4.25 us
    ppermute x2, starting transfers between devices, local(): across = lambda v: lax.ppermute(v, 'band', ring(lax.axis_size('band'), row))  3.31 us
  transfers between devices with their start and end apart: 23, of which 12 were waited for; matrix products, arithmetic and copies ran while one was open for 0% of the time, Pallas kernels for 17%

profile of v4, /device:TPU:0, one launch (start us, length us, event | category | flops | bytes accessed | tf_op | source)
XLA Modules:
  0.0 85.1 jit_solution(9004076281591426453)
XLA Ops:
  0.6 0.0 copy-start.1
  0.6 2.1 %cut_panel.1 = (bf16[256,256]{1,0:T(8,128)(2,1)}, bf16[256,256]{1,0:T(8,128)(2,1)}, bf16[256,256]{1,0:T(8,128)(2,1)}, bf16[256,256]{1,0:T(8,128)(2,1)}, bf16[256...) custom-call(bf16[4,4,256,256]{3,2,1,0:T(8,128)(2,1)} %o.1), custom_call_target="tpu_custom_call" | custom-call | tf_op jit(solution)/shard_map/cut_panel/pallas_call | solution.py:292
  2.8 1.6 %collective-permute-start.7 = (bf16[256,256]{1,0:T(8,128)(2,1)}, bf16[256,256]{1,0:T(8,128)(2,1)S(1)}, u32[]{:S(2)}, u32[]{:S(2)}) collective-permute-start(bf16[256,256]{1,0:T(8,128)(2,1)} %get-tuple-element.31), channel_id=1, source_target_pairs={{0,16},{16,32},{32,48},{48,0},{64,80},{80,96},{96,112},{112,64},{1... | collective-permute-start | bytes 393224 | tf_op jit(solution)/shard_map/ppermute | solution.py:399
  4.4 2.7 %collective-permute-start.8 = (bf16[256,256]{1,0:T(8,128)(2,1)}, bf16[256,256]{1,0:T(8,128)(2,1)S(1)}, u32[]{:S(2)}, u32[]{:S(2)}) collective-permute-start(bf16[256,256]{1,0:T(8,128)(2,1)} %get-tuple-element.32), channel_id=1, source_target_pairs={{0,32},{16,48},{32,0},{48,16},{64,96},{80,112},{96,64},{112,80},{1... | collective-permute-start | bytes 393224 | tf_op jit(solution)/shard_map/ppermute | solution.py:399
  7.2 1.4 %collective-permute-start.9 = (bf16[256,256]{1,0:T(8,128)(2,1)}, bf16[256,256]{1,0:T(8,128)(2,1)S(1)}, u32[]{:S(2)}, u32[]{:S(2)}) collective-permute-start(bf16[256,256]{1,0:T(8,128)(2,1)} %get-tuple-element.33), channel_id=1, source_target_pairs={{0,48},{16,0},{32,16},{48,32},{64,112},{80,64},{96,80},{112,96},{1... | collective-permute-start | bytes 393224 | tf_op jit(solution)/shard_map/ppermute | solution.py:399
  8.6 0.6 collective-permute-start
  9.2 0.9 %collective-permute-start.1 = (bf16[256,256]{1,0:T(8,128)(2,1)}, bf16[256,256]{1,0:T(8,128)(2,1)S(1)}, u32[]{:S(2)}, u32[]{:S(2)}) collective-permute-start(bf16[256,256]{1,0:T(8,128)(2,1)} %get-tuple-element.25), channel_id=1, source_target_pairs={{0,32},{16,48},{32,0},{48,16},{64,96},{80,112},{96,64},{112,80},{1... | collective-permute-start | bytes 393224 | tf_op jit(solution)/shard_map/ppermute | solution.py:399
  10.7 2.6 %edge_planes.1 = (bf16[4,2,256,256]{3,2,1,0:T(8,128)(2,1)}, bf16[4,2,256,256]{3,2,1,0:T(8,128)(2,1)}) custom-call(bf16[4,4,256,256]{3,2,1,0:T(8,128)(2,1)} %o.1), custom_call_target="tpu_custom_call" | custom-call | tf_op jit(solution)/shard_map/edge_planes/pallas_call | solution.py:323
  13.4 1.9 %collective-permute-start.2 = (bf16[256,256]{1,0:T(8,128)(2,1)}, bf16[256,256]{1,0:T(8,128)(2,1)S(1)}, u32[]{:S(2)}, u32[]{:S(2)}) collective-permute-start(bf16[256,256]{1,0:T(8,128)(2,1)} %get-tuple-element.26), channel_id=1, source_target_pairs={{0,48},{16,0},{32,16},{48,32},{64,112},{80,64},{96,80},{112,96},{1... | collective-permute-start | bytes 393224 | tf_op jit(solution)/shard_map/ppermute | solution.py:399
  15.2 0.0 collective-permute-done.8
  15.3 1.7 %collective-permute-start.10 = (bf16[256,256]{1,0:T(8,128)(2,1)S(1)}, bf16[256,256]{1,0:T(8,128)(2,1)S(1)}, u32[]{:S(2)}, u32[]{:S(2)}) collective-permute-start(bf16[256,256]{1,0:T(8,128)(2,1)S(1)} %select_select_fusion), channel_id=1, source_target_pairs={{0,64},{16,80},{32,96},{48,112},{64,0},{80,16},{96,32},{112,48},{1... | collective-permute-start | bytes 393224 | tf_op jit(solution)/shard_map/ppermute | solution.py:400
  16.9 0.3 collective-permute-done
  17.2 1.8 %collective-permute-done.1 = bf16[256,256]{1,0:T(8,128)(2,1)S(1)} collective-permute-done((bf16[256,256]{1,0:T(8,128)(2,1)}, bf16[256,256]{1,0:T(8,128)(2,1)S(1)}, u32[]{:S(2)}, u32[]{:S(2)}) %collective-permute-start.1) | collective-permute-done | bytes 131104 | tf_op jit(solution)/shard_map/ppermute | solution.py:399
  19.0 0.2 collective-permute-done.2
  19.3 1.7 %collective-permute-start.3 = (bf16[256,256]{1,0:T(8,128)(2,1)S(1)}, bf16[256,256]{1,0:T(8,128)(2,1)S(1)}, u32[]{:S(2)}, u32[]{:S(2)}) collective-permute-start(bf16[256,256]{1,0:T(8,128)(2,1)S(1)} %select_select_fusion.1), channel_id=1, source_target_pairs={{0,64},{16,80},{32,96},{48,112},{64,0},{80,16},{96,32},{112,48},{1... | collective-permute-start | bytes 393224 | tf_op jit(solution)/shard_map/ppermute | solution.py:400
  20.9 5.4 %collective-permute-start.15 = (bf16[4,2,256,256]{3,2,1,0:T(8,128)(2,1)}, bf16[4,2,256,256]{3,2,1,0:T(8,128)(2,1)}, u32[]{:S(2)}, u32[]{:S(2)}) collective-permute-start(bf16[4,2,256,256]{3,2,1,0:T(8,128)(2,1)} %get-tuple-element.38), channel_id=1, source_target_pairs={{0,15},{1,0},{2,1},{3,2},{4,3},{5,4},{6,5},{7,6},{8,7},{9,8},{10,9... | collective-permute-start | bytes 3145736 | tf_op jit(solution)/shard_map/ppermute | solution.py:398
  26.3 2.5 %collective-permute-start.13 = (bf16[256,256]{1,0:T(8,128)(2,1)S(1)}, bf16[256,256]{1,0:T(8,128)(2,1)S(1)}, u32[]{:S(2)}, u32[]{:S(2)}) collective-permute-start(bf16[256,256]{1,0:T(8,128)(2,1)S(1)} %broadcast_select_fusion.refs_4_), channel_id=1, source_target_pairs={{0,48},{16,0},{32,16},{48,32},{64,112},{80,64},{96,80},{112,96},{1... | collective-permute-start | bytes 393224 | tf_op jit(solution)/shard_map/ppermute | solution.py:399
  28.8 1.7 %collective-permute-start.12 = (bf16[256,256]{1,0:T(8,128)(2,1)S(1)}, bf16[256,256]{1,0:T(8,128)(2,1)S(1)}, u32[]{:S(2)}, u32[]{:S(2)}) collective-permute-start(bf16[256,256]{1,0:T(8,128)(2,1)S(1)} %broadcast_select_fusion.refs_4_), channel_id=1, source_target_pairs={{0,32},{16,48},{32,0},{48,16},{64,96},{80,112},{96,64},{112,80},{1... | collective-permute-start | bytes 393224 | tf_op jit(solution)/shard_map/ppermute | solution.py:399
  30.5 0.6 collective-permute-start.11
  31.2 1.5 %collective-permute-done.13.refs_7_ = bf16[256,256]{1,0:T(8,128)(2,1)S(1)} collective-permute-done((bf16[256,256]{1,0:T(8,128)(2,1)S(1)}, bf16[256,256]{1,0:T(8,128)(2,1)S(1)}, u32[]{:S(2)}, u32[]{:S(2)}) %collective-permute-start.13) | collective-permute-done | bytes 131104 | tf_op jit(solution)/shard_map/ppermute | solution.py:399
  32.7 2.3 %collective-permute-start.6 = (bf16[256,256]{1,0:T(8,128)(2,1)S(1)}, bf16[256,256]{1,0:T(8,128)(2,1)S(1)}, u32[]{:S(2)}, u32[]{:S(2)}) collective-permute-start(bf16[256,256]{1,0:T(8,128)(2,1)S(1)} %broadcast_select_fusion.1.refs_0_), channel_id=1, source_target_pairs={{0,48},{16,0},{32,16},{48,32},{64,112},{80,64},{96,80},{112,96},{1... | collective-permute-start | bytes 393224 | tf_op jit(solution)/shard_map/ppermute | solution.py:399
  35.0 0.2 collective-permute-done.12.refs_6_
  35.3 1.8 %collective-permute-start.5 = (bf16[256,256]{1,0:T(8,128)(2,1)S(1)}, bf16[256,256]{1,0:T(8,128)(2,1)S(1)}, u32[]{:S(2)}, u32[]{:S(2)}) collective-permute-start(bf16[256,256]{1,0:T(8,128)(2,1)S(1)} %broadcast_select_fusion.1.refs_0_), channel_id=1, source_target_pairs={{0,32},{16,48},{32,0},{48,16},{64,96},{80,112},{96,64},{112,80},{1... | collective-permute-start | bytes 393224 | tf_op jit(solution)/shard_map/ppermute | solution.py:399
  37.1 1.1 %collective-permute-done.11.refs_5_ = bf16[256,256]{1,0:T(8,128)(2,1)S(1)} collective-permute-done((bf16[256,256]{1,0:T(8,128)(2,1)S(1)}, bf16[256,256]{1,0:T(8,128)(2,1)S(1)}, u32[]{:S(2)}, u32[]{:S(2)}) %collective-permute-start.11) | collective-permute-done | bytes 131104 | tf_op jit(solution)/shard_map/ppermute | solution.py:399
  38.3 0.1 collective-permute-start.4
  38.4 3.4 %collective-permute-done.5.refs_2_ = bf16[256,256]{1,0:T(8,128)(2,1)S(1)} collective-permute-done((bf16[256,256]{1,0:T(8,128)(2,1)S(1)}, bf16[256,256]{1,0:T(8,128)(2,1)S(1)}, u32[]{:S(2)}, u32[]{:S(2)}) %collective-permute-start.5) | collective-permute-done | bytes 131104 | tf_op jit(solution)/shard_map/ppermute | solution.py:399
  41.8 0.6 copy-done.8
  42.4 2.1 %collective-permute-done.4.refs_1_ = bf16[256,256]{1,0:T(8,128)(2,1)} collective-permute-done((bf16[256,256]{1,0:T(8,128)(2,1)S(1)}, bf16[256,256]{1,0:T(8,128)(2,1)}, u32[]{:S(2)}, u32[]{:S(2)}) %collective-permute-start.4) | collective-permute-done | bytes 131104 | tf_op jit(solution)/shard_map/ppermute | solution.py:399
  44.5 1.4 %join_panel.1 = (bf16[2,4,256,256]{3,2,1,0:T(8,128)(2,1)S(1)}, bf16[2,2,256,256]{3,2,1,0:T(8,128)(2,1)S(1)}, bf16[2,2,256,256]{3,2,1,0:T(8,128)(2,1)S(1)}) custom-call(bf16[256,256]{1,0:T(8,128)(2,1)} %copy-done.3, bf16[256,256]{1,0:T(8,128)(2,1)} %collective-permute-done.4.refs_1_, bf16[256,256]{1,0:T(8,128)(2,1)} %copy-done.8, bf16[256,256]{1,0:T(8,128)(2,1)} %copy-done.7, ...), custom_call_target="tpu_custom_call" | custom-call | tf_op jit(solution)/shard_map/join_panel/pallas_call | solution.py:361
  46.0 0.1 collective-permute-start.16
  46.1 5.3 %collective-permute-start.17 = (bf16[2,2,256,256]{3,2,1,0:T(8,128)(2,1)S(1)}, bf16[2,2,256,256]{3,2,1,0:T(8,128)(2,1)S(1)}, u32[]{:S(2)}, u32[]{:S(2)}) collective-permute-start(bf16[2,2,256,256]{3,2,1,0:T(8,128)(2,1)S(1)} %get-tuple-element.41), channel_id=1, source_target_pairs={{0,15},{1,0},{2,1},{3,2},{4,3},{5,4},{6,5},{7,6},{8,7},{9,8},{10,9... | collective-permute-start | bytes 1572872 | tf_op jit(solution)/shard_map/ppermute | solution.py:398
  51.4 1.6 %copy-done = bf16[4,4,256,256]{3,2,1,0:T(8,128)(2,1)S(1)} copy-done((bf16[4,4,256,256]{3,2,1,0:T(8,128)(2,1)S(1)}, bf16[4,4,256,256]{3,2,1,0:T(8,128)(2,1)}, u32[]{:S(2)}) %copy-start) | copy-done | bytes 2097176
  53.0 10.3 %inner_field.1 = (f32[4,4,256,256]{3,2,1,0:T(8,128)S(1)}, f32[4,4,256,256]{3,2,1,0:T(8,128)S(1)}, f32[2,4,256,256]{3,2,1,0:T(8,128)S(1)}) custom-call(bf16[4,4,256,256]{3,2,1,0:T(8,128)(2,1)S(1)} %copy-done, bf16[2,4,256,256]{3,2,1,0:T(8,128)(2,1)S(1)} %get-tuple-element.34.p, bf16[768,256]{1,0:T(8,128)(2,1)S(1)} %copy-done.1), custom_call_target="tpu_custom_call" | custom-call | flops 6000000000 | bytes 8388608 | tf_op jit(solution)/shard_map/inner_field/pallas_call | solution.py:140
  63.4 0.0 collective-permute-done.16.plo
  63.4 0.0 collective-permute-done.15.halo_high
  63.4 7.7 %outer_field.1 = (f32[4,4,256,256]{3,2,1,0:T(8,128)}, f32[8,128]{1,0:T(8,128)S(1)}) custom-call(f32[4,4,256,256]{3,2,1,0:T(8,128)S(1)} %get-tuple-element.35.e_in, f32[4,4,256,256]{3,2,1,0:T(8,128)S(1)} %get-tuple-element.36.o, bf16[4,2,256,256]{3,2,1,0:T(8,128)(2,1)S(1)} %collective-permute-done.14.halo_low, ...), custom_call_target="tpu_custom_call" | custom-call | flops 3000000000 | bytes 14680064 | tf_op jit(solution)/shard_map/outer_field/pallas_call | solution.py:253
  71.1 0.0 collective-permute-start.18
  71.1 1.2 %collective-permute-done.18 = f32[8,128]{1,0:T(8,128)S(1)} collective-permute-done((f32[8,128]{1,0:T(8,128)S(1)}, f32[8,128]{1,0:T(8,128)S(1)}, u32[]{:S(2)}, u32[]{:S(2)}) %collective-permute-start.18) | collective-permute-done | bytes 4128 | tf_op jit(solution)/shard_map/ppermute | solution.py:383
  72.3 0.2 collective-permute-start.19
  72.4 5.0 %collective-permute-done.19 = f32[8,128]{1,0:T(8,128)S(1)} collective-permute-done((f32[8,128]{1,0:T(8,128)S(1)}, f32[8,128]{1,0:T(8,128)S(1)}, u32[]{:S(2)}, u32[]{:S(2)}) %collective-permute-start.19) | collective-permute-done | bytes 4128 | tf_op jit(solution)/shard_map/ppermute | solution.py:383
  77.4 1.8 %collective-permute-start.22 = (f32[8,128]{1,0:T(8,128)S(1)}, f32[8,128]{1,0:T(8,128)S(1)}, u32[]{:S(2)}, u32[]{:S(2)}) collective-permute-start(f32[8,128]{1,0:T(8,128)S(1)} %add.20), channel_id=1, source_target_pairs={{0,12},{1,13},{2,14},{3,15},{4,8},{5,9},{6,10},{7,11},{8,4},{9,5},... | collective-permute-start | bytes 12296 | tf_op jit(solution)/shard_map/ppermute | solution.py:383
  79.2 0.4 collective-permute-start.21
  79.5 1.9 %collective-permute-start.20 = (f32[8,128]{1,0:T(8,128)S(1)}, f32[8,128]{1,0:T(8,128)S(1)}, u32[]{:S(2)}, u32[]{:S(2)}) collective-permute-start(f32[8,128]{1,0:T(8,128)S(1)} %add.20), channel_id=1, source_target_pairs={{0,4},{1,5},{2,6},{3,7},{4,0},{5,1},{6,2},{7,3},{8,12},{9,13},{10,... | collective-permute-start | bytes 12296 | tf_op jit(solution)/shard_map/ppermute | solution.py:383
  81.5 0.7 collective-permute-done.22
  82.2 2.1 %collective-permute-done.21 = f32[8,128]{1,0:T(8,128)S(1)} collective-permute-done((f32[8,128]{1,0:T(8,128)S(1)}, f32[8,128]{1,0:T(8,128)S(1)}, u32[]{:S(2)}, u32[]{:S(2)}) %collective-permute-start.21) | collective-permute-done | bytes 4128 | tf_op jit(solution)/shard_map/ppermute | solution.py:383
  84.3 0.1 reshape.16
  84.4 0.1 reduce_sum.9
  84.5 0.7 copy.6
  (32 shorter events, 0.2 us)
Async XLA Ops:
  0.6 50.8 %copy-start.1 = (bf16[768,256]{1,0:T(8,128)(2,1)S(1)}, bf16[768,256]{1,0:T(8,128)(2,1)}, u32[]{:S(2)}) copy-start(bf16[768,256]{1,0:T(8,128)(2,1)} %constant.32.mix) | copy-start | bytes 1179652
  2.8 10.6 %collective-permute-start.7 = (bf16[256,256]{1,0:T(8,128)(2,1)}, bf16[256,256]{1,0:T(8,128)(2,1)S(1)}, u32[]{:S(2)}, u32[]{:S(2)}) collective-permute-start(bf16[256,256]{1,0:T(8,128)(2,1)} %get-tuple-element.31), channel_id=1, source_target_pairs={{0,16},{16,32},{32,48},{48,0},{64,80},{80,96},{96,112},{112,64},{1... | collective-permute-start | bytes 393224 | tf_op jit(solution)/shard_map/ppermute | solution.py:399
  4.4 10.8 %collective-permute-start.8 = (bf16[256,256]{1,0:T(8,128)(2,1)}, bf16[256,256]{1,0:T(8,128)(2,1)S(1)}, u32[]{:S(2)}, u32[]{:S(2)}) collective-permute-start(bf16[256,256]{1,0:T(8,128)(2,1)} %get-tuple-element.32), channel_id=1, source_target_pairs={{0,32},{16,48},{32,0},{48,16},{64,96},{80,112},{96,64},{112,80},{1... | collective-permute-start | bytes 393224 | tf_op jit(solution)/shard_map/ppermute | solution.py:399
  7.2 8.1 %collective-permute-start.9 = (bf16[256,256]{1,0:T(8,128)(2,1)}, bf16[256,256]{1,0:T(8,128)(2,1)S(1)}, u32[]{:S(2)}, u32[]{:S(2)}) collective-permute-start(bf16[256,256]{1,0:T(8,128)(2,1)} %get-tuple-element.33), channel_id=1, source_target_pairs={{0,48},{16,0},{32,16},{48,32},{64,112},{80,64},{96,80},{112,96},{1... | collective-permute-start | bytes 393224 | tf_op jit(solution)/shard_map/ppermute | solution.py:399
  8.6 8.6 %collective-permute-start = (bf16[256,256]{1,0:T(8,128)(2,1)}, bf16[256,256]{1,0:T(8,128)(2,1)S(1)}, u32[]{:S(2)}, u32[]{:S(2)}) collective-permute-start(bf16[256,256]{1,0:T(8,128)(2,1)} %get-tuple-element.24), channel_id=1, source_target_pairs={{0,16},{16,32},{32,48},{48,0},{64,80},{80,96},{96,112},{112,64},{1... | collective-permute-start | bytes 393224 | tf_op jit(solution)/shard_map/ppermute | solution.py:399
  9.2 9.8 %collective-permute-start.1 = (bf16[256,256]{1,0:T(8,128)(2,1)}, bf16[256,256]{1,0:T(8,128)(2,1)S(1)}, u32[]{:S(2)}, u32[]{:S(2)}) collective-permute-start(bf16[256,256]{1,0:T(8,128)(2,1)} %get-tuple-element.25), channel_id=1, source_target_pairs={{0,32},{16,48},{32,0},{48,16},{64,96},{80,112},{96,64},{112,80},{1... | collective-permute-start | bytes 393224 | tf_op jit(solution)/shard_map/ppermute | solution.py:399
  13.4 5.9 %collective-permute-start.2 = (bf16[256,256]{1,0:T(8,128)(2,1)}, bf16[256,256]{1,0:T(8,128)(2,1)S(1)}, u32[]{:S(2)}, u32[]{:S(2)}) collective-permute-start(bf16[256,256]{1,0:T(8,128)(2,1)} %get-tuple-element.26), channel_id=1, source_target_pairs={{0,48},{16,0},{32,16},{48,32},{64,112},{80,64},{96,80},{112,96},{1... | collective-permute-start | bytes 393224 | tf_op jit(solution)/shard_map/ppermute | solution.py:399
  15.3 11.0 %collective-permute-start.10 = (bf16[256,256]{1,0:T(8,128)(2,1)S(1)}, bf16[256,256]{1,0:T(8,128)(2,1)S(1)}, u32[]{:S(2)}, u32[]{:S(2)}) collective-permute-start(bf16[256,256]{1,0:T(8,128)(2,1)S(1)} %select_select_fusion), channel_id=1, source_target_pairs={{0,64},{16,80},{32,96},{48,112},{64,0},{80,16},{96,32},{112,48},{1... | collective-permute-start | bytes 393224 | tf_op jit(solution)/shard_map/ppermute | solution.py:400
  19.3 11.3 %collective-permute-start.3 = (bf16[256,256]{1,0:T(8,128)(2,1)S(1)}, bf16[256,256]{1,0:T(8,128)(2,1)S(1)}, u32[]{:S(2)}, u32[]{:S(2)}) collective-permute-start(bf16[256,256]{1,0:T(8,128)(2,1)S(1)} %select_select_fusion.1), channel_id=1, source_target_pairs={{0,64},{16,80},{32,96},{48,112},{64,0},{80,16},{96,32},{112,48},{1... | collective-permute-start | bytes 393224 | tf_op jit(solution)/shard_map/ppermute | solution.py:400
  20.9 42.5 %collective-permute-start.14 = (bf16[4,2,256,256]{3,2,1,0:T(8,128)(2,1)}, bf16[4,2,256,256]{3,2,1,0:T(8,128)(2,1)S(1)}, u32[]{:S(2)}, u32[]{:S(2)}) collective-permute-start(bf16[4,2,256,256]{3,2,1,0:T(8,128)(2,1)} %get-tuple-element.37), channel_id=1, source_target_pairs={{0,1},{1,2},{2,3},{3,4},{4,5},{5,6},{6,7},{7,8},{8,9},{9,10},{10,1... | collective-permute-start | bytes 3145736 | tf_op jit(solution)/shard_map/ppermute | solution.py:397
  20.9 42.5 %collective-permute-start.15 = (bf16[4,2,256,256]{3,2,1,0:T(8,128)(2,1)}, bf16[4,2,256,256]{3,2,1,0:T(8,128)(2,1)}, u32[]{:S(2)}, u32[]{:S(2)}) collective-permute-start(bf16[4,2,256,256]{3,2,1,0:T(8,128)(2,1)} %get-tuple-element.38), channel_id=1, source_target_pairs={{0,15},{1,0},{2,1},{3,2},{4,3},{5,4},{6,5},{7,6},{8,7},{9,8},{10,9... | collective-permute-start | bytes 3145736 | tf_op jit(solution)/shard_map/ppermute | solution.py:398
  26.3 15.4 %copy-start.2 = (bf16[256,256]{1,0:T(8,128)(2,1)}, bf16[256,256]{1,0:T(8,128)(2,1)S(1)}, u32[]{:S(2)}) copy-start(bf16[256,256]{1,0:T(8,128)(2,1)S(1)} %broadcast_select_fusion.refs_4_) | copy-start | bytes 393220
  26.3 6.4 %collective-permute-start.13 = (bf16[256,256]{1,0:T(8,128)(2,1)S(1)}, bf16[256,256]{1,0:T(8,128)(2,1)S(1)}, u32[]{:S(2)}, u32[]{:S(2)}) collective-permute-start(bf16[256,256]{1,0:T(8,128)(2,1)S(1)} %broadcast_select_fusion.refs_4_), channel_id=1, source_target_pairs={{0,48},{16,0},{32,16},{48,32},{64,112},{80,64},{96,80},{112,96},{1... | collective-permute-start | bytes 393224 | tf_op jit(solution)/shard_map/ppermute | solution.py:399
  28.8 6.5 %collective-permute-start.12 = (bf16[256,256]{1,0:T(8,128)(2,1)S(1)}, bf16[256,256]{1,0:T(8,128)(2,1)S(1)}, u32[]{:S(2)}, u32[]{:S(2)}) collective-permute-start(bf16[256,256]{1,0:T(8,128)(2,1)S(1)} %broadcast_select_fusion.refs_4_), channel_id=1, source_target_pairs={{0,32},{16,48},{32,0},{48,16},{64,96},{80,112},{96,64},{112,80},{1... | collective-permute-start | bytes 393224 | tf_op jit(solution)/shard_map/ppermute | solution.py:399
  30.5 7.7 %collective-permute-start.11 = (bf16[256,256]{1,0:T(8,128)(2,1)S(1)}, bf16[256,256]{1,0:T(8,128)(2,1)S(1)}, u32[]{:S(2)}, u32[]{:S(2)}) collective-permute-start(bf16[256,256]{1,0:T(8,128)(2,1)S(1)} %broadcast_select_fusion.refs_4_), channel_id=1, source_target_pairs={{0,16},{16,32},{32,48},{48,0},{64,80},{80,96},{96,112},{112,64},{1... | collective-permute-start | bytes 393224 | tf_op jit(solution)/shard_map/ppermute | solution.py:399
  31.2 10.6 %copy-start.3 = (bf16[256,256]{1,0:T(8,128)(2,1)}, bf16[256,256]{1,0:T(8,128)(2,1)S(1)}, u32[]{:S(2)}) copy-start(bf16[256,256]{1,0:T(8,128)(2,1)S(1)} %broadcast_select_fusion.1.refs_0_) | copy-start | bytes 393220
  32.7 9.0 %copy-start.4 = (bf16[256,256]{1,0:T(8,128)(2,1)}, bf16[256,256]{1,0:T(8,128)(2,1)S(1)}, u32[]{:S(2)}) copy-start(bf16[256,256]{1,0:T(8,128)(2,1)S(1)} %collective-permute-done.13.refs_7_) | copy-start | bytes 393220
  32.7 5.6 %collective-permute-start.6 = (bf16[256,256]{1,0:T(8,128)(2,1)S(1)}, bf16[256,256]{1,0:T(8,128)(2,1)S(1)}, u32[]{:S(2)}, u32[]{:S(2)}) collective-permute-start(bf16[256,256]{1,0:T(8,128)(2,1)S(1)} %broadcast_select_fusion.1.refs_0_), channel_id=1, source_target_pairs={{0,48},{16,0},{32,16},{48,32},{64,112},{80,64},{96,80},{112,96},{1... | collective-permute-start | bytes 393224 | tf_op jit(solution)/shard_map/ppermute | solution.py:399
  35.3 6.5 %copy-start.5 = (bf16[256,256]{1,0:T(8,128)(2,1)}, bf16[256,256]{1,0:T(8,128)(2,1)S(1)}, u32[]{:S(2)}) copy-start(bf16[256,256]{1,0:T(8,128)(2,1)S(1)} %collective-permute-done.12.refs_6_) | copy-start | bytes 393220
  35.3 6.5 %collective-permute-start.5 = (bf16[256,256]{1,0:T(8,128)(2,1)S(1)}, bf16[256,256]{1,0:T(8,128)(2,1)S(1)}, u32[]{:S(2)}, u32[]{:S(2)}) collective-permute-start(bf16[256,256]{1,0:T(8,128)(2,1)S(1)} %broadcast_select_fusion.1.refs_0_), channel_id=1, source_target_pairs={{0,32},{16,48},{32,0},{48,16},{64,96},{80,112},{96,64},{112,80},{1... | collective-permute-start | bytes 393224 | tf_op jit(solution)/shard_map/ppermute | solution.py:399
  38.3 3.5 %copy-start.6 = (bf16[256,256]{1,0:T(8,128)(2,1)}, bf16[256,256]{1,0:T(8,128)(2,1)S(1)}, u32[]{:S(2)}) copy-start(bf16[256,256]{1,0:T(8,128)(2,1)S(1)} %collective-permute-done.11.refs_5_) | copy-start | bytes 393220
  38.3 6.3 %collective-permute-start.4 = (bf16[256,256]{1,0:T(8,128)(2,1)S(1)}, bf16[256,256]{1,0:T(8,128)(2,1)}, u32[]{:S(2)}, u32[]{:S(2)}) collective-permute-start(bf16[256,256]{1,0:T(8,128)(2,1)S(1)} %broadcast_select_fusion.1.refs_0_), channel_id=1, source_target_pairs={{0,16},{16,32},{32,48},{48,0},{64,80},{80,96},{96,112},{112,64},{1... | collective-permute-start | bytes 393224 | tf_op jit(solution)/shard_map/ppermute | solution.py:399
  38.4 3.4 %copy-start.7 = (bf16[256,256]{1,0:T(8,128)(2,1)}, bf16[256,256]{1,0:T(8,128)(2,1)S(1)}, u32[]{:S(2)}) copy-start(bf16[256,256]{1,0:T(8,128)(2,1)S(1)} %collective-permute-done.6.refs_3_) | copy-start | bytes 393220
  41.8 0.7 copy-start.8
  46.0 17.4 %collective-permute-start.16 = (bf16[2,2,256,256]{3,2,1,0:T(8,128)(2,1)S(1)}, bf16[2,2,256,256]{3,2,1,0:T(8,128)(2,1)S(1)}, u32[]{:S(2)}, u32[]{:S(2)}) collective-permute-start(bf16[2,2,256,256]{3,2,1,0:T(8,128)(2,1)S(1)} %get-tuple-element.40), channel_id=1, source_target_pairs={{0,1},{1,2},{2,3},{3,4},{4,5},{5,6},{6,7},{7,8},{8,9},{9,10},{10,1... | collective-permute-start | bytes 1572872 | tf_op jit(solution)/shard_map/ppermute | solution.py:397
  46.1 17.3 %collective-permute-start.17 = (bf16[2,2,256,256]{3,2,1,0:T(8,128)(2,1)S(1)}, bf16[2,2,256,256]{3,2,1,0:T(8,128)(2,1)S(1)}, u32[]{:S(2)}, u32[]{:S(2)}) collective-permute-start(bf16[2,2,256,256]{3,2,1,0:T(8,128)(2,1)S(1)} %get-tuple-element.41), channel_id=1, source_target_pairs={{0,15},{1,0},{2,1},{3,2},{4,3},{5,4},{6,5},{7,6},{8,7},{9,8},{10,9... | collective-permute-start | bytes 1572872 | tf_op jit(solution)/shard_map/ppermute | solution.py:398
  51.4 1.6 %copy-start = (bf16[4,4,256,256]{3,2,1,0:T(8,128)(2,1)S(1)}, bf16[4,4,256,256]{3,2,1,0:T(8,128)(2,1)}, u32[]{:S(2)}) copy-start(bf16[4,4,256,256]{3,2,1,0:T(8,128)(2,1)} %o.1) | copy-start | bytes 6291460
  71.1 1.2 %collective-permute-start.18 = (f32[8,128]{1,0:T(8,128)S(1)}, f32[8,128]{1,0:T(8,128)S(1)}, u32[]{:S(2)}, u32[]{:S(2)}) collective-permute-start(f32[8,128]{1,0:T(8,128)S(1)} %get-tuple-element.43), channel_id=1, source_target_pairs={{0,1},{1,0},{2,3},{3,2},{4,5},{5,4},{6,7},{7,6},{8,9},{9,8},{10,11... | collective-permute-start | bytes 12296 | tf_op jit(solution)/shard_map/ppermute | solution.py:383
  72.3 5.1 %collective-permute-start.19 = (f32[8,128]{1,0:T(8,128)S(1)}, f32[8,128]{1,0:T(8,128)S(1)}, u32[]{:S(2)}, u32[]{:S(2)}) collective-permute-start(f32[8,128]{1,0:T(8,128)S(1)} %add.19), channel_id=1, source_target_pairs={{0,2},{1,3},{2,0},{3,1},{4,6},{5,7},{6,4},{7,5},{8,10},{9,11},{10,... | collective-permute-start | bytes 12296 | tf_op jit(solution)/shard_map/ppermute | solution.py:383
  77.4 4.8 %collective-permute-start.22 = (f32[8,128]{1,0:T(8,128)S(1)}, f32[8,128]{1,0:T(8,128)S(1)}, u32[]{:S(2)}, u32[]{:S(2)}) collective-permute-start(f32[8,128]{1,0:T(8,128)S(1)} %add.20), channel_id=1, source_target_pairs={{0,12},{1,13},{2,14},{3,15},{4,8},{5,9},{6,10},{7,11},{8,4},{9,5},... | collective-permute-start | bytes 12296 | tf_op jit(solution)/shard_map/ppermute | solution.py:383
  79.2 5.1 %collective-permute-start.21 = (f32[8,128]{1,0:T(8,128)S(1)}, f32[8,128]{1,0:T(8,128)S(1)}, u32[]{:S(2)}, u32[]{:S(2)}) collective-permute-start(f32[8,128]{1,0:T(8,128)S(1)} %add.20), channel_id=1, source_target_pairs={{0,8},{1,9},{2,10},{3,11},{4,12},{5,13},{6,14},{7,15},{8,0},{9,1},... | collective-permute-start | bytes 12296 | tf_op jit(solution)/shard_map/ppermute | solution.py:383
  79.5 4.7 %collective-permute-start.20 = (f32[8,128]{1,0:T(8,128)S(1)}, f32[8,128]{1,0:T(8,128)S(1)}, u32[]{:S(2)}, u32[]{:S(2)}) collective-permute-start(f32[8,128]{1,0:T(8,128)S(1)} %add.20), channel_id=1, source_target_pairs={{0,4},{1,5},{2,6},{3,7},{4,0},{5,1},{6,2},{7,3},{8,12},{9,13},{10,... | collective-permute-start | bytes 12296 | tf_op jit(solution)/shard_map/ppermute | solution.py:383

commit v5 on v4

--- a/solution.py
+++ b/solution.py
@@ -254,7 +254,7 @@
         outer_kernel,
         grid=(nj,),
         out_shape=(jax.ShapeDtypeStruct(e.shape, f32), jax.ShapeDtypeStruct((8, LANES), f32)),
-        in_specs=[pl.BlockSpec(memory_space=pltpu.VMEM), pl.BlockSpec(memory_space=pltpu.VMEM), *[each(h.shape) for h in halo], pl.BlockSpec(memory_space=pltpu.VMEM), whole(plo.shape), whole(phi.shape), whole(mix.shape)],
+        in_specs=[pl.BlockSpec(memory_space=pltpu.VMEM), pl.BlockSpec(memory_space=pltpu.VMEM), *[each(h.shape) for h in halo], pl.BlockSpec(memory_space=pltpu.VMEM), whole(plo.shape), whole(phi.shape), pl.BlockSpec(memory_space=pltpu.VMEM)],
         out_specs=(each(e.shape), pl.BlockSpec((8, LANES), lambda j: (0, 0))),
         scratch_shapes=[pltpu.VMEM((na, nz // LANES, ny + 2 * PAD, LANES), f32)] * 2
         + [pltpu.VMEM((na, ny, 2 * nz), bf)] * 2
@@ -331,13 +331,9 @@
 
 
 def join_kernel(row, *refs):
-    parts, (panel, top, bottom, loaded, stored) = refs[:PANEL * row], refs[PANEL * row:]
+    parts, (panel, top, bottom, loaded, stored) = refs[:row], refs[row:]
     x = lax.rem(lax.axis_index("band"), row)
-    loads = [
-        pltpu.make_async_copy(parts[a * row + k], panel.at[a, lax.rem(x + row - k, row)], loaded.at[a * row + k])
-        for a in range(PANEL)
-        for k in range(row)
-    ]
+    loads = [pltpu.make_async_copy(parts[k], panel.at[:, lax.rem(x + row - k, row)], loaded.at[k]) for k in range(row)]
     stores = [
         pltpu.make_async_copy(panel.at[:, row - 2:], top, stored.at[0]),
         pltpu.make_async_copy(panel.at[:, :2], bottom, stored.at[1]),
@@ -353,17 +349,17 @@
 
 
 def join(parts):
-    row = len(parts) // PANEL
-    ny, nz = parts[0].shape
+    row = len(parts)
+    _, ny, nz = parts[0].shape
     dtype = parts[0].dtype
     hbm = pl.BlockSpec(memory_space=pl.ANY)
     edge = pltpu.VMEM((PANEL, 2, ny, nz), dtype)
     return pl.pallas_call(
         lambda *refs: join_kernel(row, *refs),
         out_shape=(pltpu.VMEM((PANEL, row, ny, nz), dtype), edge, edge),
-        in_specs=[hbm] * (PANEL * row),
+        in_specs=[hbm] * row,
         out_specs=(pl.BlockSpec(memory_space=pltpu.VMEM),) * 3,
-        scratch_shapes=[pltpu.SemaphoreType.DMA((PANEL * row,)), pltpu.SemaphoreType.DMA((2,))],
+        scratch_shapes=[pltpu.SemaphoreType.DMA((row,)), pltpu.SemaphoreType.DMA((2,))],
         name="join_panel",
     )(*parts)
 
@@ -405,9 +401,9 @@
     mine = [lax.select_n(behind, *g) for g in got]
     mine[0], o_top, o_bottom = lax.optimization_barrier((mine[0], o_top, o_bottom))
     halo = (up(o_top), down(o_bottom))
-    mine = [jnp.where(same, m, across(m)) for m in mine]
-    parts = [[m, *[along(m, n) for n in range(1, row)]] for m in mine]
-    panel, top, bottom = join(parts[0] + parts[1])
+    other = [across(m) for m in mine]
+    both = jnp.where(same, jnp.stack(mine), jnp.stack(other))
+    panel, top, bottom = join([both] + [along(both, n) for n in range(1, row)])
     low, high = up(top), down(bottom)
     exchange, o_wide, p_wide = inner(orbitals, panel)
     exchange, sums = outer(exchange, o_wide, halo, p_wide, low, high)

time: 85.4 us -> 84.3 us (0.987)
  starting transfers between devices: 36.6 us -> 33.8 us
  other arithmetic: 0.21 us -> 2.01 us
    ppermute x12 -> x9, starting transfers between devices: 18.3 us -> 12.5 us  [local(): along = lambda v, k: lax.ppermute(v, 'band', rows(k, row))]
    ppermute x5, starting transfers between devices: 4.25 us -> 7.25 us  [total(): lax.ppermute(part, 'dom', [(i, i ^ k) for i in range(count)])]
    ppermute x5, waiting for transfers between devices: 8.93 us -> 7.1 us  [total(): lax.ppermute(part, 'dom', [(i, i ^ k) for i in range(count)])]
    select_n x2, other arithmetic: 0.07 us -> 1.86 us  [local(): mine = [lax.select_n(behind, *g) for g in got]]
    ppermute x12 -> x9, waiting for transfers between devices: 10.7 us -> 11.7 us  [local(): along = lambda v, k: lax.ppermute(v, 'band', rows(k, row))]
    unnamed x18 -> x10, local copies, waits for them, and re-layouts: 2.26 us -> 2.33 us
  transfers between devices with their start and end apart: 23 -> 20, of which waited for: 12 -> 10; matrix products, arithmetic and copies ran while one was open for 0% -> 2% of each run, Pallas kernels for 17% -> 17%
where the time goes in v5:
time: 84.3 us; the launch traced here: 84 us
  starting transfers between devices  33.8 us (40%)
  Pallas kernels  24.1 us (29%)
  waiting for transfers between devices  19.6 us (23%)
  local copies, waits for them, and re-layouts  3.08 us (4%)
  other arithmetic  2.01 us (2%)
  between operations  1.41 us (2%)
    ppermute x9, starting transfers between devices, local(): along = lambda v, k: lax.ppermute(v, 'band', rows(k, row))  12.5 us
    ppermute x9, waiting for transfers between devices, local(): along = lambda v, k: lax.ppermute(v, 'band', rows(k, row))  11.7 us
    ppermute x2, starting transfers between devices, local(): down = lambda v: lax.ppermute(v, 'dom', ring(lax.axis_size('dom'), -1))  10.7 us
    pallas_call x1, Pallas kernels, inner(): pl.pallas_call(inner_kernel, grid=(nj,), out_shape=(pltpu.VMEM((nj, nx, n...  10.4 us
    pallas_call x1, Pallas kernels, outer(): pl.pallas_call(outer_kernel, grid=(nj,), out_shape=(jax.ShapeDtypeStruct(...  7.69 us
    ppermute x5, starting transfers between devices, total(): lax.ppermute(part, 'dom', [(i, i ^ k) for i in range(count)])  7.25 us
    ppermute x5, waiting for transfers between devices, total(): lax.ppermute(part, 'dom', [(i, i ^ k) for i in range(count)])  7.1 us
    ppermute x2, starting transfers between devices, local(): across = lambda v: lax.ppermute(v, 'band', ring(lax.axis_size('band'), row))  3.31 us
  transfers between devices with their start and end apart: 20, of which 10 were waited for; matrix products, arithmetic and copies ran while one was open for 2% of the time, Pallas kernels for 17%

profile of v5, /device:TPU:0, one launch (start us, length us, event | category | flops | bytes accessed | tf_op | source)
XLA Modules:
  0.0 84.0 jit_solution(13221430341966366616)
XLA Ops:
  0.6 0.0 copy-start.1
  0.6 2.1 %cut_panel.1 = (bf16[256,256]{1,0:T(8,128)(2,1)}, bf16[256,256]{1,0:T(8,128)(2,1)}, bf16[256,256]{1,0:T(8,128)(2,1)}, bf16[256,256]{1,0:T(8,128)(2,1)}, bf16[256...) custom-call(bf16[4,4,256,256]{3,2,1,0:T(8,128)(2,1)} %o.1), custom_call_target="tpu_custom_call" | custom-call | tf_op jit(solution)/shard_map/cut_panel/pallas_call | solution.py:292
  2.8 1.6 %collective-permute-start.3 = (bf16[256,256]{1,0:T(8,128)(2,1)}, bf16[256,256]{1,0:T(8,128)(2,1)S(1)}, u32[]{:S(2)}, u32[]{:S(2)}) collective-permute-start(bf16[256,256]{1,0:T(8,128)(2,1)} %get-tuple-element.31), channel_id=1, source_target_pairs={{0,16},{16,32},{32,48},{48,0},{64,80},{80,96},{96,112},{112,64},{1... | collective-permute-start | bytes 393224 | tf_op jit(solution)/shard_map/ppermute | solution.py:395
  4.4 2.7 %collective-permute-start.4 = (bf16[256,256]{1,0:T(8,128)(2,1)}, bf16[256,256]{1,0:T(8,128)(2,1)S(1)}, u32[]{:S(2)}, u32[]{:S(2)}) collective-permute-start(bf16[256,256]{1,0:T(8,128)(2,1)} %get-tuple-element.32), channel_id=1, source_target_pairs={{0,32},{16,48},{32,0},{48,16},{64,96},{80,112},{96,64},{112,80},{1... | collective-permute-start | bytes 393224 | tf_op jit(solution)/shard_map/ppermute | solution.py:395
  7.2 1.4 %collective-permute-start.5 = (bf16[256,256]{1,0:T(8,128)(2,1)}, bf16[256,256]{1,0:T(8,128)(2,1)S(1)}, u32[]{:S(2)}, u32[]{:S(2)}) collective-permute-start(bf16[256,256]{1,0:T(8,128)(2,1)} %get-tuple-element.33), channel_id=1, source_target_pairs={{0,48},{16,0},{32,16},{48,32},{64,112},{80,64},{96,80},{112,96},{1... | collective-permute-start | bytes 393224 | tf_op jit(solution)/shard_map/ppermute | solution.py:395
  8.6 0.6 collective-permute-start
  9.2 0.9 %collective-permute-start.1 = (bf16[256,256]{1,0:T(8,128)(2,1)}, bf16[256,256]{1,0:T(8,128)(2,1)S(1)}, u32[]{:S(2)}, u32[]{:S(2)}) collective-permute-start(bf16[256,256]{1,0:T(8,128)(2,1)} %get-tuple-element.25), channel_id=1, source_target_pairs={{0,32},{16,48},{32,0},{48,16},{64,96},{80,112},{96,64},{112,80},{1... | collective-permute-start | bytes 393224 | tf_op jit(solution)/shard_map/ppermute | solution.py:395
  10.7 2.6 %edge_planes.1 = (bf16[4,2,256,256]{3,2,1,0:T(8,128)(2,1)}, bf16[4,2,256,256]{3,2,1,0:T(8,128)(2,1)}) custom-call(bf16[4,4,256,256]{3,2,1,0:T(8,128)(2,1)} %o.1), custom_call_target="tpu_custom_call" | custom-call | tf_op jit(solution)/shard_map/edge_planes/pallas_call | solution.py:323
  13.4 0.0 collective-permute-done.3
  13.4 1.9 %collective-permute-start.2 = (bf16[256,256]{1,0:T(8,128)(2,1)}, bf16[256,256]{1,0:T(8,128)(2,1)S(1)}, u32[]{:S(2)}, u32[]{:S(2)}) collective-permute-start(bf16[256,256]{1,0:T(8,128)(2,1)} %get-tuple-element.26), channel_id=1, source_target_pairs={{0,48},{16,0},{32,16},{48,32},{64,112},{80,64},{96,80},{112,96},{1... | collective-permute-start | bytes 393224 | tf_op jit(solution)/shard_map/ppermute | solution.py:395
  15.2 0.0 collective-permute-done.4
  15.2 0.0 collective-permute-done.5
  15.2 0.9 %select_select_fusion = bf16[256,256]{1,0:T(8,128)(2,1)S(1)} fusion(bf16[256,256]{1,0:T(8,128)(2,1)S(1)} %collective-permute-done.4, bf16[256,256]{1,0:T(8,128)(2,1)S(1)} %collective-permute-done.5, bf16[256,256]{1,0:T(8,128)(2,1)} %get-tuple-element.30, bf16[256,256]{1,0:T(8,128)(2,1)S(1)} %collective-permute-done.3, pred[]{:T(512)S(6)} %select_n.56, ...), kind=kLoop, calls=%fused_computation.1 | loop fusion | flops 196608 | bytes 655363 | tf_op jit(solution)/shard_map/select_n | solution.py:401
  16.2 1.7 %collective-permute-start.7 = (bf16[256,256]{1,0:T(8,128)(2,1)S(1)}, bf16[256,256]{1,0:T(8,128)(2,1)S(1)}, u32[]{:S(2)}, u32[]{:S(2)}) collective-permute-start(bf16[256,256]{1,0:T(8,128)(2,1)S(1)} %select_select_fusion), channel_id=1, source_target_pairs={{0,64},{16,80},{32,96},{48,112},{64,0},{80,16},{96,32},{112,48},{1... | collective-permute-start | bytes 393224 | tf_op jit(solution)/shard_map/ppermute | solution.py:396
  17.8 0.0 collective-permute-done
  17.8 1.2 %collective-permute-done.1 = bf16[256,256]{1,0:T(8,128)(2,1)S(1)} collective-permute-done((bf16[256,256]{1,0:T(8,128)(2,1)}, bf16[256,256]{1,0:T(8,128)(2,1)S(1)}, u32[]{:S(2)}, u32[]{:S(2)}) %collective-permute-start.1) | collective-permute-done | bytes 131104 | tf_op jit(solution)/shard_map/ppermute | solution.py:395
  19.0 0.2 collective-permute-done.2
  19.2 0.9 %select_select_fusion.1 = bf16[256,256]{1,0:T(8,128)(2,1)S(1)} fusion(bf16[256,256]{1,0:T(8,128)(2,1)S(1)} %collective-permute-done.1, bf16[256,256]{1,0:T(8,128)(2,1)S(1)} %collective-permute-done.2, bf16[256,256]{1,0:T(8,128)(2,1)} %get-tuple-element.23, bf16[256,256]{1,0:T(8,128)(2,1)S(1)} %collective-permute-done, pred[]{:T(512)S(6)} %select_n.56, ...), kind=kLoop, calls=%fused_computation.2 | loop fusion | flops 196608 | bytes 655363 | tf_op jit(solution)/shard_map/select_n | solution.py:401
  20.2 1.7 %collective-permute-start.6 = (bf16[256,256]{1,0:T(8,128)(2,1)S(1)}, bf16[256,256]{1,0:T(8,128)(2,1)S(1)}, u32[]{:S(2)}, u32[]{:S(2)}) collective-permute-start(bf16[256,256]{1,0:T(8,128)(2,1)S(1)} %select_select_fusion.1), channel_id=1, source_target_pairs={{0,64},{16,80},{32,96},{48,112},{64,0},{80,16},{96,32},{112,48},{1... | collective-permute-start | bytes 393224 | tf_op jit(solution)/shard_map/ppermute | solution.py:396
  21.8 0.0 collective-permute-start.11
  21.8 5.4 %collective-permute-start.12 = (bf16[4,2,256,256]{3,2,1,0:T(8,128)(2,1)}, bf16[4,2,256,256]{3,2,1,0:T(8,128)(2,1)}, u32[]{:S(2)}, u32[]{:S(2)}) collective-permute-start(bf16[4,2,256,256]{3,2,1,0:T(8,128)(2,1)} %get-tuple-element.38), channel_id=1, source_target_pairs={{0,15},{1,0},{2,1},{3,2},{4,3},{5,4},{6,5},{7,6},{8,7},{9,8},{10,9... | collective-permute-start | bytes 3145736 | tf_op jit(solution)/shard_map/ppermute | solution.py:394
  27.2 0.0 collective-permute-done.6
  27.2 1.6 %collective-permute-start.10 = (bf16[2,256,256]{2,1,0:T(8,128)(2,1)S(1)}, bf16[2,256,256]{2,1,0:T(8,128)(2,1)S(1)}, u32[]{:S(2)}, u32[]{:S(2)}) collective-permute-start(bf16[2,256,256]{2,1,0:T(8,128)(2,1)S(1)} %maximum_select_fusion.refs_0_), channel_id=1, source_target_pairs={{0,48},{16,0},{32,16},{48,32},{64,112},{80,64},{96,80},{112,96},{1... | collective-permute-start | bytes 786440 | tf_op jit(solution)/shard_map/ppermute | solution.py:395
  28.8 1.7 %collective-permute-start.9 = (bf16[2,256,256]{2,1,0:T(8,128)(2,1)S(1)}, bf16[2,256,256]{2,1,0:T(8,128)(2,1)S(1)}, u32[]{:S(2)}, u32[]{:S(2)}) collective-permute-start(bf16[2,256,256]{2,1,0:T(8,128)(2,1)S(1)} %maximum_select_fusion.refs_0_), channel_id=1, source_target_pairs={{0,32},{16,48},{32,0},{48,16},{64,96},{80,112},{96,64},{112,80},{1... | collective-permute-start | bytes 786440 | tf_op jit(solution)/shard_map/ppermute | solution.py:395
  30.6 0.0 collective-permute-start.8
  30.6 5.4 %collective-permute-done.10.refs_3_ = bf16[2,256,256]{2,1,0:T(8,128)(2,1)S(1)} collective-permute-done((bf16[2,256,256]{2,1,0:T(8,128)(2,1)S(1)}, bf16[2,256,256]{2,1,0:T(8,128)(2,1)S(1)}, u32[]{:S(2)}, u32[]{:S(2)}) %collective-permute-start.10) | collective-permute-done | bytes 262176 | tf_op jit(solution)/shard_map/ppermute | solution.py:395
  36.0 2.8 %collective-permute-done.9.refs_2_ = bf16[2,256,256]{2,1,0:T(8,128)(2,1)S(1)} collective-permute-done((bf16[2,256,256]{2,1,0:T(8,128)(2,1)S(1)}, bf16[2,256,256]{2,1,0:T(8,128)(2,1)S(1)}, u32[]{:S(2)}, u32[]{:S(2)}) %collective-permute-start.9) | collective-permute-done | bytes 262176 | tf_op jit(solution)/shard_map/ppermute | solution.py:395
  38.8 0.7 copy-done.4
  39.5 2.1 %collective-permute-done.8.refs_1_ = bf16[2,256,256]{2,1,0:T(8,128)(2,1)} collective-permute-done((bf16[2,256,256]{2,1,0:T(8,128)(2,1)S(1)}, bf16[2,256,256]{2,1,0:T(8,128)(2,1)}, u32[]{:S(2)}, u32[]{:S(2)}) %collective-permute-start.8) | collective-permute-done | bytes 262176 | tf_op jit(solution)/shard_map/ppermute | solution.py:395
  41.6 1.3 %join_panel.1 = (bf16[2,4,256,256]{3,2,1,0:T(8,128)(2,1)S(1)}, bf16[2,2,256,256]{3,2,1,0:T(8,128)(2,1)S(1)}, bf16[2,2,256,256]{3,2,1,0:T(8,128)(2,1)S(1)}) custom-call(bf16[2,256,256]{2,1,0:T(8,128)(2,1)} %copy-done.2, bf16[2,256,256]{2,1,0:T(8,128)(2,1)} %collective-permute-done.8.refs_1_, bf16[2,256,256]{2,1,0:T(8,128)(2,1)} %copy-done.4, ...), custom_call_target="tpu_custom_call" | custom-call | tf_op jit(solution)/shard_map/join_panel/pallas_call | solution.py:357
  43.0 0.1 collective-permute-start.13
  43.0 5.3 %collective-permute-start.14 = (bf16[2,2,256,256]{3,2,1,0:T(8,128)(2,1)S(1)}, bf16[2,2,256,256]{3,2,1,0:T(8,128)(2,1)S(1)}, u32[]{:S(2)}, u32[]{:S(2)}) collective-permute-start(bf16[2,2,256,256]{3,2,1,0:T(8,128)(2,1)S(1)} %get-tuple-element.41), channel_id=1, source_target_pairs={{0,15},{1,0},{2,1},{3,2},{4,3},{5,4},{6,5},{7,6},{8,7},{9,8},{10,9... | collective-permute-start | bytes 1572872 | tf_op jit(solution)/shard_map/ppermute | solution.py:394
  48.4 1.6 %copy-done = bf16[4,4,256,256]{3,2,1,0:T(8,128)(2,1)S(1)} copy-done((bf16[4,4,256,256]{3,2,1,0:T(8,128)(2,1)S(1)}, bf16[4,4,256,256]{3,2,1,0:T(8,128)(2,1)}, u32[]{:S(2)}) %copy-start) | copy-done | bytes 2097176
  50.0 10.4 %inner_field.1 = (f32[4,4,256,256]{3,2,1,0:T(8,128)S(1)}, f32[4,4,256,256]{3,2,1,0:T(8,128)S(1)}, f32[2,4,256,256]{3,2,1,0:T(8,128)S(1)}) custom-call(bf16[4,4,256,256]{3,2,1,0:T(8,128)(2,1)S(1)} %copy-done, bf16[2,4,256,256]{3,2,1,0:T(8,128)(2,1)S(1)} %get-tuple-element.34.p, bf16[768,256]{1,0:T(8,128)(2,1)S(1)} %copy-done.1), custom_call_target="tpu_custom_call" | custom-call | flops 6000000000 | bytes 8388608 | tf_op jit(solution)/shard_map/inner_field/pallas_call | solution.py:140
  60.3 0.7 collective-permute-done.13.plo
  61.1 7.7 %outer_field.1 = (f32[4,4,256,256]{3,2,1,0:T(8,128)}, f32[8,128]{1,0:T(8,128)S(1)}) custom-call(f32[4,4,256,256]{3,2,1,0:T(8,128)S(1)} %get-tuple-element.35.e_in, f32[4,4,256,256]{3,2,1,0:T(8,128)S(1)} %get-tuple-element.36.o, bf16[4,2,256,256]{3,2,1,0:T(8,128)(2,1)S(1)} %collective-permute-done.11.halo_low, ...), custom_call_target="tpu_custom_call" | custom-call | flops 3000000000 | bytes 14680064 | tf_op jit(solution)/shard_map/outer_field/pallas_call | solution.py:253
  68.8 0.3 collective-permute-start.15
  69.1 0.9 %collective-permute-done.15 = f32[8,128]{1,0:T(8,128)S(1)} collective-permute-done((f32[8,128]{1,0:T(8,128)S(1)}, f32[8,128]{1,0:T(8,128)S(1)}, u32[]{:S(2)}, u32[]{:S(2)}) %collective-permute-start.15) | collective-permute-done | bytes 4128 | tf_op jit(solution)/shard_map/ppermute | solution.py:379
  69.9 2.9 %collective-permute-start.16 = (f32[8,128]{1,0:T(8,128)S(1)}, f32[8,128]{1,0:T(8,128)S(1)}, u32[]{:S(2)}, u32[]{:S(2)}) collective-permute-start(f32[8,128]{1,0:T(8,128)S(1)} %add.19), channel_id=1, source_target_pairs={{0,2},{1,3},{2,0},{3,1},{4,6},{5,7},{6,4},{7,5},{8,10},{9,11},{10,... | collective-permute-start | bytes 12296 | tf_op jit(solution)/shard_map/ppermute | solution.py:379
  72.8 2.3 %collective-permute-done.16 = f32[8,128]{1,0:T(8,128)S(1)} collective-permute-done((f32[8,128]{1,0:T(8,128)S(1)}, f32[8,128]{1,0:T(8,128)S(1)}, u32[]{:S(2)}, u32[]{:S(2)}) %collective-permute-start.16) | collective-permute-done | bytes 4128 | tf_op jit(solution)/shard_map/ppermute | solution.py:379
  75.1 3.0 %collective-permute-start.19 = (f32[8,128]{1,0:T(8,128)S(1)}, f32[8,128]{1,0:T(8,128)S(1)}, u32[]{:S(2)}, u32[]{:S(2)}) collective-permute-start(f32[8,128]{1,0:T(8,128)S(1)} %add.20), channel_id=1, source_target_pairs={{0,12},{1,13},{2,14},{3,15},{4,8},{5,9},{6,10},{7,11},{8,4},{9,5},... | collective-permute-start | bytes 12296 | tf_op jit(solution)/shard_map/ppermute | solution.py:379
  78.0 1.0 %collective-permute-start.18 = (f32[8,128]{1,0:T(8,128)S(1)}, f32[8,128]{1,0:T(8,128)S(1)}, u32[]{:S(2)}, u32[]{:S(2)}) collective-permute-start(f32[8,128]{1,0:T(8,128)S(1)} %add.20), channel_id=1, source_target_pairs={{0,8},{1,9},{2,10},{3,11},{4,12},{5,13},{6,14},{7,15},{8,0},{9,1},... | collective-permute-start | bytes 12296 | tf_op jit(solution)/shard_map/ppermute | solution.py:379
  79.0 0.1 collective-permute-start.17
  79.2 0.7 collective-permute-done.19
  79.9 3.3 %collective-permute-done.18 = f32[8,128]{1,0:T(8,128)S(1)} collective-permute-done((f32[8,128]{1,0:T(8,128)S(1)}, f32[8,128]{1,0:T(8,128)S(1)}, u32[]{:S(2)}, u32[]{:S(2)}) %collective-permute-start.18) | collective-permute-done | bytes 4128 | tf_op jit(solution)/shard_map/ppermute | solution.py:379
  83.1 0.1 reshape.16
  83.2 0.1 reduce_sum.9
  83.3 0.7 copy.6
  (17 shorter events, 0.1 us)
Async XLA Ops:
  0.6 47.8 %copy-start.1 = (bf16[768,256]{1,0:T(8,128)(2,1)S(1)}, bf16[768,256]{1,0:T(8,128)(2,1)}, u32[]{:S(2)}) copy-start(bf16[768,256]{1,0:T(8,128)(2,1)} %constant.32.mix) | copy-start | bytes 1179652
  2.8 10.6 %collective-permute-start.3 = (bf16[256,256]{1,0:T(8,128)(2,1)}, bf16[256,256]{1,0:T(8,128)(2,1)S(1)}, u32[]{:S(2)}, u32[]{:S(2)}) collective-permute-start(bf16[256,256]{1,0:T(8,128)(2,1)} %get-tuple-element.31), channel_id=1, source_target_pairs={{0,16},{16,32},{32,48},{48,0},{64,80},{80,96},{96,112},{112,64},{1... | collective-permute-start | bytes 393224 | tf_op jit(solution)/shard_map/ppermute | solution.py:395
  4.4 10.8 %collective-permute-start.4 = (bf16[256,256]{1,0:T(8,128)(2,1)}, bf16[256,256]{1,0:T(8,128)(2,1)S(1)}, u32[]{:S(2)}, u32[]{:S(2)}) collective-permute-start(bf16[256,256]{1,0:T(8,128)(2,1)} %get-tuple-element.32), channel_id=1, source_target_pairs={{0,32},{16,48},{32,0},{48,16},{64,96},{80,112},{96,64},{112,80},{1... | collective-permute-start | bytes 393224 | tf_op jit(solution)/shard_map/ppermute | solution.py:395
  7.2 8.1 %collective-permute-start.5 = (bf16[256,256]{1,0:T(8,128)(2,1)}, bf16[256,256]{1,0:T(8,128)(2,1)S(1)}, u32[]{:S(2)}, u32[]{:S(2)}) collective-permute-start(bf16[256,256]{1,0:T(8,128)(2,1)} %get-tuple-element.33), channel_id=1, source_target_pairs={{0,48},{16,0},{32,16},{48,32},{64,112},{80,64},{96,80},{112,96},{1... | collective-permute-start | bytes 393224 | tf_op jit(solution)/shard_map/ppermute | solution.py:395
  8.6 9.2 %collective-permute-start = (bf16[256,256]{1,0:T(8,128)(2,1)}, bf16[256,256]{1,0:T(8,128)(2,1)S(1)}, u32[]{:S(2)}, u32[]{:S(2)}) collective-permute-start(bf16[256,256]{1,0:T(8,128)(2,1)} %get-tuple-element.24), channel_id=1, source_target_pairs={{0,16},{16,32},{32,48},{48,0},{64,80},{80,96},{96,112},{112,64},{1... | collective-permute-start | bytes 393224 | tf_op jit(solution)/shard_map/ppermute | solution.py:395
  9.2 9.8 %collective-permute-start.1 = (bf16[256,256]{1,0:T(8,128)(2,1)}, bf16[256,256]{1,0:T(8,128)(2,1)S(1)}, u32[]{:S(2)}, u32[]{:S(2)}) collective-permute-start(bf16[256,256]{1,0:T(8,128)(2,1)} %get-tuple-element.25), channel_id=1, source_target_pairs={{0,32},{16,48},{32,0},{48,16},{64,96},{80,112},{96,64},{112,80},{1... | collective-permute-start | bytes 393224 | tf_op jit(solution)/shard_map/ppermute | solution.py:395
  13.4 5.9 %collective-permute-start.2 = (bf16[256,256]{1,0:T(8,128)(2,1)}, bf16[256,256]{1,0:T(8,128)(2,1)S(1)}, u32[]{:S(2)}, u32[]{:S(2)}) collective-permute-start(bf16[256,256]{1,0:T(8,128)(2,1)} %get-tuple-element.26), channel_id=1, source_target_pairs={{0,48},{16,0},{32,16},{48,32},{64,112},{80,64},{96,80},{112,96},{1... | collective-permute-start | bytes 393224 | tf_op jit(solution)/shard_map/ppermute | solution.py:395
  16.2 11.0 %collective-permute-start.7 = (bf16[256,256]{1,0:T(8,128)(2,1)S(1)}, bf16[256,256]{1,0:T(8,128)(2,1)S(1)}, u32[]{:S(2)}, u32[]{:S(2)}) collective-permute-start(bf16[256,256]{1,0:T(8,128)(2,1)S(1)} %select_select_fusion), channel_id=1, source_target_pairs={{0,64},{16,80},{32,96},{48,112},{64,0},{80,16},{96,32},{112,48},{1... | collective-permute-start | bytes 393224 | tf_op jit(solution)/shard_map/ppermute | solution.py:396
  20.2 7.0 %collective-permute-start.6 = (bf16[256,256]{1,0:T(8,128)(2,1)S(1)}, bf16[256,256]{1,0:T(8,128)(2,1)S(1)}, u32[]{:S(2)}, u32[]{:S(2)}) collective-permute-start(bf16[256,256]{1,0:T(8,128)(2,1)S(1)} %select_select_fusion.1), channel_id=1, source_target_pairs={{0,64},{16,80},{32,96},{48,112},{64,0},{80,16},{96,32},{112,48},{1... | collective-permute-start | bytes 393224 | tf_op jit(solution)/shard_map/ppermute | solution.py:396
  21.8 39.3 %collective-permute-start.11 = (bf16[4,2,256,256]{3,2,1,0:T(8,128)(2,1)}, bf16[4,2,256,256]{3,2,1,0:T(8,128)(2,1)S(1)}, u32[]{:S(2)}, u32[]{:S(2)}) collective-permute-start(bf16[4,2,256,256]{3,2,1,0:T(8,128)(2,1)} %get-tuple-element.37), channel_id=1, source_target_pairs={{0,1},{1,2},{2,3},{3,4},{4,5},{5,6},{6,7},{7,8},{8,9},{9,10},{10,1... | collective-permute-start | bytes 3145736 | tf_op jit(solution)/shard_map/ppermute | solution.py:393
  21.8 39.3 %collective-permute-start.12 = (bf16[4,2,256,256]{3,2,1,0:T(8,128)(2,1)}, bf16[4,2,256,256]{3,2,1,0:T(8,128)(2,1)}, u32[]{:S(2)}, u32[]{:S(2)}) collective-permute-start(bf16[4,2,256,256]{3,2,1,0:T(8,128)(2,1)} %get-tuple-element.38), channel_id=1, source_target_pairs={{0,15},{1,0},{2,1},{3,2},{4,3},{5,4},{6,5},{7,6},{8,7},{9,8},{10,9... | collective-permute-start | bytes 3145736 | tf_op jit(solution)/shard_map/ppermute | solution.py:394
  27.2 11.6 %copy-start.2 = (bf16[2,256,256]{2,1,0:T(8,128)(2,1)}, bf16[2,256,256]{2,1,0:T(8,128)(2,1)S(1)}, u32[]{:S(2)}) copy-start(bf16[2,256,256]{2,1,0:T(8,128)(2,1)S(1)} %maximum_select_fusion.refs_0_) | copy-start | bytes 786436
  27.2 8.8 %collective-permute-start.10 = (bf16[2,256,256]{2,1,0:T(8,128)(2,1)S(1)}, bf16[2,256,256]{2,1,0:T(8,128)(2,1)S(1)}, u32[]{:S(2)}, u32[]{:S(2)}) collective-permute-start(bf16[2,256,256]{2,1,0:T(8,128)(2,1)S(1)} %maximum_select_fusion.refs_0_), channel_id=1, source_target_pairs={{0,48},{16,0},{32,16},{48,32},{64,112},{80,64},{96,80},{112,96},{1... | collective-permute-start | bytes 786440 | tf_op jit(solution)/shard_map/ppermute | solution.py:395
  28.8 10.0 %collective-permute-start.9 = (bf16[2,256,256]{2,1,0:T(8,128)(2,1)S(1)}, bf16[2,256,256]{2,1,0:T(8,128)(2,1)S(1)}, u32[]{:S(2)}, u32[]{:S(2)}) collective-permute-start(bf16[2,256,256]{2,1,0:T(8,128)(2,1)S(1)} %maximum_select_fusion.refs_0_), channel_id=1, source_target_pairs={{0,32},{16,48},{32,0},{48,16},{64,96},{80,112},{96,64},{112,80},{1... | collective-permute-start | bytes 786440 | tf_op jit(solution)/shard_map/ppermute | solution.py:395
  30.6 11.1 %collective-permute-start.8 = (bf16[2,256,256]{2,1,0:T(8,128)(2,1)S(1)}, bf16[2,256,256]{2,1,0:T(8,128)(2,1)}, u32[]{:S(2)}, u32[]{:S(2)}) collective-permute-start(bf16[2,256,256]{2,1,0:T(8,128)(2,1)S(1)} %maximum_select_fusion.refs_0_), channel_id=1, source_target_pairs={{0,16},{16,32},{32,48},{48,0},{64,80},{80,96},{96,112},{112,64},{1... | collective-permute-start | bytes 786440 | tf_op jit(solution)/shard_map/ppermute | solution.py:395
  36.0 2.8 %copy-start.3 = (bf16[2,256,256]{2,1,0:T(8,128)(2,1)}, bf16[2,256,256]{2,1,0:T(8,128)(2,1)S(1)}, u32[]{:S(2)}) copy-start(bf16[2,256,256]{2,1,0:T(8,128)(2,1)S(1)} %collective-permute-done.10.refs_3_) | copy-start | bytes 786436
  38.8 0.7 copy-start.4
  43.0 18.1 %collective-permute-start.13 = (bf16[2,2,256,256]{3,2,1,0:T(8,128)(2,1)S(1)}, bf16[2,2,256,256]{3,2,1,0:T(8,128)(2,1)S(1)}, u32[]{:S(2)}, u32[]{:S(2)}) collective-permute-start(bf16[2,2,256,256]{3,2,1,0:T(8,128)(2,1)S(1)} %get-tuple-element.40), channel_id=1, source_target_pairs={{0,1},{1,2},{2,3},{3,4},{4,5},{5,6},{6,7},{7,8},{8,9},{9,10},{10,1... | collective-permute-start | bytes 1572872 | tf_op jit(solution)/shard_map/ppermute | solution.py:393
  43.0 18.0 %collective-permute-start.14 = (bf16[2,2,256,256]{3,2,1,0:T(8,128)(2,1)S(1)}, bf16[2,2,256,256]{3,2,1,0:T(8,128)(2,1)S(1)}, u32[]{:S(2)}, u32[]{:S(2)}) collective-permute-start(bf16[2,2,256,256]{3,2,1,0:T(8,128)(2,1)S(1)} %get-tuple-element.41), channel_id=1, source_target_pairs={{0,15},{1,0},{2,1},{3,2},{4,3},{5,4},{6,5},{7,6},{8,7},{9,8},{10,9... | collective-permute-start | bytes 1572872 | tf_op jit(solution)/shard_map/ppermute | solution.py:394
  48.4 1.6 %copy-start = (bf16[4,4,256,256]{3,2,1,0:T(8,128)(2,1)S(1)}, bf16[4,4,256,256]{3,2,1,0:T(8,128)(2,1)}, u32[]{:S(2)}) copy-start(bf16[4,4,256,256]{3,2,1,0:T(8,128)(2,1)} %o.1) | copy-start | bytes 6291460
  68.8 1.2 %collective-permute-start.15 = (f32[8,128]{1,0:T(8,128)S(1)}, f32[8,128]{1,0:T(8,128)S(1)}, u32[]{:S(2)}, u32[]{:S(2)}) collective-permute-start(f32[8,128]{1,0:T(8,128)S(1)} %get-tuple-element.43), channel_id=1, source_target_pairs={{0,1},{1,0},{2,3},{3,2},{4,5},{5,4},{6,7},{7,6},{8,9},{9,8},{10,11... | collective-permute-start | bytes 12296 | tf_op jit(solution)/shard_map/ppermute | solution.py:379
  69.9 5.1 %collective-permute-start.16 = (f32[8,128]{1,0:T(8,128)S(1)}, f32[8,128]{1,0:T(8,128)S(1)}, u32[]{:S(2)}, u32[]{:S(2)}) collective-permute-start(f32[8,128]{1,0:T(8,128)S(1)} %add.19), channel_id=1, source_target_pairs={{0,2},{1,3},{2,0},{3,1},{4,6},{5,7},{6,4},{7,5},{8,10},{9,11},{10,... | collective-permute-start | bytes 12296 | tf_op jit(solution)/shard_map/ppermute | solution.py:379
  75.1 4.8 %collective-permute-start.19 = (f32[8,128]{1,0:T(8,128)S(1)}, f32[8,128]{1,0:T(8,128)S(1)}, u32[]{:S(2)}, u32[]{:S(2)}) collective-permute-start(f32[8,128]{1,0:T(8,128)S(1)} %add.20), channel_id=1, source_target_pairs={{0,12},{1,13},{2,14},{3,15},{4,8},{5,9},{6,10},{7,11},{8,4},{9,5},... | collective-permute-start | bytes 12296 | tf_op jit(solution)/shard_map/ppermute | solution.py:379
  78.0 5.1 %collective-permute-start.18 = (f32[8,128]{1,0:T(8,128)S(1)}, f32[8,128]{1,0:T(8,128)S(1)}, u32[]{:S(2)}, u32[]{:S(2)}) collective-permute-start(f32[8,128]{1,0:T(8,128)S(1)} %add.20), channel_id=1, source_target_pairs={{0,8},{1,9},{2,10},{3,11},{4,12},{5,13},{6,14},{7,15},{8,0},{9,1},... | collective-permute-start | bytes 12296 | tf_op jit(solution)/shard_map/ppermute | solution.py:379
  79.0 4.1 %collective-permute-start.17 = (f32[8,128]{1,0:T(8,128)S(1)}, f32[8,128]{1,0:T(8,128)S(1)}, u32[]{:S(2)}, u32[]{:S(2)}) collective-permute-start(f32[8,128]{1,0:T(8,128)S(1)} %add.20), channel_id=1, source_target_pairs={{0,4},{1,5},{2,6},{3,7},{4,0},{5,1},{6,2},{7,3},{8,12},{9,13},{10,... | collective-permute-start | bytes 12296 | tf_op jit(solution)/shard_map/ppermute | solution.py:379

commit v6 on v5

--- a/solution.py
+++ b/solution.py
@@ -171,7 +171,7 @@
         rho, left, base = rhos[s], lefts[s], bases[s]
         for i in range(steps):
             for h in range(halves):
-                ov = at(halo, (0, h1), i * STRIP, STRIP, h).astype(f32)
+                ov = at(halo, (pl.program_id(0), h1), i * STRIP, STRIP, h).astype(f32)
                 for a in range(na):
                     rho[a, h, PAD + i * STRIP:PAD + (i + 1) * STRIP, :] = at(ph, (a, h1), i * STRIP, STRIP, h).astype(f32) * ov
         for a in range(na):
@@ -181,7 +181,7 @@
                 r = PAD + i * STRIP
                 rows = slice(i * STRIP, (i + 1) * STRIP)
                 lanes = slice(h * LANES, (h + 1) * LANES)
-                ov = at(halo, (0, h2), i * STRIP, STRIP, h).astype(f32)
+                ov = at(halo, (pl.program_id(0), h2), i * STRIP, STRIP, h).astype(f32)
                 step = None
                 for a in range(na):
                     c = sp(rho, (a,), r, STRIP, h)
@@ -254,7 +254,7 @@
         outer_kernel,
         grid=(nj,),
         out_shape=(jax.ShapeDtypeStruct(e.shape, f32), jax.ShapeDtypeStruct((8, LANES), f32)),
-        in_specs=[pl.BlockSpec(memory_space=pltpu.VMEM), pl.BlockSpec(memory_space=pltpu.VMEM), *[each(h.shape) for h in halo], pl.BlockSpec(memory_space=pltpu.VMEM), whole(plo.shape), whole(phi.shape), pl.BlockSpec(memory_space=pltpu.VMEM)],
+        in_specs=[pl.BlockSpec(memory_space=pltpu.VMEM), pl.BlockSpec(memory_space=pltpu.VMEM), *[pl.BlockSpec(memory_space=pltpu.VMEM)] * 2, pl.BlockSpec(memory_space=pltpu.VMEM), whole(plo.shape), whole(phi.shape), pl.BlockSpec(memory_space=pltpu.VMEM)],
         out_specs=(each(e.shape), pl.BlockSpec((8, LANES), lambda j: (0, 0))),
         scratch_shapes=[pltpu.VMEM((na, nz // LANES, ny + 2 * PAD, LANES), f32)] * 2
         + [pltpu.VMEM((na, ny, 2 * nz), bf)] * 2
@@ -263,6 +263,27 @@
         cost_estimate=pl.CostEstimate(flops=3 * 10**9, bytes_accessed=14 * 2**20, transcendentals=0),
         name="outer_field",
     )(e, o, *halo, p, plo, phi, mix)
+
+
+def hold_kernel(low_in, high_in, after, low, high, sems):
+    copies = [pltpu.make_async_copy(low_in, low, sems.at[0]), pltpu.make_async_copy(high_in, high, sems.at[1])]
+    for c in copies:
+        c.start()
+    for c in copies:
+        c.wait()
+
+
+def hold(halo, after):
+    vmem = pl.BlockSpec(memory_space=pltpu.VMEM)
+    return pl.pallas_call(
+        hold_kernel,
+        out_shape=tuple(pltpu.VMEM(h.shape, h.dtype) for h in halo),
+        in_specs=[pl.BlockSpec(memory_space=pl.ANY)] * 2 + [vmem],
+        out_specs=(vmem, vmem),
+        scratch_shapes=[pltpu.SemaphoreType.DMA((2,))],
+        compiler_params=pltpu.CompilerParams(vmem_limit_bytes=2**20),
+        name="hold_halo",
+    )(*halo, after)
 
 
 def cut_kernel(row, orbitals, *refs):
@@ -406,6 +427,7 @@
     panel, top, bottom = join([both] + [along(both, n) for n in range(1, row)])
     low, high = up(top), down(bottom)
     exchange, o_wide, p_wide = inner(orbitals, panel)
+    halo = hold(halo, p_wide)
     exchange, sums = outer(exchange, o_wide, halo, p_wide, low, high)
     cells = float(nx * slabs * ny * nz)
     ace_block = jnp.sum(total(sums)[:PANEL + nj].reshape(PANEL + nj, nj, -1), axis=2) / cells

time: 84.3 us -> 84.2 us (level)
  other arithmetic: 2.01 us -> 0.21 us
  waiting for transfers between devices: 19.6 us -> 20.8 us
    ppermute x5, starting transfers between devices: 7.25 us -> 5.42 us  [total(): lax.ppermute(part, 'dom', [(i, i ^ k) for i in range(count)])]
    select_n x2, other arithmetic: 1.86 us -> 0.06 us  [local(): mine = [lax.select_n(behind, *g) for g in got]]
    ppermute x5, waiting for transfers between devices: 7.1 us -> 8.8 us  [total(): lax.ppermute(part, 'dom', [(i, i ^ k) for i in range(count)])]
    ppermute x9, starting transfers between devices: 12.5 us -> 14 us  [local(): along = lambda v, k: lax.ppermute(v, 'band', rows(k, row))]
    pallas_call x0 -> x1, Pallas kernels: none -> 1.31 us  [hold(): pl.pallas_call(hold_kernel, out_shape=tuple((pltpu.VMEM(h.shape, h.dtype)...]
  transfers between devices with their start and end apart: 20 -> 20, of which waited for: 10 -> 10; matrix products, arithmetic and copies ran while one was open for 2% -> 0% of each run, Pallas kernels for 17% -> 19%
where the time goes in v6:
time: 84.2 us; the launch traced here: 83.9 us
  starting transfers between devices  33.5 us (40%)
  Pallas kernels  24.9 us (30%)
  waiting for transfers between devices  20.8 us (25%)
  local copies, waits for them, and re-layouts  3.09 us (4%)
  between operations  1.45 us (2%)
    ppermute x9, starting transfers between devices, local(): along = lambda v, k: lax.ppermute(v, 'band', rows(k, row))  14 us
    ppermute x9, waiting for transfers between devices, local(): along = lambda v, k: lax.ppermute(v, 'band', rows(k, row))  12 us
    ppermute x2, starting transfers between devices, local(): down = lambda v: lax.ppermute(v, 'dom', ring(lax.axis_size('dom'), -1))  10.7 us
    pallas_call x1, Pallas kernels, inner(): pl.pallas_call(inner_kernel, grid=(nj,), out_shape=(pltpu.VMEM((nj, nx, n...  10.3 us
    ppermute x5, waiting for transfers between devices, total(): lax.ppermute(part, 'dom', [(i, i ^ k) for i in range(count)])  8.8 us
    pallas_call x1, Pallas kernels, outer(): pl.pallas_call(outer_kernel, grid=(nj,), out_shape=(jax.ShapeDtypeStruct(...  7.14 us
    ppermute x5, starting transfers between devices, total(): lax.ppermute(part, 'dom', [(i, i ^ k) for i in range(count)])  5.42 us
    ppermute x2, starting transfers between devices, local(): across = lambda v: lax.ppermute(v, 'band', ring(lax.axis_size('band'), row))  3.31 us
  transfers between devices with their start and end apart: 20, of which 10 were waited for; matrix products, arithmetic and copies ran while one was open for 0% of the time, Pallas kernels for 19%

profile of v6, /device:TPU:0, one launch (start us, length us, event | category | flops | bytes accessed | tf_op | source)
XLA Modules:
  0.0 83.9 jit_solution(14305504158472480170)
XLA Ops:
  0.6 0.0 copy-start.1
  0.6 2.1 %cut_panel.1 = (bf16[256,256]{1,0:T(8,128)(2,1)}, bf16[256,256]{1,0:T(8,128)(2,1)}, bf16[256,256]{1,0:T(8,128)(2,1)}, bf16[256,256]{1,0:T(8,128)(2,1)}, bf16[256...) custom-call(bf16[4,4,256,256]{3,2,1,0:T(8,128)(2,1)} %o.1), custom_call_target="tpu_custom_call" | custom-call | tf_op jit(solution)/shard_map/cut_panel/pallas_call | solution.py:313
  2.8 1.6 %collective-permute-start.3 = (bf16[256,256]{1,0:T(8,128)(2,1)}, bf16[256,256]{1,0:T(8,128)(2,1)S(1)}, u32[]{:S(2)}, u32[]{:S(2)}) collective-permute-start(bf16[256,256]{1,0:T(8,128)(2,1)} %get-tuple-element.33), channel_id=1, source_target_pairs={{0,16},{16,32},{32,48},{48,0},{64,80},{80,96},{96,112},{112,64},{1... | collective-permute-start | bytes 393224 | tf_op jit(solution)/shard_map/ppermute | solution.py:416
  4.4 2.7 %collective-permute-start.4 = (bf16[256,256]{1,0:T(8,128)(2,1)}, bf16[256,256]{1,0:T(8,128)(2,1)S(1)}, u32[]{:S(2)}, u32[]{:S(2)}) collective-permute-start(bf16[256,256]{1,0:T(8,128)(2,1)} %get-tuple-element.34), channel_id=1, source_target_pairs={{0,32},{16,48},{32,0},{48,16},{64,96},{80,112},{96,64},{112,80},{1... | collective-permute-start | bytes 393224 | tf_op jit(solution)/shard_map/ppermute | solution.py:416
  7.2 1.4 %collective-permute-start.5 = (bf16[256,256]{1,0:T(8,128)(2,1)}, bf16[256,256]{1,0:T(8,128)(2,1)S(1)}, u32[]{:S(2)}, u32[]{:S(2)}) collective-permute-start(bf16[256,256]{1,0:T(8,128)(2,1)} %get-tuple-element.35), channel_id=1, source_target_pairs={{0,48},{16,0},{32,16},{48,32},{64,112},{80,64},{96,80},{112,96},{1... | collective-permute-start | bytes 393224 | tf_op jit(solution)/shard_map/ppermute | solution.py:416
  8.6 0.6 collective-permute-start
  9.2 0.9 %collective-permute-start.1 = (bf16[256,256]{1,0:T(8,128)(2,1)}, bf16[256,256]{1,0:T(8,128)(2,1)S(1)}, u32[]{:S(2)}, u32[]{:S(2)}) collective-permute-start(bf16[256,256]{1,0:T(8,128)(2,1)} %get-tuple-element.27), channel_id=1, source_target_pairs={{0,32},{16,48},{32,0},{48,16},{64,96},{80,112},{96,64},{112,80},{1... | collective-permute-start | bytes 393224 | tf_op jit(solution)/shard_map/ppermute | solution.py:416
  10.7 2.6 %edge_planes.1 = (bf16[4,2,256,256]{3,2,1,0:T(8,128)(2,1)}, bf16[4,2,256,256]{3,2,1,0:T(8,128)(2,1)}) custom-call(bf16[4,4,256,256]{3,2,1,0:T(8,128)(2,1)} %o.1), custom_call_target="tpu_custom_call" | custom-call | tf_op jit(solution)/shard_map/edge_planes/pallas_call | solution.py:344
  13.4 0.0 collective-permute-done.3
  13.4 1.9 %collective-permute-start.2 = (bf16[256,256]{1,0:T(8,128)(2,1)}, bf16[256,256]{1,0:T(8,128)(2,1)S(1)}, u32[]{:S(2)}, u32[]{:S(2)}) collective-permute-start(bf16[256,256]{1,0:T(8,128)(2,1)} %get-tuple-element.28), channel_id=1, source_target_pairs={{0,48},{16,0},{32,16},{48,32},{64,112},{80,64},{96,80},{112,96},{1... | collective-permute-start | bytes 393224 | tf_op jit(solution)/shard_map/ppermute | solution.py:416
  15.2 0.0 collective-permute-done.4
  15.2 0.0 collective-permute-done.5
  15.3 1.7 %collective-permute-start.7 = (bf16[256,256]{1,0:T(8,128)(2,1)S(1)}, bf16[256,256]{1,0:T(8,128)(2,1)S(1)}, u32[]{:S(2)}, u32[]{:S(2)}) collective-permute-start(bf16[256,256]{1,0:T(8,128)(2,1)S(1)} %select_select_fusion), channel_id=1, source_target_pairs={{0,64},{16,80},{32,96},{48,112},{64,0},{80,16},{96,32},{112,48},{1... | collective-permute-start | bytes 393224 | tf_op jit(solution)/shard_map/ppermute | solution.py:417
  16.9 0.3 collective-permute-done
  17.2 1.8 %collective-permute-done.1 = bf16[256,256]{1,0:T(8,128)(2,1)S(1)} collective-permute-done((bf16[256,256]{1,0:T(8,128)(2,1)}, bf16[256,256]{1,0:T(8,128)(2,1)S(1)}, u32[]{:S(2)}, u32[]{:S(2)}) %collective-permute-start.1) | collective-permute-done | bytes 131104 | tf_op jit(solution)/shard_map/ppermute | solution.py:416
  19.0 0.2 collective-permute-done.2
  19.3 1.7 %collective-permute-start.6 = (bf16[256,256]{1,0:T(8,128)(2,1)S(1)}, bf16[256,256]{1,0:T(8,128)(2,1)S(1)}, u32[]{:S(2)}, u32[]{:S(2)}) collective-permute-start(bf16[256,256]{1,0:T(8,128)(2,1)S(1)} %select_select_fusion.1), channel_id=1, source_target_pairs={{0,64},{16,80},{32,96},{48,112},{64,0},{80,16},{96,32},{112,48},{1... | collective-permute-start | bytes 393224 | tf_op jit(solution)/shard_map/ppermute | solution.py:417
  20.9 0.0 collective-permute-start.11
  20.9 5.4 %collective-permute-start.12 = (bf16[4,2,256,256]{3,2,1,0:T(8,128)(2,1)}, bf16[4,2,256,256]{3,2,1,0:T(8,128)(2,1)}, u32[]{:S(2)}, u32[]{:S(2)}) collective-permute-start(bf16[4,2,256,256]{3,2,1,0:T(8,128)(2,1)} %get-tuple-element.40), channel_id=1, source_target_pairs={{0,15},{1,0},{2,1},{3,2},{4,3},{5,4},{6,5},{7,6},{8,7},{9,8},{10,9... | collective-permute-start | bytes 3145736 | tf_op jit(solution)/shard_map/ppermute | solution.py:415
  26.3 0.0 collective-permute-done.7
  26.3 0.0 collective-permute-done.6
  26.3 2.5 %collective-permute-start.10 = (bf16[2,256,256]{2,1,0:T(8,128)(2,1)S(1)}, bf16[2,256,256]{2,1,0:T(8,128)(2,1)S(1)}, u32[]{:S(2)}, u32[]{:S(2)}) collective-permute-start(bf16[2,256,256]{2,1,0:T(8,128)(2,1)S(1)} %maximum_select_fusion.refs_0_), channel_id=1, source_target_pairs={{0,48},{16,0},{32,16},{48,32},{64,112},{80,64},{96,80},{112,96},{1... | collective-permute-start | bytes 786440 | tf_op jit(solution)/shard_map/ppermute | solution.py:416
  28.8 1.7 %collective-permute-start.9 = (bf16[2,256,256]{2,1,0:T(8,128)(2,1)S(1)}, bf16[2,256,256]{2,1,0:T(8,128)(2,1)S(1)}, u32[]{:S(2)}, u32[]{:S(2)}) collective-permute-start(bf16[2,256,256]{2,1,0:T(8,128)(2,1)S(1)} %maximum_select_fusion.refs_0_), channel_id=1, source_target_pairs={{0,32},{16,48},{32,0},{48,16},{64,96},{80,112},{96,64},{112,80},{1... | collective-permute-start | bytes 786440 | tf_op jit(solution)/shard_map/ppermute | solution.py:416
  30.6 0.6 collective-permute-start.8
  31.2 6.7 %collective-permute-done.10.refs_3_ = bf16[2,256,256]{2,1,0:T(8,128)(2,1)S(1)} collective-permute-done((bf16[2,256,256]{2,1,0:T(8,128)(2,1)S(1)}, bf16[2,256,256]{2,1,0:T(8,128)(2,1)S(1)}, u32[]{:S(2)}, u32[]{:S(2)}) %collective-permute-start.10) | collective-permute-done | bytes 262176 | tf_op jit(solution)/shard_map/ppermute | solution.py:416
  37.9 0.9 %collective-permute-done.9.refs_2_ = bf16[2,256,256]{2,1,0:T(8,128)(2,1)S(1)} collective-permute-done((bf16[2,256,256]{2,1,0:T(8,128)(2,1)S(1)}, bf16[2,256,256]{2,1,0:T(8,128)(2,1)S(1)}, u32[]{:S(2)}, u32[]{:S(2)}) %collective-permute-start.9) | collective-permute-done | bytes 262176 | tf_op jit(solution)/shard_map/ppermute | solution.py:416
  38.8 0.7 copy-done.4
  39.5 2.1 %collective-permute-done.8.refs_1_ = bf16[2,256,256]{2,1,0:T(8,128)(2,1)} collective-permute-done((bf16[2,256,256]{2,1,0:T(8,128)(2,1)S(1)}, bf16[2,256,256]{2,1,0:T(8,128)(2,1)}, u32[]{:S(2)}, u32[]{:S(2)}) %collective-permute-start.8) | collective-permute-done | bytes 262176 | tf_op jit(solution)/shard_map/ppermute | solution.py:416
  41.6 1.3 %join_panel.1 = (bf16[2,4,256,256]{3,2,1,0:T(8,128)(2,1)S(1)}, bf16[2,2,256,256]{3,2,1,0:T(8,128)(2,1)S(1)}, bf16[2,2,256,256]{3,2,1,0:T(8,128)(2,1)S(1)}) custom-call(bf16[2,256,256]{2,1,0:T(8,128)(2,1)} %copy-done.2, bf16[2,256,256]{2,1,0:T(8,128)(2,1)} %collective-permute-done.8.refs_1_, bf16[2,256,256]{2,1,0:T(8,128)(2,1)} %copy-done.4, ...), custom_call_target="tpu_custom_call" | custom-call | tf_op jit(solution)/shard_map/join_panel/pallas_call | solution.py:378
  43.0 0.1 collective-permute-start.13
  43.0 5.3 %collective-permute-start.14 = (bf16[2,2,256,256]{3,2,1,0:T(8,128)(2,1)S(1)}, bf16[2,2,256,256]{3,2,1,0:T(8,128)(2,1)S(1)}, u32[]{:S(2)}, u32[]{:S(2)}) collective-permute-start(bf16[2,2,256,256]{3,2,1,0:T(8,128)(2,1)S(1)} %get-tuple-element.45), channel_id=1, source_target_pairs={{0,15},{1,0},{2,1},{3,2},{4,3},{5,4},{6,5},{7,6},{8,7},{9,8},{10,9... | collective-permute-start | bytes 1572872 | tf_op jit(solution)/shard_map/ppermute | solution.py:415
  48.4 1.6 %copy-done = bf16[4,4,256,256]{3,2,1,0:T(8,128)(2,1)S(1)} copy-done((bf16[4,4,256,256]{3,2,1,0:T(8,128)(2,1)S(1)}, bf16[4,4,256,256]{3,2,1,0:T(8,128)(2,1)}, u32[]{:S(2)}) %copy-start) | copy-done | bytes 2097176
  50.0 10.3 %inner_field.1 = (f32[4,4,256,256]{3,2,1,0:T(8,128)S(1)}, f32[4,4,256,256]{3,2,1,0:T(8,128)S(1)}, f32[2,4,256,256]{3,2,1,0:T(8,128)S(1)}) custom-call(bf16[4,4,256,256]{3,2,1,0:T(8,128)(2,1)S(1)} %copy-done, bf16[2,4,256,256]{3,2,1,0:T(8,128)(2,1)S(1)} %get-tuple-element.36.p, bf16[768,256]{1,0:T(8,128)(2,1)S(1)} %copy-done.1), custom_call_target="tpu_custom_call" | custom-call | flops 6000000000 | bytes 8388608 | tf_op jit(solution)/shard_map/inner_field/pallas_call | solution.py:140
  60.4 0.0 collective-permute-done.12.high_in
  60.4 1.3 %hold_halo.1 = (bf16[4,2,256,256]{3,2,1,0:T(8,128)(2,1)S(1)}, bf16[4,2,256,256]{3,2,1,0:T(8,128)(2,1)S(1)}) custom-call(bf16[4,2,256,256]{3,2,1,0:T(8,128)(2,1)S(1)} %collective-permute-done.11.low_in, bf16[4,2,256,256]{3,2,1,0:T(8,128)(2,1)} %collective-permute-done.12.high_in, f32[2,4,256,256]{3,2,1,0:T(8,128)S(1)} %get-tuple-element.41.after.p), custom_call_target="tpu_custom_call" | custom-call | tf_op jit(solution)/shard_map/hold_halo/pallas_call | solution.py:278
  61.7 7.1 %outer_field.1 = (f32[4,4,256,256]{3,2,1,0:T(8,128)}, f32[8,128]{1,0:T(8,128)S(1)}) custom-call(f32[4,4,256,256]{3,2,1,0:T(8,128)S(1)} %get-tuple-element.37.e_in, f32[4,4,256,256]{3,2,1,0:T(8,128)S(1)} %get-tuple-element.38.o, bf16[4,2,256,256]{3,2,1,0:T(8,128)(2,1)S(1)} %get-tuple-element.42.halo_low, ...), custom_call_target="tpu_custom_call" | custom-call | flops 3000000000 | bytes 14680064 | tf_op jit(solution)/shard_map/outer_field/pallas_call | solution.py:253
  68.8 0.0 collective-permute-start.15
  68.9 1.2 %collective-permute-done.15 = f32[8,128]{1,0:T(8,128)S(1)} collective-permute-done((f32[8,128]{1,0:T(8,128)S(1)}, f32[8,128]{1,0:T(8,128)S(1)}, u32[]{:S(2)}, u32[]{:S(2)}) %collective-permute-start.15) | collective-permute-done | bytes 4128 | tf_op jit(solution)/shard_map/ppermute | solution.py:400
  70.0 1.3 %collective-permute-start.16 = (f32[8,128]{1,0:T(8,128)S(1)}, f32[8,128]{1,0:T(8,128)S(1)}, u32[]{:S(2)}, u32[]{:S(2)}) collective-permute-start(f32[8,128]{1,0:T(8,128)S(1)} %add.19), channel_id=1, source_target_pairs={{0,2},{1,3},{2,0},{3,1},{4,6},{5,7},{6,4},{7,5},{8,10},{9,11},{10,... | collective-permute-start | bytes 12296 | tf_op jit(solution)/shard_map/ppermute | solution.py:400
  71.3 3.8 %collective-permute-done.16 = f32[8,128]{1,0:T(8,128)S(1)} collective-permute-done((f32[8,128]{1,0:T(8,128)S(1)}, f32[8,128]{1,0:T(8,128)S(1)}, u32[]{:S(2)}, u32[]{:S(2)}) %collective-permute-start.16) | collective-permute-done | bytes 4128 | tf_op jit(solution)/shard_map/ppermute | solution.py:400
  75.1 2.8 %collective-permute-start.19 = (f32[8,128]{1,0:T(8,128)S(1)}, f32[8,128]{1,0:T(8,128)S(1)}, u32[]{:S(2)}, u32[]{:S(2)}) collective-permute-start(f32[8,128]{1,0:T(8,128)S(1)} %add.20), channel_id=1, source_target_pairs={{0,12},{1,13},{2,14},{3,15},{4,8},{5,9},{6,10},{7,11},{8,4},{9,5},... | collective-permute-start | bytes 12296 | tf_op jit(solution)/shard_map/ppermute | solution.py:400
  78.0 0.0 collective-permute-start.18
  78.0 1.3 %collective-permute-start.17 = (f32[8,128]{1,0:T(8,128)S(1)}, f32[8,128]{1,0:T(8,128)S(1)}, u32[]{:S(2)}, u32[]{:S(2)}) collective-permute-start(f32[8,128]{1,0:T(8,128)S(1)} %add.20), channel_id=1, source_target_pairs={{0,4},{1,5},{2,6},{3,7},{4,0},{5,1},{6,2},{7,3},{8,12},{9,13},{10,... | collective-permute-start | bytes 12296 | tf_op jit(solution)/shard_map/ppermute | solution.py:400
  79.2 0.7 collective-permute-done.19
  80.0 3.1 %collective-permute-done.18 = f32[8,128]{1,0:T(8,128)S(1)} collective-permute-done((f32[8,128]{1,0:T(8,128)S(1)}, f32[8,128]{1,0:T(8,128)S(1)}, u32[]{:S(2)}, u32[]{:S(2)}) %collective-permute-start.18) | collective-permute-done | bytes 4128 | tf_op jit(solution)/shard_map/ppermute | solution.py:400
  83.1 0.1 reshape.16
  83.2 0.1 reduce_sum.9
  83.3 0.7 copy.6
  (18 shorter events, 0.1 us)
Async XLA Ops:
  0.6 47.8 %copy-start.1 = (bf16[768,256]{1,0:T(8,128)(2,1)S(1)}, bf16[768,256]{1,0:T(8,128)(2,1)}, u32[]{:S(2)}) copy-start(bf16[768,256]{1,0:T(8,128)(2,1)} %constant.32.mix) | copy-start | bytes 1179652
  2.8 10.6 %collective-permute-start.3 = (bf16[256,256]{1,0:T(8,128)(2,1)}, bf16[256,256]{1,0:T(8,128)(2,1)S(1)}, u32[]{:S(2)}, u32[]{:S(2)}) collective-permute-start(bf16[256,256]{1,0:T(8,128)(2,1)} %get-tuple-element.33), channel_id=1, source_target_pairs={{0,16},{16,32},{32,48},{48,0},{64,80},{80,96},{96,112},{112,64},{1... | collective-permute-start | bytes 393224 | tf_op jit(solution)/shard_map/ppermute | solution.py:416
  4.4 10.8 %collective-permute-start.4 = (bf16[256,256]{1,0:T(8,128)(2,1)}, bf16[256,256]{1,0:T(8,128)(2,1)S(1)}, u32[]{:S(2)}, u32[]{:S(2)}) collective-permute-start(bf16[256,256]{1,0:T(8,128)(2,1)} %get-tuple-element.34), channel_id=1, source_target_pairs={{0,32},{16,48},{32,0},{48,16},{64,96},{80,112},{96,64},{112,80},{1... | collective-permute-start | bytes 393224 | tf_op jit(solution)/shard_map/ppermute | solution.py:416
  7.2 8.1 %collective-permute-start.5 = (bf16[256,256]{1,0:T(8,128)(2,1)}, bf16[256,256]{1,0:T(8,128)(2,1)S(1)}, u32[]{:S(2)}, u32[]{:S(2)}) collective-permute-start(bf16[256,256]{1,0:T(8,128)(2,1)} %get-tuple-element.35), channel_id=1, source_target_pairs={{0,48},{16,0},{32,16},{48,32},{64,112},{80,64},{96,80},{112,96},{1... | collective-permute-start | bytes 393224 | tf_op jit(solution)/shard_map/ppermute | solution.py:416
  8.6 8.6 %collective-permute-start = (bf16[256,256]{1,0:T(8,128)(2,1)}, bf16[256,256]{1,0:T(8,128)(2,1)S(1)}, u32[]{:S(2)}, u32[]{:S(2)}) collective-permute-start(bf16[256,256]{1,0:T(8,128)(2,1)} %get-tuple-element.26), channel_id=1, source_target_pairs={{0,16},{16,32},{32,48},{48,0},{64,80},{80,96},{96,112},{112,64},{1... | collective-permute-start | bytes 393224 | tf_op jit(solution)/shard_map/ppermute | solution.py:416
  9.2 9.8 %collective-permute-start.1 = (bf16[256,256]{1,0:T(8,128)(2,1)}, bf16[256,256]{1,0:T(8,128)(2,1)S(1)}, u32[]{:S(2)}, u32[]{:S(2)}) collective-permute-start(bf16[256,256]{1,0:T(8,128)(2,1)} %get-tuple-element.27), channel_id=1, source_target_pairs={{0,32},{16,48},{32,0},{48,16},{64,96},{80,112},{96,64},{112,80},{1... | collective-permute-start | bytes 393224 | tf_op jit(solution)/shard_map/ppermute | solution.py:416
  13.4 5.9 %collective-permute-start.2 = (bf16[256,256]{1,0:T(8,128)(2,1)}, bf16[256,256]{1,0:T(8,128)(2,1)S(1)}, u32[]{:S(2)}, u32[]{:S(2)}) collective-permute-start(bf16[256,256]{1,0:T(8,128)(2,1)} %get-tuple-element.28), channel_id=1, source_target_pairs={{0,48},{16,0},{32,16},{48,32},{64,112},{80,64},{96,80},{112,96},{1... | collective-permute-start | bytes 393224 | tf_op jit(solution)/shard_map/ppermute | solution.py:416
  15.3 11.0 %collective-permute-start.7 = (bf16[256,256]{1,0:T(8,128)(2,1)S(1)}, bf16[256,256]{1,0:T(8,128)(2,1)S(1)}, u32[]{:S(2)}, u32[]{:S(2)}) collective-permute-start(bf16[256,256]{1,0:T(8,128)(2,1)S(1)} %select_select_fusion), channel_id=1, source_target_pairs={{0,64},{16,80},{32,96},{48,112},{64,0},{80,16},{96,32},{112,48},{1... | collective-permute-start | bytes 393224 | tf_op jit(solution)/shard_map/ppermute | solution.py:417
  19.3 7.0 %collective-permute-start.6 = (bf16[256,256]{1,0:T(8,128)(2,1)S(1)}, bf16[256,256]{1,0:T(8,128)(2,1)S(1)}, u32[]{:S(2)}, u32[]{:S(2)}) collective-permute-start(bf16[256,256]{1,0:T(8,128)(2,1)S(1)} %select_select_fusion.1), channel_id=1, source_target_pairs={{0,64},{16,80},{32,96},{48,112},{64,0},{80,16},{96,32},{112,48},{1... | collective-permute-start | bytes 393224 | tf_op jit(solution)/shard_map/ppermute | solution.py:417
  20.9 39.4 %collective-permute-start.11 = (bf16[4,2,256,256]{3,2,1,0:T(8,128)(2,1)}, bf16[4,2,256,256]{3,2,1,0:T(8,128)(2,1)S(1)}, u32[]{:S(2)}, u32[]{:S(2)}) collective-permute-start(bf16[4,2,256,256]{3,2,1,0:T(8,128)(2,1)} %get-tuple-element.39), channel_id=1, source_target_pairs={{0,1},{1,2},{2,3},{3,4},{4,5},{5,6},{6,7},{7,8},{8,9},{9,10},{10,1... | collective-permute-start | bytes 3145736 | tf_op jit(solution)/shard_map/ppermute | solution.py:414
  20.9 39.4 %collective-permute-start.12 = (bf16[4,2,256,256]{3,2,1,0:T(8,128)(2,1)}, bf16[4,2,256,256]{3,2,1,0:T(8,128)(2,1)}, u32[]{:S(2)}, u32[]{:S(2)}) collective-permute-start(bf16[4,2,256,256]{3,2,1,0:T(8,128)(2,1)} %get-tuple-element.40), channel_id=1, source_target_pairs={{0,15},{1,0},{2,1},{3,2},{4,3},{5,4},{6,5},{7,6},{8,7},{9,8},{10,9... | collective-permute-start | bytes 3145736 | tf_op jit(solution)/shard_map/ppermute | solution.py:415
  26.3 12.5 %copy-start.2 = (bf16[2,256,256]{2,1,0:T(8,128)(2,1)}, bf16[2,256,256]{2,1,0:T(8,128)(2,1)S(1)}, u32[]{:S(2)}) copy-start(bf16[2,256,256]{2,1,0:T(8,128)(2,1)S(1)} %maximum_select_fusion.refs_0_) | copy-start | bytes 786436
  26.3 11.5 %collective-permute-start.10 = (bf16[2,256,256]{2,1,0:T(8,128)(2,1)S(1)}, bf16[2,256,256]{2,1,0:T(8,128)(2,1)S(1)}, u32[]{:S(2)}, u32[]{:S(2)}) collective-permute-start(bf16[2,256,256]{2,1,0:T(8,128)(2,1)S(1)} %maximum_select_fusion.refs_0_), channel_id=1, source_target_pairs={{0,48},{16,0},{32,16},{48,32},{64,112},{80,64},{96,80},{112,96},{1... | collective-permute-start | bytes 786440 | tf_op jit(solution)/shard_map/ppermute | solution.py:416
  28.8 10.0 %collective-permute-start.9 = (bf16[2,256,256]{2,1,0:T(8,128)(2,1)S(1)}, bf16[2,256,256]{2,1,0:T(8,128)(2,1)S(1)}, u32[]{:S(2)}, u32[]{:S(2)}) collective-permute-start(bf16[2,256,256]{2,1,0:T(8,128)(2,1)S(1)} %maximum_select_fusion.refs_0_), channel_id=1, source_target_pairs={{0,32},{16,48},{32,0},{48,16},{64,96},{80,112},{96,64},{112,80},{1... | collective-permute-start | bytes 786440 | tf_op jit(solution)/shard_map/ppermute | solution.py:416
  30.6 11.1 %collective-permute-start.8 = (bf16[2,256,256]{2,1,0:T(8,128)(2,1)S(1)}, bf16[2,256,256]{2,1,0:T(8,128)(2,1)}, u32[]{:S(2)}, u32[]{:S(2)}) collective-permute-start(bf16[2,256,256]{2,1,0:T(8,128)(2,1)S(1)} %maximum_select_fusion.refs_0_), channel_id=1, source_target_pairs={{0,16},{16,32},{32,48},{48,0},{64,80},{80,96},{96,112},{112,64},{1... | collective-permute-start | bytes 786440 | tf_op jit(solution)/shard_map/ppermute | solution.py:416
  37.9 0.9 %copy-start.3 = (bf16[2,256,256]{2,1,0:T(8,128)(2,1)}, bf16[2,256,256]{2,1,0:T(8,128)(2,1)S(1)}, u32[]{:S(2)}) copy-start(bf16[2,256,256]{2,1,0:T(8,128)(2,1)S(1)} %collective-permute-done.10.refs_3_) | copy-start | bytes 786436
  38.8 0.7 copy-start.4
  43.0 18.7 %collective-permute-start.13 = (bf16[2,2,256,256]{3,2,1,0:T(8,128)(2,1)S(1)}, bf16[2,2,256,256]{3,2,1,0:T(8,128)(2,1)S(1)}, u32[]{:S(2)}, u32[]{:S(2)}) collective-permute-start(bf16[2,2,256,256]{3,2,1,0:T(8,128)(2,1)S(1)} %get-tuple-element.44), channel_id=1, source_target_pairs={{0,1},{1,2},{2,3},{3,4},{4,5},{5,6},{6,7},{7,8},{8,9},{9,10},{10,1... | collective-permute-start | bytes 1572872 | tf_op jit(solution)/shard_map/ppermute | solution.py:414
  43.0 18.7 %collective-permute-start.14 = (bf16[2,2,256,256]{3,2,1,0:T(8,128)(2,1)S(1)}, bf16[2,2,256,256]{3,2,1,0:T(8,128)(2,1)S(1)}, u32[]{:S(2)}, u32[]{:S(2)}) collective-permute-start(bf16[2,2,256,256]{3,2,1,0:T(8,128)(2,1)S(1)} %get-tuple-element.45), channel_id=1, source_target_pairs={{0,15},{1,0},{2,1},{3,2},{4,3},{5,4},{6,5},{7,6},{8,7},{9,8},{10,9... | collective-permute-start | bytes 1572872 | tf_op jit(solution)/shard_map/ppermute | solution.py:415
  48.4 1.6 %copy-start = (bf16[4,4,256,256]{3,2,1,0:T(8,128)(2,1)S(1)}, bf16[4,4,256,256]{3,2,1,0:T(8,128)(2,1)}, u32[]{:S(2)}) copy-start(bf16[4,4,256,256]{3,2,1,0:T(8,128)(2,1)} %o.1) | copy-start | bytes 6291460
  68.8 1.2 %collective-permute-start.15 = (f32[8,128]{1,0:T(8,128)S(1)}, f32[8,128]{1,0:T(8,128)S(1)}, u32[]{:S(2)}, u32[]{:S(2)}) collective-permute-start(f32[8,128]{1,0:T(8,128)S(1)} %get-tuple-element.47), channel_id=1, source_target_pairs={{0,1},{1,0},{2,3},{3,2},{4,5},{5,4},{6,7},{7,6},{8,9},{9,8},{10,11... | collective-permute-start | bytes 12296 | tf_op jit(solution)/shard_map/ppermute | solution.py:400
  70.0 5.1 %collective-permute-start.16 = (f32[8,128]{1,0:T(8,128)S(1)}, f32[8,128]{1,0:T(8,128)S(1)}, u32[]{:S(2)}, u32[]{:S(2)}) collective-permute-start(f32[8,128]{1,0:T(8,128)S(1)} %add.19), channel_id=1, source_target_pairs={{0,2},{1,3},{2,0},{3,1},{4,6},{5,7},{6,4},{7,5},{8,10},{9,11},{10,... | collective-permute-start | bytes 12296 | tf_op jit(solution)/shard_map/ppermute | solution.py:400
  75.1 4.8 %collective-permute-start.19 = (f32[8,128]{1,0:T(8,128)S(1)}, f32[8,128]{1,0:T(8,128)S(1)}, u32[]{:S(2)}, u32[]{:S(2)}) collective-permute-start(f32[8,128]{1,0:T(8,128)S(1)} %add.20), channel_id=1, source_target_pairs={{0,12},{1,13},{2,14},{3,15},{4,8},{5,9},{6,10},{7,11},{8,4},{9,5},... | collective-permute-start | bytes 12296 | tf_op jit(solution)/shard_map/ppermute | solution.py:400
  78.0 5.1 %collective-permute-start.18 = (f32[8,128]{1,0:T(8,128)S(1)}, f32[8,128]{1,0:T(8,128)S(1)}, u32[]{:S(2)}, u32[]{:S(2)}) collective-permute-start(f32[8,128]{1,0:T(8,128)S(1)} %add.20), channel_id=1, source_target_pairs={{0,8},{1,9},{2,10},{3,11},{4,12},{5,13},{6,14},{7,15},{8,0},{9,1},... | collective-permute-start | bytes 12296 | tf_op jit(solution)/shard_map/ppermute | solution.py:400
  78.0 5.1 %collective-permute-start.17 = (f32[8,128]{1,0:T(8,128)S(1)}, f32[8,128]{1,0:T(8,128)S(1)}, u32[]{:S(2)}, u32[]{:S(2)}) collective-permute-start(f32[8,128]{1,0:T(8,128)S(1)} %add.20), channel_id=1, source_target_pairs={{0,4},{1,5},{2,6},{3,7},{4,0},{5,1},{6,2},{7,3},{8,12},{9,13},{10,... | collective-permute-start | bytes 12296 | tf_op jit(solution)/shard_map/ppermute | solution.py:400

commit v7 on v5

--- a/solution.py
+++ b/solution.py
@@ -304,28 +304,24 @@
     return [parts[a * row:(a + 1) * row] for a in range(PANEL)]
 
 
-def edges_kernel(orbitals, top, bottom, held, loaded, stored):
+def edges_kernel(orbitals, top, bottom, loaded):
     nx = orbitals.shape[1]
-    loads = [pltpu.make_async_copy(orbitals.at[:, a:a + 2], held.at[n], loaded.at[n]) for n, a in enumerate((nx - 2, 0))]
-    stores = [pltpu.make_async_copy(held.at[n], out, stored.at[n]) for n, out in enumerate((top, bottom))]
+    loads = [pltpu.make_async_copy(orbitals.at[:, x:x + 2], out, loaded.at[n]) for n, (x, out) in enumerate(((nx - 2, top), (0, bottom)))]
     for c in loads:
         c.start()
-    for load, store in zip(loads, stores):
-        load.wait()
-        store.start()
-    for c in stores:
+    for c in loads:
         c.wait()
 
 
 def edges(orbitals):
     nj, _, ny, nz = orbitals.shape
-    hbm = pl.BlockSpec(memory_space=pltpu.HBM)
+    vmem = pl.BlockSpec(memory_space=pltpu.VMEM)
     return pl.pallas_call(
         edges_kernel,
-        out_shape=(jax.ShapeDtypeStruct((nj, 2, ny, nz), orbitals.dtype),) * 2,
-        in_specs=[hbm],
-        out_specs=(hbm, hbm),
-        scratch_shapes=[pltpu.VMEM((2, nj, 2, ny, nz), orbitals.dtype), pltpu.SemaphoreType.DMA((2,)), pltpu.SemaphoreType.DMA((2,))],
+        out_shape=(pltpu.VMEM((nj, 2, ny, nz), orbitals.dtype),) * 2,
+        in_specs=[pl.BlockSpec(memory_space=pltpu.HBM)],
+        out_specs=(vmem, vmem),
+        scratch_shapes=[pltpu.SemaphoreType.DMA((2,))],
         name="edge_planes",
     )(orbitals)
 

time: 84.3 us -> 84.3 us (level)
  no operation moved by 1% of the time
where the time goes in v7:
time: 84.3 us; the launch traced here: 84 us
  starting transfers between devices  33.9 us (40%)
  Pallas kernels  24.4 us (29%)
  waiting for transfers between devices  19.2 us (23%)
  local copies, waits for them, and re-layouts  3.08 us (4%)
  other arithmetic  2.01 us (2%)
  between operations  1.41 us (2%)
    ppermute x9, starting transfers between devices, local(): along = lambda v, k: lax.ppermute(v, 'band', rows(k, row))  12.4 us
    ppermute x9, waiting for transfers between devices, local(): along = lambda v, k: lax.ppermute(v, 'band', rows(k, row))  11.8 us
    ppermute x2, starting transfers between devices, local(): down = lambda v: lax.ppermute(v, 'dom', ring(lax.axis_size('dom'), -1))  10.7 us
    pallas_call x1, Pallas kernels, inner(): pl.pallas_call(inner_kernel, grid=(nj,), out_shape=(pltpu.VMEM((nj, nx, n...  10.3 us
    pallas_call x1, Pallas kernels, outer(): pl.pallas_call(outer_kernel, grid=(nj,), out_shape=(jax.ShapeDtypeStruct(...  7.68 us
    ppermute x5, starting transfers between devices, total(): lax.ppermute(part, 'dom', [(i, i ^ k) for i in range(count)])  7.45 us
    ppermute x5, waiting for transfers between devices, total(): lax.ppermute(part, 'dom', [(i, i ^ k) for i in range(count)])  6.77 us
    ppermute x2, starting transfers between devices, local(): across = lambda v: lax.ppermute(v, 'band', ring(lax.axis_size('band'), row))  3.31 us
  transfers between devices with their start and end apart: 20, of which 10 were waited for; matrix products, arithmetic and copies ran while one was open for 2% of the time, Pallas kernels for 17%

profile of v7, /device:TPU:0, one launch (start us, length us, event | category | flops | bytes accessed | tf_op | source)
XLA Modules:
  0.0 84.0 jit_solution(685138017682098388)
XLA Ops:
  0.6 0.0 copy-start.1
  0.6 2.1 %cut_panel.1 = (bf16[256,256]{1,0:T(8,128)(2,1)}, bf16[256,256]{1,0:T(8,128)(2,1)}, bf16[256,256]{1,0:T(8,128)(2,1)}, bf16[256,256]{1,0:T(8,128)(2,1)}, bf16[256...) custom-call(bf16[4,4,256,256]{3,2,1,0:T(8,128)(2,1)} %o.1), custom_call_target="tpu_custom_call" | custom-call | tf_op jit(solution)/shard_map/cut_panel/pallas_call | solution.py:292
  2.8 1.6 %collective-permute-start.3 = (bf16[256,256]{1,0:T(8,128)(2,1)}, bf16[256,256]{1,0:T(8,128)(2,1)S(1)}, u32[]{:S(2)}, u32[]{:S(2)}) collective-permute-start(bf16[256,256]{1,0:T(8,128)(2,1)} %get-tuple-element.31), channel_id=1, source_target_pairs={{0,16},{16,32},{32,48},{48,0},{64,80},{80,96},{96,112},{112,64},{1... | collective-permute-start | bytes 393224 | tf_op jit(solution)/shard_map/ppermute | solution.py:391
  4.4 2.7 %collective-permute-start.4 = (bf16[256,256]{1,0:T(8,128)(2,1)}, bf16[256,256]{1,0:T(8,128)(2,1)S(1)}, u32[]{:S(2)}, u32[]{:S(2)}) collective-permute-start(bf16[256,256]{1,0:T(8,128)(2,1)} %get-tuple-element.32), channel_id=1, source_target_pairs={{0,32},{16,48},{32,0},{48,16},{64,96},{80,112},{96,64},{112,80},{1... | collective-permute-start | bytes 393224 | tf_op jit(solution)/shard_map/ppermute | solution.py:391
  7.2 1.4 %collective-permute-start.5 = (bf16[256,256]{1,0:T(8,128)(2,1)}, bf16[256,256]{1,0:T(8,128)(2,1)S(1)}, u32[]{:S(2)}, u32[]{:S(2)}) collective-permute-start(bf16[256,256]{1,0:T(8,128)(2,1)} %get-tuple-element.33), channel_id=1, source_target_pairs={{0,48},{16,0},{32,16},{48,32},{64,112},{80,64},{96,80},{112,96},{1... | collective-permute-start | bytes 393224 | tf_op jit(solution)/shard_map/ppermute | solution.py:391
  8.6 0.6 collective-permute-start
  9.2 0.9 %collective-permute-start.1 = (bf16[256,256]{1,0:T(8,128)(2,1)}, bf16[256,256]{1,0:T(8,128)(2,1)S(1)}, u32[]{:S(2)}, u32[]{:S(2)}) collective-permute-start(bf16[256,256]{1,0:T(8,128)(2,1)} %get-tuple-element.25), channel_id=1, source_target_pairs={{0,32},{16,48},{32,0},{48,16},{64,96},{80,112},{96,64},{112,80},{1... | collective-permute-start | bytes 393224 | tf_op jit(solution)/shard_map/ppermute | solution.py:391
  10.7 2.9 %edge_planes.1 = (bf16[4,2,256,256]{3,2,1,0:T(8,128)(2,1)}, bf16[4,2,256,256]{3,2,1,0:T(8,128)(2,1)}) custom-call(bf16[4,4,256,256]{3,2,1,0:T(8,128)(2,1)} %o.1), custom_call_target="tpu_custom_call" | custom-call | tf_op jit(solution)/shard_map/edge_planes/pallas_call | solution.py:319
  13.7 0.0 collective-permute-done.3
  13.7 1.9 %collective-permute-start.2 = (bf16[256,256]{1,0:T(8,128)(2,1)}, bf16[256,256]{1,0:T(8,128)(2,1)S(1)}, u32[]{:S(2)}, u32[]{:S(2)}) collective-permute-start(bf16[256,256]{1,0:T(8,128)(2,1)} %get-tuple-element.26), channel_id=1, source_target_pairs={{0,48},{16,0},{32,16},{48,32},{64,112},{80,64},{96,80},{112,96},{1... | collective-permute-start | bytes 393224 | tf_op jit(solution)/shard_map/ppermute | solution.py:391
  15.5 0.0 collective-permute-done.4
  15.5 0.0 collective-permute-done.5
  15.5 0.9 %select_select_fusion = bf16[256,256]{1,0:T(8,128)(2,1)S(1)} fusion(bf16[256,256]{1,0:T(8,128)(2,1)S(1)} %collective-permute-done.4, bf16[256,256]{1,0:T(8,128)(2,1)S(1)} %collective-permute-done.5, bf16[256,256]{1,0:T(8,128)(2,1)} %get-tuple-element.30, bf16[256,256]{1,0:T(8,128)(2,1)S(1)} %collective-permute-done.3, pred[]{:T(512)S(6)} %select_n.56, ...), kind=kLoop, calls=%fused_computation.1 | loop fusion | flops 196608 | bytes 655363 | tf_op jit(solution)/shard_map/select_n | solution.py:397
  16.5 1.7 %collective-permute-start.7 = (bf16[256,256]{1,0:T(8,128)(2,1)S(1)}, bf16[256,256]{1,0:T(8,128)(2,1)S(1)}, u32[]{:S(2)}, u32[]{:S(2)}) collective-permute-start(bf16[256,256]{1,0:T(8,128)(2,1)S(1)} %select_select_fusion), channel_id=1, source_target_pairs={{0,64},{16,80},{32,96},{48,112},{64,0},{80,16},{96,32},{112,48},{1... | collective-permute-start | bytes 393224 | tf_op jit(solution)/shard_map/ppermute | solution.py:392
  18.1 0.0 collective-permute-done
  18.1 0.9 %collective-permute-done.1 = bf16[256,256]{1,0:T(8,128)(2,1)S(1)} collective-permute-done((bf16[256,256]{1,0:T(8,128)(2,1)}, bf16[256,256]{1,0:T(8,128)(2,1)S(1)}, u32[]{:S(2)}, u32[]{:S(2)}) %collective-permute-start.1) | collective-permute-done | bytes 131104 | tf_op jit(solution)/shard_map/ppermute | solution.py:391
  19.0 0.5 collective-permute-done.2
  19.5 0.9 %select_select_fusion.1 = bf16[256,256]{1,0:T(8,128)(2,1)S(1)} fusion(bf16[256,256]{1,0:T(8,128)(2,1)S(1)} %collective-permute-done.1, bf16[256,256]{1,0:T(8,128)(2,1)S(1)} %collective-permute-done.2, bf16[256,256]{1,0:T(8,128)(2,1)} %get-tuple-element.23, bf16[256,256]{1,0:T(8,128)(2,1)S(1)} %collective-permute-done, pred[]{:T(512)S(6)} %select_n.56, ...), kind=kLoop, calls=%fused_computation.2 | loop fusion | flops 196608 | bytes 655363 | tf_op jit(solution)/shard_map/select_n | solution.py:397
  20.5 1.7 %collective-permute-start.6 = (bf16[256,256]{1,0:T(8,128)(2,1)S(1)}, bf16[256,256]{1,0:T(8,128)(2,1)S(1)}, u32[]{:S(2)}, u32[]{:S(2)}) collective-permute-start(bf16[256,256]{1,0:T(8,128)(2,1)S(1)} %select_select_fusion.1), channel_id=1, source_target_pairs={{0,64},{16,80},{32,96},{48,112},{64,0},{80,16},{96,32},{112,48},{1... | collective-permute-start | bytes 393224 | tf_op jit(solution)/shard_map/ppermute | solution.py:392
  22.1 0.0 collective-permute-start.11
  22.1 5.4 %collective-permute-start.12 = (bf16[4,2,256,256]{3,2,1,0:T(8,128)(2,1)}, bf16[4,2,256,256]{3,2,1,0:T(8,128)(2,1)}, u32[]{:S(2)}, u32[]{:S(2)}) collective-permute-start(bf16[4,2,256,256]{3,2,1,0:T(8,128)(2,1)} %get-tuple-element.38), channel_id=1, source_target_pairs={{0,15},{1,0},{2,1},{3,2},{4,3},{5,4},{6,5},{7,6},{8,7},{9,8},{10,9... | collective-permute-start | bytes 3145736 | tf_op jit(solution)/shard_map/ppermute | solution.py:390
  27.5 1.6 %collective-permute-start.10 = (bf16[2,256,256]{2,1,0:T(8,128)(2,1)S(1)}, bf16[2,256,256]{2,1,0:T(8,128)(2,1)S(1)}, u32[]{:S(2)}, u32[]{:S(2)}) collective-permute-start(bf16[2,256,256]{2,1,0:T(8,128)(2,1)S(1)} %maximum_select_fusion.refs_0_), channel_id=1, source_target_pairs={{0,48},{16,0},{32,16},{48,32},{64,112},{80,64},{96,80},{112,96},{1... | collective-permute-start | bytes 786440 | tf_op jit(solution)/shard_map/ppermute | solution.py:391
  29.1 1.7 %collective-permute-start.9 = (bf16[2,256,256]{2,1,0:T(8,128)(2,1)S(1)}, bf16[2,256,256]{2,1,0:T(8,128)(2,1)S(1)}, u32[]{:S(2)}, u32[]{:S(2)}) collective-permute-start(bf16[2,256,256]{2,1,0:T(8,128)(2,1)S(1)} %maximum_select_fusion.refs_0_), channel_id=1, source_target_pairs={{0,32},{16,48},{32,0},{48,16},{64,96},{80,112},{96,64},{112,80},{1... | collective-permute-start | bytes 786440 | tf_op jit(solution)/shard_map/ppermute | solution.py:391
  30.8 0.0 collective-permute-start.8
  30.8 5.5 %collective-permute-done.10.refs_3_ = bf16[2,256,256]{2,1,0:T(8,128)(2,1)S(1)} collective-permute-done((bf16[2,256,256]{2,1,0:T(8,128)(2,1)S(1)}, bf16[2,256,256]{2,1,0:T(8,128)(2,1)S(1)}, u32[]{:S(2)}, u32[]{:S(2)}) %collective-permute-start.10) | collective-permute-done | bytes 262176 | tf_op jit(solution)/shard_map/ppermute | solution.py:391
  36.3 2.8 %collective-permute-done.9.refs_2_ = bf16[2,256,256]{2,1,0:T(8,128)(2,1)S(1)} collective-permute-done((bf16[2,256,256]{2,1,0:T(8,128)(2,1)S(1)}, bf16[2,256,256]{2,1,0:T(8,128)(2,1)S(1)}, u32[]{:S(2)}, u32[]{:S(2)}) %collective-permute-start.9) | collective-permute-done | bytes 262176 | tf_op jit(solution)/shard_map/ppermute | solution.py:391
  39.1 0.7 copy-done.4
  39.8 2.1 %collective-permute-done.8.refs_1_ = bf16[2,256,256]{2,1,0:T(8,128)(2,1)} collective-permute-done((bf16[2,256,256]{2,1,0:T(8,128)(2,1)S(1)}, bf16[2,256,256]{2,1,0:T(8,128)(2,1)}, u32[]{:S(2)}, u32[]{:S(2)}) %collective-permute-start.8) | collective-permute-done | bytes 262176 | tf_op jit(solution)/shard_map/ppermute | solution.py:391
  41.9 1.3 %join_panel.1 = (bf16[2,4,256,256]{3,2,1,0:T(8,128)(2,1)S(1)}, bf16[2,2,256,256]{3,2,1,0:T(8,128)(2,1)S(1)}, bf16[2,2,256,256]{3,2,1,0:T(8,128)(2,1)S(1)}) custom-call(bf16[2,256,256]{2,1,0:T(8,128)(2,1)} %copy-done.2, bf16[2,256,256]{2,1,0:T(8,128)(2,1)} %collective-permute-done.8.refs_1_, bf16[2,256,256]{2,1,0:T(8,128)(2,1)} %copy-done.4, ...), custom_call_target="tpu_custom_call" | custom-call | tf_op jit(solution)/shard_map/join_panel/pallas_call | solution.py:353
  43.3 0.1 collective-permute-start.13
  43.3 5.3 %collective-permute-start.14 = (bf16[2,2,256,256]{3,2,1,0:T(8,128)(2,1)S(1)}, bf16[2,2,256,256]{3,2,1,0:T(8,128)(2,1)S(1)}, u32[]{:S(2)}, u32[]{:S(2)}) collective-permute-start(bf16[2,2,256,256]{3,2,1,0:T(8,128)(2,1)S(1)} %get-tuple-element.41), channel_id=1, source_target_pairs={{0,15},{1,0},{2,1},{3,2},{4,3},{5,4},{6,5},{7,6},{8,7},{9,8},{10,9... | collective-permute-start | bytes 1572872 | tf_op jit(solution)/shard_map/ppermute | solution.py:390
  48.7 1.6 %copy-done = bf16[4,4,256,256]{3,2,1,0:T(8,128)(2,1)S(1)} copy-done((bf16[4,4,256,256]{3,2,1,0:T(8,128)(2,1)S(1)}, bf16[4,4,256,256]{3,2,1,0:T(8,128)(2,1)}, u32[]{:S(2)}) %copy-start) | copy-done | bytes 2097176
  50.3 10.3 %inner_field.1 = (f32[4,4,256,256]{3,2,1,0:T(8,128)S(1)}, f32[4,4,256,256]{3,2,1,0:T(8,128)S(1)}, f32[2,4,256,256]{3,2,1,0:T(8,128)S(1)}) custom-call(bf16[4,4,256,256]{3,2,1,0:T(8,128)(2,1)S(1)} %copy-done, bf16[2,4,256,256]{3,2,1,0:T(8,128)(2,1)S(1)} %get-tuple-element.34.p, bf16[768,256]{1,0:T(8,128)(2,1)S(1)} %copy-done.1), custom_call_target="tpu_custom_call" | custom-call | flops 6000000000 | bytes 8388608 | tf_op jit(solution)/shard_map/inner_field/pallas_call | solution.py:140
  60.6 0.6 collective-permute-done.13.plo
  61.2 0.0 collective-permute-done.12.halo_high
  61.2 7.7 %outer_field.1 = (f32[4,4,256,256]{3,2,1,0:T(8,128)}, f32[8,128]{1,0:T(8,128)S(1)}) custom-call(f32[4,4,256,256]{3,2,1,0:T(8,128)S(1)} %get-tuple-element.35.e_in, f32[4,4,256,256]{3,2,1,0:T(8,128)S(1)} %get-tuple-element.36.o, bf16[4,2,256,256]{3,2,1,0:T(8,128)(2,1)S(1)} %collective-permute-done.11.halo_low, ...), custom_call_target="tpu_custom_call" | custom-call | flops 3000000000 | bytes 14680064 | tf_op jit(solution)/shard_map/outer_field/pallas_call | solution.py:253
  68.9 0.5 collective-permute-start.15
  69.4 0.8 collective-permute-done.15
  70.2 2.9 %collective-permute-start.16 = (f32[8,128]{1,0:T(8,128)S(1)}, f32[8,128]{1,0:T(8,128)S(1)}, u32[]{:S(2)}, u32[]{:S(2)}) collective-permute-start(f32[8,128]{1,0:T(8,128)S(1)} %add.19), channel_id=1, source_target_pairs={{0,2},{1,3},{2,0},{3,1},{4,6},{5,7},{6,4},{7,5},{8,10},{9,11},{10,... | collective-permute-start | bytes 12296 | tf_op jit(solution)/shard_map/ppermute | solution.py:375
  73.1 2.2 %collective-permute-done.16 = f32[8,128]{1,0:T(8,128)S(1)} collective-permute-done((f32[8,128]{1,0:T(8,128)S(1)}, f32[8,128]{1,0:T(8,128)S(1)}, u32[]{:S(2)}, u32[]{:S(2)}) %collective-permute-start.16) | collective-permute-done | bytes 4128 | tf_op jit(solution)/shard_map/ppermute | solution.py:375
  75.3 2.7 %collective-permute-start.19 = (f32[8,128]{1,0:T(8,128)S(1)}, f32[8,128]{1,0:T(8,128)S(1)}, u32[]{:S(2)}, u32[]{:S(2)}) collective-permute-start(f32[8,128]{1,0:T(8,128)S(1)} %add.20), channel_id=1, source_target_pairs={{0,12},{1,13},{2,14},{3,15},{4,8},{5,9},{6,10},{7,11},{8,4},{9,5},... | collective-permute-start | bytes 12296 | tf_op jit(solution)/shard_map/ppermute | solution.py:375
  78.0 1.3 %collective-permute-start.18 = (f32[8,128]{1,0:T(8,128)S(1)}, f32[8,128]{1,0:T(8,128)S(1)}, u32[]{:S(2)}, u32[]{:S(2)}) collective-permute-start(f32[8,128]{1,0:T(8,128)S(1)} %add.20), channel_id=1, source_target_pairs={{0,8},{1,9},{2,10},{3,11},{4,12},{5,13},{6,14},{7,15},{8,0},{9,1},... | collective-permute-start | bytes 12296 | tf_op jit(solution)/shard_map/ppermute | solution.py:375
  79.3 0.1 collective-permute-start.17
  79.4 0.7 collective-permute-done.19
  80.1 3.0 %collective-permute-done.18 = f32[8,128]{1,0:T(8,128)S(1)} collective-permute-done((f32[8,128]{1,0:T(8,128)S(1)}, f32[8,128]{1,0:T(8,128)S(1)}, u32[]{:S(2)}, u32[]{:S(2)}) %collective-permute-start.18) | collective-permute-done | bytes 4128 | tf_op jit(solution)/shard_map/ppermute | solution.py:375
  83.2 0.1 reshape.16
  83.2 0.1 reduce_sum.9
  83.3 0.7 copy.6
  (17 shorter events, 0.1 us)
Async XLA Ops:
  0.6 48.1 %copy-start.1 = (bf16[768,256]{1,0:T(8,128)(2,1)S(1)}, bf16[768,256]{1,0:T(8,128)(2,1)}, u32[]{:S(2)}) copy-start(bf16[768,256]{1,0:T(8,128)(2,1)} %constant.32.mix) | copy-start | bytes 1179652
  2.8 10.9 %collective-permute-start.3 = (bf16[256,256]{1,0:T(8,128)(2,1)}, bf16[256,256]{1,0:T(8,128)(2,1)S(1)}, u32[]{:S(2)}, u32[]{:S(2)}) collective-permute-start(bf16[256,256]{1,0:T(8,128)(2,1)} %get-tuple-element.31), channel_id=1, source_target_pairs={{0,16},{16,32},{32,48},{48,0},{64,80},{80,96},{96,112},{112,64},{1... | collective-permute-start | bytes 393224 | tf_op jit(solution)/shard_map/ppermute | solution.py:391
  4.4 11.1 %collective-permute-start.4 = (bf16[256,256]{1,0:T(8,128)(2,1)}, bf16[256,256]{1,0:T(8,128)(2,1)S(1)}, u32[]{:S(2)}, u32[]{:S(2)}) collective-permute-start(bf16[256,256]{1,0:T(8,128)(2,1)} %get-tuple-element.32), channel_id=1, source_target_pairs={{0,32},{16,48},{32,0},{48,16},{64,96},{80,112},{96,64},{112,80},{1... | collective-permute-start | bytes 393224 | tf_op jit(solution)/shard_map/ppermute | solution.py:391
  7.2 8.4 %collective-permute-start.5 = (bf16[256,256]{1,0:T(8,128)(2,1)}, bf16[256,256]{1,0:T(8,128)(2,1)S(1)}, u32[]{:S(2)}, u32[]{:S(2)}) collective-permute-start(bf16[256,256]{1,0:T(8,128)(2,1)} %get-tuple-element.33), channel_id=1, source_target_pairs={{0,48},{16,0},{32,16},{48,32},{64,112},{80,64},{96,80},{112,96},{1... | collective-permute-start | bytes 393224 | tf_op jit(solution)/shard_map/ppermute | solution.py:391
  8.6 9.5 %collective-permute-start = (bf16[256,256]{1,0:T(8,128)(2,1)}, bf16[256,256]{1,0:T(8,128)(2,1)S(1)}, u32[]{:S(2)}, u32[]{:S(2)}) collective-permute-start(bf16[256,256]{1,0:T(8,128)(2,1)} %get-tuple-element.24), channel_id=1, source_target_pairs={{0,16},{16,32},{32,48},{48,0},{64,80},{80,96},{96,112},{112,64},{1... | collective-permute-start | bytes 393224 | tf_op jit(solution)/shard_map/ppermute | solution.py:391
  9.2 9.8 %collective-permute-start.1 = (bf16[256,256]{1,0:T(8,128)(2,1)}, bf16[256,256]{1,0:T(8,128)(2,1)S(1)}, u32[]{:S(2)}, u32[]{:S(2)}) collective-permute-start(bf16[256,256]{1,0:T(8,128)(2,1)} %get-tuple-element.25), channel_id=1, source_target_pairs={{0,32},{16,48},{32,0},{48,16},{64,96},{80,112},{96,64},{112,80},{1... | collective-permute-start | bytes 393224 | tf_op jit(solution)/shard_map/ppermute | solution.py:391
  13.7 5.9 %collective-permute-start.2 = (bf16[256,256]{1,0:T(8,128)(2,1)}, bf16[256,256]{1,0:T(8,128)(2,1)S(1)}, u32[]{:S(2)}, u32[]{:S(2)}) collective-permute-start(bf16[256,256]{1,0:T(8,128)(2,1)} %get-tuple-element.26), channel_id=1, source_target_pairs={{0,48},{16,0},{32,16},{48,32},{64,112},{80,64},{96,80},{112,96},{1... | collective-permute-start | bytes 393224 | tf_op jit(solution)/shard_map/ppermute | solution.py:391
  16.5 11.0 %collective-permute-start.7 = (bf16[256,256]{1,0:T(8,128)(2,1)S(1)}, bf16[256,256]{1,0:T(8,128)(2,1)S(1)}, u32[]{:S(2)}, u32[]{:S(2)}) collective-permute-start(bf16[256,256]{1,0:T(8,128)(2,1)S(1)} %select_select_fusion), channel_id=1, source_target_pairs={{0,64},{16,80},{32,96},{48,112},{64,0},{80,16},{96,32},{112,48},{1... | collective-permute-start | bytes 393224 | tf_op jit(solution)/shard_map/ppermute | solution.py:392
  20.5 7.0 %collective-permute-start.6 = (bf16[256,256]{1,0:T(8,128)(2,1)S(1)}, bf16[256,256]{1,0:T(8,128)(2,1)S(1)}, u32[]{:S(2)}, u32[]{:S(2)}) collective-permute-start(bf16[256,256]{1,0:T(8,128)(2,1)S(1)} %select_select_fusion.1), channel_id=1, source_target_pairs={{0,64},{16,80},{32,96},{48,112},{64,0},{80,16},{96,32},{112,48},{1... | collective-permute-start | bytes 393224 | tf_op jit(solution)/shard_map/ppermute | solution.py:392
  22.1 39.1 %collective-permute-start.11 = (bf16[4,2,256,256]{3,2,1,0:T(8,128)(2,1)}, bf16[4,2,256,256]{3,2,1,0:T(8,128)(2,1)S(1)}, u32[]{:S(2)}, u32[]{:S(2)}) collective-permute-start(bf16[4,2,256,256]{3,2,1,0:T(8,128)(2,1)} %get-tuple-element.37), channel_id=1, source_target_pairs={{0,1},{1,2},{2,3},{3,4},{4,5},{5,6},{6,7},{7,8},{8,9},{9,10},{10,1... | collective-permute-start | bytes 3145736 | tf_op jit(solution)/shard_map/ppermute | solution.py:389
  22.1 39.1 %collective-permute-start.12 = (bf16[4,2,256,256]{3,2,1,0:T(8,128)(2,1)}, bf16[4,2,256,256]{3,2,1,0:T(8,128)(2,1)}, u32[]{:S(2)}, u32[]{:S(2)}) collective-permute-start(bf16[4,2,256,256]{3,2,1,0:T(8,128)(2,1)} %get-tuple-element.38), channel_id=1, source_target_pairs={{0,15},{1,0},{2,1},{3,2},{4,3},{5,4},{6,5},{7,6},{8,7},{9,8},{10,9... | collective-permute-start | bytes 3145736 | tf_op jit(solution)/shard_map/ppermute | solution.py:390
  27.5 11.6 %copy-start.2 = (bf16[2,256,256]{2,1,0:T(8,128)(2,1)}, bf16[2,256,256]{2,1,0:T(8,128)(2,1)S(1)}, u32[]{:S(2)}) copy-start(bf16[2,256,256]{2,1,0:T(8,128)(2,1)S(1)} %maximum_select_fusion.refs_0_) | copy-start | bytes 786436
  27.5 8.8 %collective-permute-start.10 = (bf16[2,256,256]{2,1,0:T(8,128)(2,1)S(1)}, bf16[2,256,256]{2,1,0:T(8,128)(2,1)S(1)}, u32[]{:S(2)}, u32[]{:S(2)}) collective-permute-start(bf16[2,256,256]{2,1,0:T(8,128)(2,1)S(1)} %maximum_select_fusion.refs_0_), channel_id=1, source_target_pairs={{0,48},{16,0},{32,16},{48,32},{64,112},{80,64},{96,80},{112,96},{1... | collective-permute-start | bytes 786440 | tf_op jit(solution)/shard_map/ppermute | solution.py:391
  29.1 10.0 %collective-permute-start.9 = (bf16[2,256,256]{2,1,0:T(8,128)(2,1)S(1)}, bf16[2,256,256]{2,1,0:T(8,128)(2,1)S(1)}, u32[]{:S(2)}, u32[]{:S(2)}) collective-permute-start(bf16[2,256,256]{2,1,0:T(8,128)(2,1)S(1)} %maximum_select_fusion.refs_0_), channel_id=1, source_target_pairs={{0,32},{16,48},{32,0},{48,16},{64,96},{80,112},{96,64},{112,80},{1... | collective-permute-start | bytes 786440 | tf_op jit(solution)/shard_map/ppermute | solution.py:391
  30.8 11.1 %collective-permute-start.8 = (bf16[2,256,256]{2,1,0:T(8,128)(2,1)S(1)}, bf16[2,256,256]{2,1,0:T(8,128)(2,1)}, u32[]{:S(2)}, u32[]{:S(2)}) collective-permute-start(bf16[2,256,256]{2,1,0:T(8,128)(2,1)S(1)} %maximum_select_fusion.refs_0_), channel_id=1, source_target_pairs={{0,16},{16,32},{32,48},{48,0},{64,80},{80,96},{96,112},{112,64},{1... | collective-permute-start | bytes 786440 | tf_op jit(solution)/shard_map/ppermute | solution.py:391
  36.3 2.8 %copy-start.3 = (bf16[2,256,256]{2,1,0:T(8,128)(2,1)}, bf16[2,256,256]{2,1,0:T(8,128)(2,1)S(1)}, u32[]{:S(2)}) copy-start(bf16[2,256,256]{2,1,0:T(8,128)(2,1)S(1)} %collective-permute-done.10.refs_3_) | copy-start | bytes 786436
  39.1 0.7 copy-start.4
  43.3 18.0 %collective-permute-start.13 = (bf16[2,2,256,256]{3,2,1,0:T(8,128)(2,1)S(1)}, bf16[2,2,256,256]{3,2,1,0:T(8,128)(2,1)S(1)}, u32[]{:S(2)}, u32[]{:S(2)}) collective-permute-start(bf16[2,2,256,256]{3,2,1,0:T(8,128)(2,1)S(1)} %get-tuple-element.40), channel_id=1, source_target_pairs={{0,1},{1,2},{2,3},{3,4},{4,5},{5,6},{6,7},{7,8},{8,9},{9,10},{10,1... | collective-permute-start | bytes 1572872 | tf_op jit(solution)/shard_map/ppermute | solution.py:389
  43.3 17.9 %collective-permute-start.14 = (bf16[2,2,256,256]{3,2,1,0:T(8,128)(2,1)S(1)}, bf16[2,2,256,256]{3,2,1,0:T(8,128)(2,1)S(1)}, u32[]{:S(2)}, u32[]{:S(2)}) collective-permute-start(bf16[2,2,256,256]{3,2,1,0:T(8,128)(2,1)S(1)} %get-tuple-element.41), channel_id=1, source_target_pairs={{0,15},{1,0},{2,1},{3,2},{4,3},{5,4},{6,5},{7,6},{8,7},{9,8},{10,9... | collective-permute-start | bytes 1572872 | tf_op jit(solution)/shard_map/ppermute | solution.py:390
  48.7 1.6 %copy-start = (bf16[4,4,256,256]{3,2,1,0:T(8,128)(2,1)S(1)}, bf16[4,4,256,256]{3,2,1,0:T(8,128)(2,1)}, u32[]{:S(2)}) copy-start(bf16[4,4,256,256]{3,2,1,0:T(8,128)(2,1)} %o.1) | copy-start | bytes 6291460
  68.9 1.3 %collective-permute-start.15 = (f32[8,128]{1,0:T(8,128)S(1)}, f32[8,128]{1,0:T(8,128)S(1)}, u32[]{:S(2)}, u32[]{:S(2)}) collective-permute-start(f32[8,128]{1,0:T(8,128)S(1)} %get-tuple-element.43), channel_id=1, source_target_pairs={{0,1},{1,0},{2,3},{3,2},{4,5},{5,4},{6,7},{7,6},{8,9},{9,8},{10,11... | collective-permute-start | bytes 12296 | tf_op jit(solution)/shard_map/ppermute | solution.py:375
  70.2 5.1 %collective-permute-start.16 = (f32[8,128]{1,0:T(8,128)S(1)}, f32[8,128]{1,0:T(8,128)S(1)}, u32[]{:S(2)}, u32[]{:S(2)}) collective-permute-start(f32[8,128]{1,0:T(8,128)S(1)} %add.19), channel_id=1, source_target_pairs={{0,2},{1,3},{2,0},{3,1},{4,6},{5,7},{6,4},{7,5},{8,10},{9,11},{10,... | collective-permute-start | bytes 12296 | tf_op jit(solution)/shard_map/ppermute | solution.py:375
  75.3 4.8 %collective-permute-start.19 = (f32[8,128]{1,0:T(8,128)S(1)}, f32[8,128]{1,0:T(8,128)S(1)}, u32[]{:S(2)}, u32[]{:S(2)}) collective-permute-start(f32[8,128]{1,0:T(8,128)S(1)} %add.20), channel_id=1, source_target_pairs={{0,12},{1,13},{2,14},{3,15},{4,8},{5,9},{6,10},{7,11},{8,4},{9,5},... | collective-permute-start | bytes 12296 | tf_op jit(solution)/shard_map/ppermute | solution.py:375
  78.0 5.1 %collective-permute-start.18 = (f32[8,128]{1,0:T(8,128)S(1)}, f32[8,128]{1,0:T(8,128)S(1)}, u32[]{:S(2)}, u32[]{:S(2)}) collective-permute-start(f32[8,128]{1,0:T(8,128)S(1)} %add.20), channel_id=1, source_target_pairs={{0,8},{1,9},{2,10},{3,11},{4,12},{5,13},{6,14},{7,15},{8,0},{9,1},... | collective-permute-start | bytes 12296 | tf_op jit(solution)/shard_map/ppermute | solution.py:375
  79.3 3.9 %collective-permute-start.17 = (f32[8,128]{1,0:T(8,128)S(1)}, f32[8,128]{1,0:T(8,128)S(1)}, u32[]{:S(2)}, u32[]{:S(2)}) collective-permute-start(f32[8,128]{1,0:T(8,128)S(1)} %add.20), channel_id=1, source_target_pairs={{0,4},{1,5},{2,6},{3,7},{4,0},{5,1},{6,2},{7,3},{8,12},{9,13},{10,... | collective-permute-start | bytes 12296 | tf_op jit(solution)/shard_map/ppermute | solution.py:375
